TPU v7x, 32 devices: a whole 2x2x4 slice. The times are simulated.
32 devices in a mesh: dp: 4 (over y, x), seq: 8 (over z, core).
Axes of the slice: x: 2, y: 2, z: 4, core: 2. Of those that a mesh axis runs over, the one named last changes fastest.
Arguments:
- tokens: bfloat16 [4, 128, 128, 1024], P('dp', 'seq'), may hold values from -12 to 12
- lengths: int32 [4], P('dp'), may hold values from 8192 to 16384, as said below
- w_qkv: bfloat16 [3, 1024, 1024], replicated, may hold values from -0.1875 to 0.1875
- out_grad: bfloat16 [4, 128, 128, 1024], P('dp', 'seq'), may hold values from -6 to 6
Outputs:
- attention: bfloat16 [4, 128, 128, 1024], P('dp', 'seq')
- input_grad: bfloat16 [4, 128, 128, 1024], P('dp', 'seq')
- w_grads: float32 [3, 1024, 1024], P(None, 'seq', 'dp')
Inputs may be any that keep to these rules, and one draw needn't show every extreme that they name: Samples at positions from lengths on are padding; some sequence is full and some has exactly 8192 valid samples.
All inputs are finite; a program needn't handle non-finite values.
Results may differ from a plain program's by a relative error of at most 0.04.
The roundings to bfloat16 on the way count: a program that leaves them out, or rounds other values in their place, can miss the bound.
Values may be sent and summed in bfloat16 or wider, within the bound.
No kernel may reach another device: no remote copies, remote signals or barrier semaphores. Data moves between devices by JAX's collectives and lax.ppermute only.
A program may use at most 192 MiB of HBM per device.

v0:
```python
import math

import jax
import jax.numpy as jnp
from jax import lax
from jax.sharding import PartitionSpec as P

HEADS = 8


ROW_FORMS = ("srqhe,srkhe->srqhk", "srqhk,srkhe->srqhe", "srqhk,srqhe->srkhe")
COLUMN_FORMS = ("sqche,skche->sqchk", "sqchk,skche->sqche", "sqchk,sqche->skche")


def to_heads(values):
    return values.reshape(values.shape[:-1] + (HEADS, values.shape[-1] // HEADS))


def from_heads(values):
    return values.reshape(values.shape[:-2] + (values.shape[-2] * values.shape[-1],))


def project(inputs, w_qkv):
    stacked = jnp.einsum(
        "srcd,jdf->jsrcf", inputs, w_qkv, preferred_element_type=jnp.float32
    ).astype(jnp.bfloat16)
    return (to_heads(stacked[0]), to_heads(stacked[1]), to_heads(stacked[2]))


def partial_attend(query_h, key_h, value_h, allowed, forms):
    scaling = 1.0 / math.sqrt(query_h.shape[-1])
    scores = jnp.einsum(forms[0], query_h, key_h, preferred_element_type=jnp.float32) * scaling
    scores = jnp.where(allowed, scores, -1e30)
    highest = jnp.max(scores, axis=-1)
    weights = jnp.where(allowed, jnp.exp(scores - highest[..., None]), 0.0)
    totals = jnp.sum(weights, axis=-1)
    mixed = jnp.einsum(
        forms[1], weights.astype(jnp.bfloat16), value_h, preferred_element_type=jnp.float32
    )
    return (highest, totals, mixed)


def partial_back(query_h, key_h, value_h, grad_h, allowed, log_total, delta, forms):
    scaling = 1.0 / math.sqrt(query_h.shape[-1])
    scores = jnp.einsum(forms[0], query_h, key_h, preferred_element_type=jnp.float32) * scaling
    scores = jnp.where(allowed, scores, -1e30)
    weights = jnp.where(allowed, jnp.exp(scores - log_total[..., None]), 0.0)
    grad_weights = jnp.einsum(forms[0], grad_h, value_h, preferred_element_type=jnp.float32)
    grad_scores = (weights * (grad_weights - delta[..., None])).astype(jnp.bfloat16)
    grad_value = jnp.einsum(
        forms[2], weights.astype(jnp.bfloat16), grad_h, preferred_element_type=jnp.float32
    ).astype(jnp.bfloat16)
    grad_query = (
        jnp.einsum(forms[1], grad_scores, key_h, preferred_element_type=jnp.float32) * scaling
    ).astype(jnp.bfloat16)
    grad_key = (
        jnp.einsum(forms[2], grad_scores, query_h, preferred_element_type=jnp.float32) * scaling
    ).astype(jnp.bfloat16)
    return (grad_query, grad_key, grad_value)


def input_terms(grads, w_qkv):
    stacked = jnp.stack([from_heads(item) for item in grads])
    return jnp.einsum("jsrcf,jdf->srcd", stacked, w_qkv, preferred_element_type=jnp.float32)


def weight_terms(inputs, grads):
    stacked = jnp.stack([from_heads(item) for item in grads])
    return jnp.einsum("srcd,jsrcf->jdf", inputs, stacked, preferred_element_type=jnp.float32)


def body(tokens, lengths, w_qkv, out_grad):
    seq_count = lax.axis_size("seq")
    seq_index = lax.axis_index("seq")
    seq_local, row_local, columns, width = tokens.shape
    col_local = columns // seq_count
    all_rows = row_local * seq_count
    limit = lengths[:, None, None, None]
    row_ids = seq_index * row_local + jnp.arange(row_local, dtype=jnp.int32)
    col_ids = jnp.arange(columns, dtype=jnp.int32)
    key_pos = row_ids[:, None, None] * columns + col_ids[None, None, :]
    same_col = col_ids[None, None, :] == col_ids[None, :, None]
    causal_cols = col_ids[None, None, :] <= col_ids[None, :, None]
    row_allowed = causal_cols[None] & ((key_pos[None] < limit) | same_col[None])
    row_allowed = row_allowed[:, :, :, None, :]
    every_row = jnp.arange(all_rows, dtype=jnp.int32)
    own_cols = seq_index * col_local + jnp.arange(col_local, dtype=jnp.int32)
    causal_rows = every_row[None, None, :] < every_row[:, None, None]
    col_key_pos = every_row[None, None, :] * columns + own_cols[None, :, None]
    column_allowed = causal_rows[None] & (col_key_pos[None] < limit)
    column_allowed = column_allowed[:, :, :, None, :]
    query_r, key_r, value_r = project(tokens, w_qkv)
    row_high, row_total, row_mixed = partial_attend(query_r, key_r, value_r, row_allowed, ROW_FORMS)
    query_c, key_c, value_c = (
        lax.all_to_all(query_r, "seq", split_axis=2, concat_axis=1, tiled=True),
        lax.all_to_all(key_r, "seq", split_axis=2, concat_axis=1, tiled=True),
        lax.all_to_all(value_r, "seq", split_axis=2, concat_axis=1, tiled=True),
    )
    col_high_c, col_total_c, col_mixed_c = partial_attend(
        query_c, key_c, value_c, column_allowed, COLUMN_FORMS
    )
    col_high, col_total, col_mixed = (
        lax.all_to_all(col_high_c, "seq", split_axis=1, concat_axis=2, tiled=True),
        lax.all_to_all(col_total_c, "seq", split_axis=1, concat_axis=2, tiled=True),
        lax.all_to_all(col_mixed_c, "seq", split_axis=1, concat_axis=2, tiled=True),
    )
    joint = jnp.maximum(row_high, col_high)
    row_factor = jnp.exp(row_high - joint)
    col_factor = jnp.exp(col_high - joint)
    joint_total = row_total * row_factor + col_total * col_factor
    log_total = joint + jnp.log(joint_total)
    combined = (
        row_mixed * row_factor[..., None] + col_mixed * col_factor[..., None]
    ) / joint_total[..., None]
    attention = from_heads(combined).astype(jnp.bfloat16)
    grad_h = to_heads(out_grad)
    delta = jnp.einsum(
        "srche,srche->srch", to_heads(attention), grad_h, preferred_element_type=jnp.float32
    )
    row_grads = partial_back(
        query_r, key_r, value_r, grad_h, row_allowed, log_total, delta, ROW_FORMS
    )
    grad_c = lax.all_to_all(grad_h, "seq", split_axis=2, concat_axis=1, tiled=True)
    log_total_c, delta_c = (
        lax.all_to_all(log_total, "seq", split_axis=2, concat_axis=1, tiled=True),
        lax.all_to_all(delta, "seq", split_axis=2, concat_axis=1, tiled=True),
    )
    col_grads = partial_back(
        query_c, key_c, value_c, grad_c, column_allowed, log_total_c, delta_c, COLUMN_FORMS
    )
    back_q, back_k, back_v = (
        lax.all_to_all(col_grads[0], "seq", split_axis=1, concat_axis=2, tiled=True),
        lax.all_to_all(col_grads[1], "seq", split_axis=1, concat_axis=2, tiled=True),
        lax.all_to_all(col_grads[2], "seq", split_axis=1, concat_axis=2, tiled=True),
    )
    returned = (back_q, back_k, back_v)
    input_sum = input_terms(row_grads, w_qkv) + input_terms(returned, w_qkv)
    weight_part = weight_terms(tokens, row_grads) + weight_terms(tokens, returned)
    input_grad = input_sum.astype(jnp.bfloat16)
    partial_sum = lax.psum_scatter(
        weight_part.astype(jnp.bfloat16), "seq", scatter_dimension=1, tiled=True
    )
    w_grads = lax.psum_scatter(partial_sum, "dp", scatter_dimension=2, tiled=True).astype(
        jnp.float32
    )
    return (attention, input_grad, w_grads)


def solution(mesh):
    in_specs = (P("dp", "seq", None, None), P("dp"), P(), P("dp", "seq", None, None))
    out_specs = (P("dp", "seq", None, None), P("dp", "seq", None, None), P(None, "seq", "dp"))
    return jax.shard_map(body, mesh=mesh, in_specs=in_specs, out_specs=out_specs, check_vma=False)
```

profile of v0, /device:TPU:0, one launch (start us, length us, event | category | flops | bytes accessed | tf_op | source)
XLA Modules:
  0.0 1214.6 jit_solution(10678463840851201339)
XLA Ops:
  7.2 16.6 %convert_bitcast_fusion = bf16[3,1,16,128,1024]{3,4,2,0,1:T(8,128)(2,1)S(1)} fusion(bf16[3,1024,1024]{2,1,0:T(8,128)(2,1)} %param.6, bf16[1,16,128,1024]{3,2,1,0:T(8,128)(2,1)} %param.4), kind=kOutput, calls=%fused_computation.4 | convolution fusion | flops 12891193344 | bytes 23068672 | tf_op jit(solution)/shard_map/srcd,jdf->jsrcf/dot_general | solution.py:24
  28.6 6.7 copy.184
  35.4 6.3 all-to-all-start
  41.7 6.8 copy.187
  48.4 87.4 %all-to-all-done = bf16[1,16,128,8,128]{4,3,1,0,2:T(8,128)(2,1)} async-done(((bf16[1,16,128,8,128]{4,3,1,0,2:T(8,128)(2,1)}), bf16[1,16,128,8,128]{4,3,1,0,2:T(8,128)(2,1)}, u32[]{:S(2)}, u32[]{:S(2)}) %all-to-all-start) | async-done | bytes 4194336 | tf_op jit(solution)/shard_map/all_to_all | solution.py:96
  140.4 6.7 copy.192
  147.1 87.3 %all-to-all-done.1 = bf16[1,16,128,8,128]{4,3,1,0,2:T(8,128)(2,1)} async-done(((bf16[1,16,128,8,128]{4,3,1,0,2:T(8,128)(2,1)}), bf16[1,16,128,8,128]{4,3,1,0,2:T(8,128)(2,1)}, u32[]{:S(2)}, u32[]{:S(2)}) %all-to-all-start.1) | async-done | bytes 4194336 | tf_op jit(solution)/shard_map/all_to_all | solution.py:95
  263.7 69.4 %all-to-all-done.3 = bf16[1,16,128,8,128]{4,3,1,0,2:T(8,128)(2,1)} async-done(((bf16[1,16,128,8,128]{4,3,1,0,2:T(8,128)(2,1)}), bf16[1,16,128,8,128]{4,3,1,0,2:T(8,128)(2,1)}, u32[]{:S(2)}, u32[]{:S(2)}) %all-to-all-start.3) | async-done | bytes 4194336 | tf_op jit(solution)/shard_map/all_to_all | solution.py:97
  354.4 5.0 all-to-all-start.7
  359.8 5.5 fusion.23
  379.3 74.3 %all-to-all-done.7 = bf16[1,16,128,8,128]{4,3,1,0,2:T(8,128)(2,1)} async-done(((bf16[1,16,128,8,128]{4,3,1,0,2:T(8,128)(2,1)}), bf16[1,16,128,8,128]{4,3,1,0,2:T(8,128)(2,1)}, u32[]{:S(2)}, u32[]{:S(2)}) %all-to-all-start.7) | async-done | bytes 4194336 | tf_op jit(solution)/shard_map/all_to_all | solution.py:123
  456.9 12.6 %fusion.70 = f32[1,128,16,8,128]{1,4,3,2,0:T(8,128)} fusion(f32[16,8,128,128]{3,2,1,0:T(8,128)} %copy-done, f32[128,16,8]{0,2,1:T(8,128)S(1)} %get-tuple-element.25, pred[128,16,128]{0,2,1:T(8,128)(4,1)S(1)} %broadcast_and_fusion, bf16[128,16,8,128]{3,2,1,0:T(8,128)(2,1)} %bitcast.393), kind=kOutput, calls=%fused_computation.86 | convolution fusion | flops 547356672 | bytes 21299200 | tf_op jit(solution)/shard_map/sqchk,skche->sqche/dot_general | solution.py:37
  469.6 9.4 copy.197
  478.9 5.3 all-to-all-start.4
  494.1 174.0 %all-to-all-done.4 = f32[1,128,16,8,128]{4,3,2,0,1:T(8,128)} async-done(((f32[1,128,16,8,128]{4,3,2,0,1:T(8,128)}), f32[1,128,16,8,128]{4,3,2,0,1:T(8,128)}, u32[]{:S(2)}, u32[]{:S(2)}) %all-to-all-start.4) | async-done | bytes 8388640 | tf_op jit(solution)/shard_map/all_to_all | solution.py:105
  668.1 7.7 copy.198
  675.9 9.3 copy.199
  685.1 15.4 %bitcast_convert_fusion = (f32[16,128,8,128]{1,3,2,0:T(8,128)}, bf16[1,16,128,8,128]{2,4,3,1,0:T(8,128)(2,1)}) fusion(f32[16,128,8]{1,2,0:T(8,128)S(1)} %get-tuple-element.19, f32[1,16,128,8,128]{2,4,3,1,0:T(8,128)} %copy.199, f32[16,128,8]{1,2,0:T(8,128)S(1)} %get-tuple-element.21, f32[16,128,8]{1,2,0:T(8,128)S(1)} %get-tuple-element.20, ...), kind=kOutput, calls=%fused_computation.59 | convolution fusion | flops 559939584 | bytes 34078720 | tf_op jit(solution)/shard_map/srqhk,srkhe->srqhe/dot_general | solution.py:37
  700.5 9.4 copy.244
  709.9 6.9 multiply_reduce_fusion
  721.6 6.6 convert_bitcast_fusion.1
  732.8 5.5 all-to-all-start.11
  739.9 13.8 %fusion.41 = bf16[128,16,8,128]{0,3,2,1:T(8,128)(2,1)} fusion(f32[16,8,128,128]{3,2,1,0:T(8,128)} %copy-done, f32[128,16,8]{0,2,1:T(8,128)S(1)} %sub.117, f32[128,16,8]{0,2,1:T(8,128)S(1)} %sub.114, pred[128,16,128]{0,2,1:T(8,128)(4,1)S(1)} %broadcast_and_fusion, bf16[128,16,8,128]{3,0,2,1:T(8,128)(2,1)} %bitcast.401, bf16[128,16,8,128]{3,2,1,0:T(8,128)(2,1)} %bitcast.394), kind=kOutput, calls=%fused_computation.56 | convolution fusion | flops 551550976 | bytes 21364736 | tf_op jit(solution)/shard_map/sqche,skche->sqchk/dot_general | solution.py:48
  753.7 5.9 fusion.37
  759.6 6.6 copy.223
  766.2 66.1 %all-to-all-done.11 = bf16[1,128,16,8,128]{4,3,2,0,1:T(8,128)(2,1)} async-done(((bf16[1,128,16,8,128]{4,3,2,0,1:T(8,128)(2,1)}), bf16[1,128,16,8,128]{4,3,2,0,1:T(8,128)(2,1)}, u32[]{:S(2)}, u32[]{:S(2)}) %all-to-all-start.11) | async-done | bytes 4194336 | tf_op jit(solution)/shard_map/all_to_all | solution.py:134
  836.9 8.6 fusion.38
  845.5 6.8 copy.227
  852.3 78.6 %all-to-all-done.9 = bf16[1,128,16,8,128]{4,3,2,0,1:T(8,128)(2,1)} async-done(((bf16[1,128,16,8,128]{4,3,2,0,1:T(8,128)(2,1)}), bf16[1,128,16,8,128]{4,3,2,0,1:T(8,128)(2,1)}, u32[]{:S(2)}, u32[]{:S(2)}) %all-to-all-start.9) | async-done | bytes 4194336 | tf_op jit(solution)/shard_map/all_to_all | solution.py:132
  935.7 6.8 copy.209
  942.5 9.5 fusion.75
  952.1 6.4 copy.212
  963.2 7.3 stack_reshape.29
  970.8 9.5 fusion.40
  983.6 6.4 copy.210
  990.0 8.4 multiply_convert_fusion.2
  998.4 6.4 copy.211
  1009.6 7.5 stack_reshape.27
  1017.1 12.6 %all-to-all-done.10 = bf16[1,128,16,8,128]{4,3,2,0,1:T(8,128)(2,1)} async-done(((bf16[1,128,16,8,128]{4,3,2,0,1:T(8,128)(2,1)}), bf16[1,128,16,8,128]{4,3,2,0,1:T(8,128)(2,1)}, u32[]{:S(2)}, u32[]{:S(2)}) %all-to-all-start.10) | async-done | bytes 4194336 | tf_op jit(solution)/shard_map/all_to_all | solution.py:133
  1034.5 7.3 stack_reshape.28
  1041.8 20.5 %fusion.21 = f32[3,1024,1024,1]{2,1,0,3:T(8,128)} fusion(bf16[1,1,16,128,1024]{4,3,0,2,1:T(8,128)(2,1)} %stack_reshape.29, bf16[1,1,16,128,1024]{4,3,0,2,1:T(8,128)(2,1)} %stack_reshape.28, bf16[1,1,16,128,1024]{4,3,0,2,1:T(8,128)(2,1)} %stack_reshape.27, bf16[1,16,128,1024]{3,2,1,0:T(8,128)(2,1)} %param.4), kind=kOutput, calls=%fused_computation.40 | convolution fusion | flops 12897484800 | bytes 29360128 | tf_op jit(solution)/shard_map/srcd,jsrcf->jdf/dot_general | solution.py:69
  1062.3 21.1 %fusion.15 = bf16[3,1024,1024]{1,2,0:T(8,128)(2,1)} fusion(f32[3,1024,1024,1]{2,1,0,3:T(8,128)} %fusion.21, bf16[1,16,128,1024]{3,2,1,0:T(8,128)(2,1)} %param.4, bf16[1,1,16,128,1024]{4,3,0,2,1:T(8,128)(2,1)S(1)} %copy-done.8, bf16[1,1,16,128,1024]{4,3,0,2,1:T(8,128)(2,1)} %copy.211, bf16[1,1,16,128,1024]{4,3,0,2,1:T(8,128)(2,1)} %copy.210), kind=kOutput, calls=%fused_computation.34 | convolution fusion | flops 12903776256 | bytes 35651584 | tf_op jit(solution)/shard_map/srcd,jsrcf->jdf/dot_general | solution.py:69
  1083.4 14.4 %copy.263 = bf16[3,1024,1024]{2,0,1:T(4,128)(2,1)} copy(bf16[3,1024,1024]{1,2,0:T(8,128)(2,1)} %fusion.15) | data formatting | bytes 12582912
  1097.8 10.2 copy.267
  1108.0 6.6 copy.233
  1114.6 18.9 %fusion.17 = f32[16,128,1024,1]{2,1,3,0:T(8,128)} fusion(bf16[3,1024,1024]{2,1,0:T(8,128)(2,1)} %param.6, bf16[1,1,16,128,1024]{4,3,0,2,1:T(8,128)(2,1)} %copy.212, bf16[1,1,16,128,1024]{4,3,0,2,1:T(8,128)(2,1)} %copy.211, bf16[1,1,16,128,1024]{4,3,0,2,1:T(8,128)(2,1)} %copy.210), kind=kOutput, calls=%fused_computation.36 | convolution fusion | flops 12897484800 | bytes 27262976 | tf_op jit(solution)/shard_map/jsrcf,jdf->srcd/dot_general | solution.py:64
  1133.5 43.3 %reduce-scatter.7.cloned.1.call-done = bf16[128,3072]{1,0:T(8,128)(2,1)} async-done(((bf16[1024,3072]{1,0:T(8,128)(2,1)}), bf16[128,3072]{1,0:T(8,128)(2,1)}) %reduce-scatter.7.cloned.1.call-update) | async-done | bytes 786448
  1181.1 20.7 %fusion.39 = bf16[1,16,128,1024]{3,2,1,0:T(8,128)(2,1)} fusion(f32[16,128,1024,1]{2,1,3,0:T(8,128)} %fusion.17, bf16[3,1024,1024]{2,1,0:T(8,128)(2,1)} %param.6, bf16[1,1,16,128,1024]{4,3,0,2,1:T(8,128)(2,1)} %stack_reshape.29, bf16[1,1,16,128,1024]{4,3,0,2,1:T(8,128)(2,1)} %stack_reshape.28, bf16[1,1,16,128,1024]{4,3,0,2,1:T(8,128)(2,1)} %stack_reshape.27), kind=kOutput, calls=%fused_computation.54 | convolution fusion | flops 12901679104 | bytes 31457280 | tf_op jit(solution)/shard_map/jsrcf,jdf->srcd/dot_general | solution.py:64
  (97 shorter events, 134.9 us)
Async XLA Ops:
  35.4 100.4 %all-to-all-start = ((bf16[1,16,128,8,128]{4,3,1,0,2:T(8,128)(2,1)}), bf16[1,16,128,8,128]{4,3,1,0,2:T(8,128)(2,1)}, u32[]{:S(2)}, u32[]{:S(2)}) async-start(bf16[1,16,128,8,128]{4,3,1,0,2:T(8,128)(2,1)} %copy.184), calls=%async_computation | async-start | bytes 8388608 | tf_op jit(solution)/shard_map/all_to_all | solution.py:96
  135.8 98.6 %all-to-all-start.1 = ((bf16[1,16,128,8,128]{4,3,1,0,2:T(8,128)(2,1)}), bf16[1,16,128,8,128]{4,3,1,0,2:T(8,128)(2,1)}, u32[]{:S(2)}, u32[]{:S(2)}) async-start(bf16[1,16,128,8,128]{4,3,1,0,2:T(8,128)(2,1)} %copy.187), calls=%async_computation.1 | async-start | bytes 8388608 | tf_op jit(solution)/shard_map/all_to_all | solution.py:95
  234.4 98.7 %all-to-all-start.3 = ((bf16[1,16,128,8,128]{4,3,1,0,2:T(8,128)(2,1)}), bf16[1,16,128,8,128]{4,3,1,0,2:T(8,128)(2,1)}, u32[]{:S(2)}, u32[]{:S(2)}) async-start(bf16[1,16,128,8,128]{4,3,1,0,2:T(8,128)(2,1)} %copy.192), calls=%async_computation.3 | async-start | bytes 8388608 | tf_op jit(solution)/shard_map/all_to_all | solution.py:97
  246.2 7.5 copy-start.4
  253.7 3.1 copy-start.3
  256.8 3.2 copy-start
  333.1 9.2 all-to-all-start.5
  342.3 12.1 all-to-all-start.2
  349.3 1.9 copy-start.1
  354.4 99.1 %all-to-all-start.7 = ((bf16[1,16,128,8,128]{4,3,1,0,2:T(8,128)(2,1)}), bf16[1,16,128,8,128]{4,3,1,0,2:T(8,128)(2,1)}, u32[]{:S(2)}, u32[]{:S(2)}) async-start(bf16[1,16,128,8,128]{4,3,1,0,2:T(8,128)(2,1)} %copy.262), calls=%async_computation.7 | async-start | bytes 8388608 | tf_op jit(solution)/shard_map/all_to_all | solution.py:123
  365.3 6.1 copy-start.6
  453.6 25.4 %all-to-all-start.6 = ((f32[8,1,2048]{2,1,0:T(1,128)}), f32[8,1,2048]{2,1,0:T(1,128)S(1)}, u32[]{:S(2)}, u32[]{:S(2)}) async-start(f32[8,1,2048]{2,1,0:T(1,128)} %reshape.534), calls=%async_computation.6 | async-start | bytes 131072 | tf_op jit(solution)/shard_map/all_to_all | solution.py:125
  478.9 189.2 %all-to-all-start.4 = ((f32[1,128,16,8,128]{4,3,2,0,1:T(8,128)}), f32[1,128,16,8,128]{4,3,2,0,1:T(8,128)}, u32[]{:S(2)}, u32[]{:S(2)}) async-start(f32[1,128,16,8,128]{4,3,2,0,1:T(8,128)} %copy.197), calls=%async_computation.4 | async-start | bytes 16777216 | tf_op jit(solution)/shard_map/all_to_all | solution.py:105
  718.2 14.6 %all-to-all-start.8 = ((f32[8,1,2048]{2,1,0:T(1,128)}), f32[8,1,2048]{2,1,0:T(1,128)S(1)}, u32[]{:S(2)}, u32[]{:S(2)}) async-start(f32[8,1,2048]{2,1,0:T(1,128)} %reshape.536), calls=%async_computation.8 | async-start | bytes 131072 | tf_op jit(solution)/shard_map/all_to_all | solution.py:126
  732.8 99.5 %all-to-all-start.11 = ((bf16[1,128,16,8,128]{4,3,2,0,1:T(8,128)(2,1)}), bf16[1,128,16,8,128]{4,3,2,0,1:T(8,128)(2,1)}, u32[]{:S(2)}, u32[]{:S(2)}) async-start(bf16[1,128,16,8,128]{4,3,2,0,1:T(8,128)(2,1)} %copy.229), calls=%async_computation.11 | async-start | bytes 8388608 | tf_op jit(solution)/shard_map/all_to_all | solution.py:134
  739.9 13.8 %copy-start.5 = (bf16[1,8,16,16,8,128]{5,2,1,4,3,0:T(8,128)(2,1)S(1)}, bf16[1,8,16,16,8,128]{5,2,1,4,3,0:T(8,128)(2,1)}, u32[]{:S(2)}) copy-start(bf16[1,8,16,16,8,128]{5,2,1,4,3,0:T(8,128)(2,1)} %copy-done.4) | copy-start | bytes 12582916
  832.4 98.6 %all-to-all-start.9 = ((bf16[1,128,16,8,128]{4,3,2,0,1:T(8,128)(2,1)}), bf16[1,128,16,8,128]{4,3,2,0,1:T(8,128)(2,1)}, u32[]{:S(2)}, u32[]{:S(2)}) async-start(bf16[1,128,16,8,128]{4,3,2,0,1:T(8,128)(2,1)} %copy.223), calls=%async_computation.9 | async-start | bytes 8388608 | tf_op jit(solution)/shard_map/all_to_all | solution.py:132
  930.9 98.8 %all-to-all-start.10 = ((bf16[1,128,16,8,128]{4,3,2,0,1:T(8,128)(2,1)}), bf16[1,128,16,8,128]{4,3,2,0,1:T(8,128)(2,1)}, u32[]{:S(2)}, u32[]{:S(2)}) async-start(bf16[1,128,16,8,128]{4,3,2,0,1:T(8,128)(2,1)} %copy.227), calls=%async_computation.10 | async-start | bytes 8388608 | tf_op jit(solution)/shard_map/all_to_all | solution.py:133
  935.7 241.2 %reduce-scatter.7.cloned.1.call-start = ((), (), s32[]{:S(2)}) async-start(), calls=%async_computation.15 | async-start | bytes 7077888
  970.8 9.5 copy-start.2
  980.3 3.3 copy-start.7
  1041.8 20.5 %copy-start.8 = (bf16[1,1,16,128,1024]{4,3,0,2,1:T(8,128)(2,1)S(1)}, bf16[1,1,16,128,1024]{4,3,0,2,1:T(8,128)(2,1)}, u32[]{:S(2)}) copy-start(bf16[1,1,16,128,1024]{4,3,0,2,1:T(8,128)(2,1)} %copy.212) | copy-start | bytes 12582916
  1108.0 97.8 %reduce-scatter.5.cloned.1.call-start = ((), (), s32[]{:S(2)}) async-start(), calls=%async_computation.14 | async-start | bytes 983040 | tf_op jit(solution)/shard_map/reduce_scatter | solution.py:143
Sparse Core Ops, SparseCore 0:
  1108.1 68.6 reduce-scatter.6
  1181.2 24.4 reduce-scatter.4
where the time goes:
time: 1220 us; the launch traced here: 1210 us
  waiting for transfers between devices  702 us (58%)
  local copies, waits for them, and re-layouts  227 us (19%)
  matrix products  200 us (16%)
  starting transfers between devices  54.6 us (4%)
  other arithmetic  16.1 us (1%)
  between operations  15.4 us (1%)
    all_to_all x1, waiting for transfers between devices, body(): lax.all_to_all(col_mixed_c, 'seq', split_axis=1, concat_axis=2, tiled=True)  174 us
    all_to_all x1, waiting for transfers between devices, body(): lax.all_to_all(key_r, 'seq', split_axis=2, concat_axis=1, tiled=True)  87.4 us
    all_to_all x1, waiting for transfers between devices, body(): lax.all_to_all(query_r, 'seq', split_axis=2, concat_axis=1, tiled=True)  87.3 us
    all_to_all x1, waiting for transfers between devices, body(): lax.all_to_all(col_grads[0], 'seq', split_axis=1, concat_axis=2, tiled=True)  78.6 us
    all_to_all x1, waiting for transfers between devices, body(): lax.all_to_all(grad_h, 'seq', split_axis=2, concat_axis=1, tiled=True)  74.3 us
    all_to_all x1, waiting for transfers between devices, body(): lax.all_to_all(value_r, 'seq', split_axis=2, concat_axis=1, tiled=True)  69.4 us
    all_to_all x1, waiting for transfers between devices, body(): lax.all_to_all(col_grads[2], 'seq', split_axis=1, concat_axis=2, tiled=True)  66.1 us
    unnamed x35, local copies, waits for them, and re-layouts  59.3 us
  transfers between devices with their start and end apart: 14, of which 11 were waited for; matrix products, arithmetic and copies ran while one was open for 23% of the time, Pallas kernels for 0%

commit v1 on v0

v1 whole, which is shorter than its diff:
```python
import functools
import math

import jax
import jax.numpy as jnp
from jax import lax
from jax.experimental import pallas as pl
from jax.experimental.pallas import tpu as pltpu
from jax.sharding import PartitionSpec as P

HEADS = 8
GROUPS = 4
NONE = -1e30
FLOOR = -1e29
FAR = 1 << 20
NT = (((1,), (1,)), ((), ()))
NN = (((1,), (0,)), ((), ()))
TN = (((0,), (0,)), ((), ()))
VMEM_LIMIT = 48 * 1024 * 1024


def dot(left, right, form):
    return lax.dot_general(left, right, form, preferred_element_type=jnp.float32)


def spread(values, first, packed, width):
    zero = jnp.zeros((values.shape[0], width), values.dtype)
    lines = []
    for i in range(packed):
        own = values[:, (first + i) * width : (first + i + 1) * width]
        lines.append(jnp.concatenate([own if j == i else zero for j in range(packed)], axis=1))
    return jnp.concatenate(lines, axis=0)


def tile_lanes(values, times):
    return jnp.concatenate([values] * times, axis=1) if times > 1 else values


def part_stats(query, key, value, grad, mask, packed, store):
    width = key.shape[1] // HEADS
    scaling = 1.0 / math.sqrt(width)
    for first in range(0, HEADS, packed):
        lanes = slice(first * width, (first + packed) * width)
        scores = dot(key[:, lanes], spread(query, first, packed, width), NT) * scaling
        grad_prob = dot(value[:, lanes], spread(grad, first, packed, width), NT)
        scores = jnp.where(mask, scores, NONE)
        highest = jnp.maximum(jnp.max(scores, axis=0, keepdims=True), FLOOR)
        weights = jnp.exp(scores - highest)
        total = jnp.sum(weights, axis=0, keepdims=True)
        product = jnp.sum(weights * grad_prob, axis=0, keepdims=True)
        store(first, highest, total, product)


def part_grads(query, key, value, grad, mask, packed, load, store):
    width = key.shape[1] // HEADS
    scaling = 1.0 / math.sqrt(width)
    count = query.shape[0]
    for first in range(0, HEADS, packed):
        lanes = slice(first * width, (first + packed) * width)
        query_d = spread(query, first, packed, width)
        grad_d = spread(grad, first, packed, width)
        joint, inverse, delta = load(first)
        scores = dot(key[:, lanes], query_d, NT) * scaling
        grad_prob = dot(value[:, lanes], grad_d, NT)
        scores = jnp.where(mask, scores, NONE)
        prob = jnp.exp(scores - joint) * inverse
        grad_score = (prob * (grad_prob - delta)).astype(jnp.bfloat16)
        prob = prob.astype(jnp.bfloat16)
        grad_value = dot(prob, grad_d, NN)
        grad_key = dot(grad_score, query_d, NN) * scaling
        mixed, grad_query = [], []
        for i in range(packed):
            ours = slice(i * count, (i + 1) * count)
            head = slice((first + i) * width, (first + i + 1) * width)
            mixed.append(dot(prob[:, ours], value[:, head], TN))
            grad_query.append(dot(grad_score[:, ours], key[:, head], TN) * scaling)
        store(
            lanes,
            jnp.concatenate(mixed, axis=1),
            jnp.concatenate(grad_query, axis=1),
            grad_key,
            grad_value,
        )


def row_mask(scalars, row, count, packed):
    keys = lax.broadcasted_iota(jnp.int32, (count, count), 0)
    queries = lax.broadcasted_iota(jnp.int32, (count, count), 1)
    limit = scalars[0] - row * count
    allowed = (keys < queries) & (keys < limit) | (keys == queries)
    return tile_lanes(allowed.astype(jnp.int32), packed) > 0


def row_stats_kernel(packed, scalars, query, key, value, grad, stats):
    count = key.shape[1]
    mask = row_mask(scalars, scalars[1] + pl.program_id(0), count, packed)

    def store(first, *items):
        for j, item in enumerate(items):
            stats[0, j : j + 1, first * count : (first + packed) * count] = item

    part_stats(query[0], key[0], value[0], grad[0], mask, packed, store)


def row_grads_kernel(packed, scalars, stats, query, key, value, grad, mixed, g_query, g_key, g_value):
    count = key.shape[1]
    mask = row_mask(scalars, scalars[1] + pl.program_id(0), count, packed)

    def load(first):
        return [stats[0, j : j + 1, first * count : (first + packed) * count] for j in range(3)]

    def store(lanes, mixed_v, query_v, key_v, value_v):
        mixed[0, :, lanes] = mixed_v.astype(mixed.dtype)
        g_query[0, :, lanes] = query_v.astype(g_query.dtype)
        g_key[0, :, lanes] = key_v.astype(g_key.dtype)
        g_value[0, :, lanes] = value_v.astype(g_value.dtype)

    part_grads(query[0], key[0], value[0], grad[0], mask, packed, load, store)


def col_mask(scalars, key_rows, query_rows, column, stride):
    rows = key_rows[...]
    rows = jnp.where(rows * stride + column < scalars[0], rows, FAR)
    times = query_rows.shape[1] // rows.shape[1]
    return tile_lanes(rows, times) < query_rows[0:1, :]


def col_stats_kernel(
    packed, stride, scalars, key_rows, query_rows, query, guest, key, value, grad, guest_grad, stats, crossed
):
    count = 2 * query.shape[1]
    half = query.shape[1]
    for i in range(key.shape[0]):
        column = scalars[1] + pl.program_id(0) * key.shape[0] + i
        mask = col_mask(scalars, key_rows, query_rows, column, stride)

        def store(first, *items):
            lanes = slice(first * count, (first + packed) * count)
            for j, item in enumerate(items):
                stats[i, j : j + 1, lanes] = item
                pieces = []
                for h in range(packed):
                    pieces.append(item[:, h * count + half : (h + 1) * count])
                    pieces.append(item[:, h * count : h * count + half])
                crossed[i, j : j + 1, lanes] = jnp.concatenate(pieces, axis=1)

        query_v = jnp.concatenate([query[i], guest[i]], axis=0)
        grad_v = jnp.concatenate([grad[i], guest_grad[i]], axis=0)
        part_stats(query_v, key[i], value[i], grad_v, mask, packed, store)


def join(parts):
    highs = [jnp.where(total > 0.0, high, NONE) for high, total, _ in parts]
    joint = functools.reduce(jnp.maximum, highs)
    factors = [jnp.exp(high - joint) for high in highs]
    total = sum(part[1] * factor for part, factor in zip(parts, factors))
    product = sum(part[2] * factor for part, factor in zip(parts, factors))
    inverse = jnp.where(total > 0.0, 1.0 / jnp.where(total > 0.0, total, 1.0), 0.0)
    return joint, inverse, product * inverse


def col_grads_kernel(
    packed, stride, scalars, key_rows, query_rows, row_part, own_part, other_part,
    query, guest, key, value, grad, guest_grad,
    final, mixed, guest_mixed, g_query, g_guest, g_key, g_value,
):
    half = query.shape[1]
    count = 2 * half
    for i in range(key.shape[0]):
        column = scalars[1] + pl.program_id(0) * key.shape[0] + i
        mask = col_mask(scalars, key_rows, query_rows, column, stride)

        def load(first):
            lanes = slice(first * count, (first + packed) * count)
            parts = [
                [part[i, j : j + 1, lanes] for j in range(3)]
                for part in (row_part, own_part, other_part)
            ]
            result = join(parts)
            for j in range(3):
                final[i, j : j + 1, lanes] = result[j]
            return result

        def store(lanes, mixed_v, query_v, key_v, value_v):
            mixed[i, :, lanes] = mixed_v[:half].astype(mixed.dtype)
            guest_mixed[i, :, lanes] = mixed_v[half:].astype(mixed.dtype)
            g_query[i, :, lanes] = query_v[:half].astype(g_query.dtype)
            g_guest[i, :, lanes] = query_v[half:].astype(g_query.dtype)
            g_key[i, :, lanes] = key_v.astype(g_key.dtype)
            g_value[i, :, lanes] = value_v.astype(g_value.dtype)

        query_v = jnp.concatenate([query[i], guest[i]], axis=0)
        grad_v = jnp.concatenate([grad[i], guest_grad[i]], axis=0)
        part_grads(query_v, key[i], value[i], grad_v, mask, packed, load, store)


def call(kernel, steps, in_specs, out_specs, out_shapes, flops, operands):
    return pl.pallas_call(
        kernel,
        grid=(steps,),
        in_specs=in_specs,
        out_specs=out_specs,
        out_shape=out_shapes,
        compiler_params=pltpu.CompilerParams(vmem_limit_bytes=VMEM_LIMIT),
        cost_estimate=pl.CostEstimate(flops=flops, bytes_accessed=flops // 1000, transcendentals=0),
    )(*operands)


def block(shape, offset=0):
    rest = (0,) * (len(shape) - 1)
    return pl.BlockSpec(shape, lambda s: (s + offset,) + rest)


def whole(shape):
    return pl.BlockSpec(shape, lambda s: (0,) * len(shape))


SCALARS = pl.BlockSpec(memory_space=pltpu.SMEM)


def row_stats(scalars, query, key, value, grad):
    rows, count, width = query.shape
    packed = max(1, min(HEADS, 256 // count))
    one = block((1, count, width))
    return call(
        functools.partial(row_stats_kernel, packed),
        rows,
        [SCALARS] + [one] * 4,
        block((1, 3, HEADS * count)),
        jax.ShapeDtypeStruct((rows, 3, HEADS * count), jnp.float32),
        4 * rows * count * count * width * 4,
        (scalars, query, key, value, grad),
    )


def row_grads(scalars, stats, query, key, value, grad):
    rows, count, width = query.shape
    packed = max(1, min(HEADS, 256 // count))
    one = block((1, count, width))
    return call(
        functools.partial(row_grads_kernel, packed),
        rows,
        [SCALARS, block((1, 3, HEADS * count))] + [one] * 4,
        [one] * 4,
        [jax.ShapeDtypeStruct(query.shape, jnp.bfloat16)] * 4,
        12 * rows * count * count * width * 4,
        (scalars, stats, query, key, value, grad),
    )


def col_sizes(query, key):
    half = query.shape[1]
    packed = max(1, min(HEADS, 256 // (2 * half)))
    columns = key.shape[0]
    step = 2 if columns % 2 == 0 else 1
    return half, packed, columns, step


def col_stats(scalars, key_rows, query_rows, query, guest, key, value, grad, guest_grad, offset, stride):
    half, packed, columns, step = col_sizes(query, key)
    width = key.shape[2]
    own = block((step, half, width), offset // step)
    visitor = block((step, half, width))
    keys = block((step, key.shape[1], width))
    stat = block((step, 3, HEADS * 2 * half))
    shape = jax.ShapeDtypeStruct((columns, 3, HEADS * 2 * half), jnp.float32)
    return call(
        functools.partial(col_stats_kernel, packed, stride),
        columns // step,
        [SCALARS, whole(key_rows.shape), whole(query_rows.shape), own, visitor, keys, keys, own, visitor],
        [stat, stat],
        [shape, shape],
        4 * columns * key.shape[1] * 2 * half * width * 4,
        (scalars, key_rows, query_rows, query, guest, key, value, grad, guest_grad),
    )


def col_grads(
    scalars, key_rows, query_rows, row_part, own_part, other_part,
    query, guest, key, value, grad, guest_grad, offset, stride,
):
    half, packed, columns, step = col_sizes(query, key)
    width = key.shape[2]
    own = block((step, half, width), offset // step)
    visitor = block((step, half, width))
    keys = block((step, key.shape[1], width))
    stat = block((step, 3, HEADS * 2 * half))
    stat_off = block((step, 3, HEADS * 2 * half), offset // step)
    shape = jax.ShapeDtypeStruct((columns, 3, HEADS * 2 * half), jnp.float32)
    small = jax.ShapeDtypeStruct((columns, half, width), jnp.bfloat16)
    large = jax.ShapeDtypeStruct(key.shape, jnp.bfloat16)
    return call(
        functools.partial(col_grads_kernel, packed, stride),
        columns // step,
        [SCALARS, whole(key_rows.shape), whole(query_rows.shape), stat_off, stat, stat]
        + [own, visitor, keys, keys, own, visitor],
        [stat, visitor, visitor, visitor, visitor, keys, keys],
        [shape, small, small, small, small, large, large],
        12 * columns * key.shape[1] * 2 * half * width * 4,
        (scalars, key_rows, query_rows, row_part, own_part, other_part)
        + (query, guest, key, value, grad, guest_grad),
    )


def product(values, weight):
    return jnp.einsum("...d,df->...f", values, weight, preferred_element_type=jnp.float32)


def product_t(values, weight):
    return jnp.einsum("...f,df->...d", values, weight, preferred_element_type=jnp.float32)


def weight_product(values, grads):
    return jnp.einsum("abd,abf->df", values, grads, preferred_element_type=jnp.float32)


def narrow(values):
    return values.astype(jnp.bfloat16)


def body(tokens, lengths, w_qkv, out_grad):
    seq_count = lax.axis_size("seq")
    seq_index = lax.axis_index("seq")
    chips = seq_count // 2
    chip, core = seq_index // 2, seq_index % 2
    seq_local, row_local, columns, width = tokens.shape
    half_cols = columns // 2
    chip_rows = 2 * row_local
    group = half_cols // GROUPS
    w_q, w_k, w_v = w_qkv[0], w_qkv[1], w_qkv[2]

    def pairs(links):
        return [(2 * a + c, 2 * b + c) for a, b in links for c in (0, 1)]

    swap = [(i, i ^ 1) for i in range(seq_count)]
    up = {k: pairs([(z - 1, z) for z in range(k, chips - 1)]) for k in range(1, chips - 1)}
    down = {k: [(b, a) for a, b in up[k]] for k in up}
    guest_up = pairs([(chips - 2, chips - 1)])
    guest_down = pairs([(chips - 1, chips - 2)])

    def send(values, perm):
        return lax.ppermute(values, "seq", perm)

    def to_columns(values, axis, row_axis):
        mine = lax.dynamic_slice_in_dim(values, core * half_cols, half_cols, axis)
        others = lax.dynamic_slice_in_dim(values, (1 - core) * half_cols, half_cols, axis)
        return jnp.concatenate([mine, send(others, swap)], axis=row_axis)

    def to_rows(values, axis, row_axis):
        mine = lax.slice_in_dim(values, 0, row_local, axis=row_axis)
        others = send(lax.slice_in_dim(values, row_local, chip_rows, axis=row_axis), swap)
        return jnp.where(
            core == 0,
            jnp.concatenate([mine, others], axis=axis),
            jnp.concatenate([others, mine], axis=axis),
        )

    tokens_r, grad_r = tokens[0], out_grad[0]
    limit = lengths[0]
    tokens_c = to_columns(jnp.swapaxes(tokens_r, 0, 1), 0, 1)
    grad_c = to_columns(jnp.swapaxes(grad_r, 0, 1), 0, 1)

    order = (jnp.arange(chip_rows, dtype=jnp.int32) + core * row_local) % chip_rows
    key_ids = []
    for k in range(chips - 2, -1, -1):
        valid = (chip >= k) & (chip <= chips - 2) if k > 0 else chip >= 0
        key_ids.append(jnp.where(valid, (chip - k) * chip_rows + order, FAR))
    key_ids = jnp.concatenate(key_ids)
    query_ids = jnp.concatenate(
        [chip * chip_rows + order, jnp.where(chip == chips - 2, (chip + 1) * chip_rows + order, -1)]
    )
    packed = max(1, min(HEADS, 256 // (2 * chip_rows)))
    lane = min(128, packed * 2 * chip_rows)
    key_rows = jnp.broadcast_to(key_ids[:, None], (key_ids.shape[0], lane))
    query_rows = jnp.broadcast_to(jnp.tile(query_ids, packed)[None], (8, packed * 2 * chip_rows))

    blocks = []
    for g in range(GROUPS):
        held = [tokens_c[g * group : (g + 1) * group]]
        for k in range(1, chips - 1):
            held.append(send(held[-1], up[k]))
        blocks.append(jnp.concatenate(held[::-1], axis=1))

    query_c = narrow(product(tokens_c, w_q))
    guests, guest_grads = [], []
    for g in range(GROUPS):
        guests.append(send(query_c[g * group : (g + 1) * group], guest_down))
        guest_grads.append(send(grad_c[g * group : (g + 1) * group], guest_down))

    query_r, key_r, value_r = (narrow(product(tokens_r, w)) for w in (w_q, w_k, w_v))
    row_scalars = jnp.stack([limit, seq_index * row_local]).astype(jnp.int32)
    row_part = row_stats(row_scalars, query_r, key_r, value_r, grad_r)
    row_part = row_part.reshape(row_local, 3, HEADS, columns).transpose(3, 1, 2, 0)
    row_part = to_columns(row_part, 0, 3)
    row_part = jnp.concatenate([row_part, send(row_part, guest_down)], axis=3)
    row_part = row_part.reshape(half_cols, 3, HEADS * 2 * chip_rows)

    cross = guest_up + guest_down
    finals, mixed_c, w_parts, own_terms = [], [], [], []
    for g in range(GROUPS):
        scalars = jnp.stack([limit, core * half_cols + g * group]).astype(jnp.int32)
        key_g = narrow(product(blocks[g], w_k))
        value_g = narrow(product(blocks[g], w_v))
        operands = (query_c, guests[g], key_g, value_g, grad_c, guest_grads[g], g * group, columns)
        own_part, crossed = col_stats(scalars, key_rows, query_rows, *operands)
        other_part = send(crossed, cross)
        final, mixed, guest_mixed, g_query, g_guest, g_key, g_value = col_grads(
            scalars, key_rows, query_rows, row_part, own_part, other_part, *operands
        )
        finals.append(final)
        mixed_c.append(
            narrow(mixed.astype(jnp.float32) + send(guest_mixed, guest_up).astype(jnp.float32))
        )
        g_query = narrow(g_query.astype(jnp.float32) + send(g_guest, guest_up).astype(jnp.float32))
        terms = product_t(g_key, w_k) + product_t(g_value, w_v)
        moving = None
        for k in range(chips - 2, -1, -1):
            at = (chips - 2 - k) * chip_rows
            term = terms[:, at : at + chip_rows]
            if moving is not None:
                term = term + moving.astype(jnp.float32)
            if k > 0:
                moving = send(narrow(term), down[k])
            else:
                own_terms.append(narrow(term + product_t(g_query, w_q)))
        tokens_g = tokens_c[g * group : (g + 1) * group]
        w_parts.append(
            (
                weight_product(tokens_g, g_query),
                weight_product(blocks[g], g_key),
                weight_product(blocks[g], g_value),
            )
        )

    final = jnp.concatenate(finals, axis=0).reshape(half_cols, 3, HEADS, 2 * chip_rows)
    final = to_rows(final[..., :chip_rows], 0, 3)
    final = final.transpose(3, 1, 2, 0).reshape(row_local, 3, HEADS * columns)
    mixed_r, g_query_r, g_key_r, g_value_r = row_grads(
        row_scalars, final, query_r, key_r, value_r, grad_r
    )
    mixed_b = jnp.swapaxes(to_rows(jnp.concatenate(mixed_c, axis=0), 0, 1), 0, 1)
    attention = narrow(mixed_r.astype(jnp.float32) + mixed_b.astype(jnp.float32))
    terms_b = jnp.swapaxes(to_rows(jnp.concatenate(own_terms, axis=0), 0, 1), 0, 1)
    input_sum = (
        product_t(g_query_r, w_q) + product_t(g_key_r, w_k) + product_t(g_value_r, w_v)
    ) + terms_b.astype(jnp.float32)
    input_grad = narrow(input_sum)

    shares = []
    for j, grads in enumerate((g_query_r, g_key_r, g_value_r)):
        part = weight_product(tokens_r, grads)
        for item in w_parts:
            part = part + item[j]
        part = narrow(part).reshape(chips, 2, -1, width)
        mine = lax.dynamic_index_in_dim(part, core, 1, keepdims=False)
        others = lax.dynamic_index_in_dim(part, 1 - core, 1, keepdims=False)
        shares.append(narrow(mine.astype(jnp.float32) + send(others, swap).astype(jnp.float32)))
    share = jnp.stack(shares)
    share = lax.psum_scatter(share, "dp", scatter_dimension=3, tiled=True)
    rings = [[2 * z + c for z in range(chips)] for c in (0, 1)]
    share = lax.psum_scatter(share, "seq", scatter_dimension=1, axis_index_groups=rings, tiled=True)
    w_grads = share[:, 0].astype(jnp.float32)
    return (attention[None], input_grad[None], w_grads)


def solution(mesh):
    in_specs = (P("dp", "seq", None, None), P("dp"), P(), P("dp", "seq", None, None))
    out_specs = (P("dp", "seq", None, None), P("dp", "seq", None, None), P(None, "seq", "dp"))
    return jax.shard_map(body, mesh=mesh, in_specs=in_specs, out_specs=out_specs, check_vma=False)
```

time: 1220 us -> 927 us (0.76)
  waiting for transfers between devices: 702 us -> 256 us
  local copies, waits for them, and re-layouts: 227 us -> 69.4 us
  Pallas kernels: 0 us -> 147 us
  matrix products: 200 us -> 282 us
  starting transfers between devices: 54.6 us -> 101 us
  other arithmetic: 16.1 us -> 46.9 us
    all_to_all x12 -> x0, waiting for transfers between devices: 654 us -> none  [the longest x1 174 us: body(): lax.all_to_all(col_mixed_c, 'seq', split_axis=1, concat_axis=2, tiled=True)]
    ppermute x0 -> x46, waiting for transfers between devices: none -> 195 us  [send(): return lax.ppermute(values, 'seq', perm)]
    pallas_call x0 -> x10, Pallas kernels: none -> 147 us  [call(): pl.pallas_call(kernel, grid=(steps,), in_specs=in_specs, out_specs=out_sp...]
    ppermute x0 -> x46, starting transfers between devices: none -> 100 us  [send(): return lax.ppermute(values, 'seq', perm)]
    dot_general x17 -> x42, matrix products: 200 us -> 282 us  [the longest x15 105 us: product_t(): jnp.einsum('...f,df->...d', values, weight, preferred_element_type=jnp.fl...]
    all_to_all x23 -> x0, local copies, waits for them, and re-layouts: 61.8 us -> none  [the longest x2 17 us: body(): lax.all_to_all(col_mixed_c, 'seq', split_axis=1, concat_axis=2, tiled=True)]
    reduce_scatter x1 -> x2, waiting for transfers between devices: 3.88 us -> 61.2 us  [the longest x1 61.2 us: body(): lax.psum_scatter(share, 'seq', scatter_dimension=1, axis_index_groups=rin...]
    all_to_all x12 -> x0, starting transfers between devices: 54.5 us -> none  [the longest x1 6.33 us: body(): lax.all_to_all(key_r, 'seq', split_axis=2, concat_axis=1, tiled=True)]
  transfers between devices with their start and end apart: 14 -> 48, of which waited for: 11 -> 9; matrix products, arithmetic and copies ran while one was open for 23% -> 40% of each run, Pallas kernels for 0% -> 14%
where the time goes in v1:
time: 927 us; the launch traced here: 919 us
  matrix products  282 us (30%)
  waiting for transfers between devices  256 us (28%)
  Pallas kernels  147 us (16%)
  starting transfers between devices  101 us (11%)
  local copies, waits for them, and re-layouts  69.4 us (7%)
  other arithmetic  46.9 us (5%)
  between operations  16.6 us (2%)
    ppermute x46, waiting for transfers between devices, send(): return lax.ppermute(values, 'seq', perm)  195 us
    pallas_call x10, Pallas kernels, call(): pl.pallas_call(kernel, grid=(steps,), in_specs=in_specs, out_specs=out_sp...  147 us
    dot_general x15, matrix products, product_t(): jnp.einsum('...f,df->...d', values, weight, preferred_element_type=jnp.fl...  105 us
    ppermute x46, starting transfers between devices, send(): return lax.ppermute(values, 'seq', perm)  100 us
    dot_general x15, matrix products, weight_product(): jnp.einsum('abd,abf->df', values, grads, preferred_element_type=jnp.float32)  95.7 us
    dot_general x12, matrix products, product(): jnp.einsum('...d,df->...f', values, weight, preferred_element_type=jnp.fl...  81.5 us
    reduce_scatter x1, waiting for transfers between devices, body(): lax.psum_scatter(share, 'seq', scatter_dimension=1, axis_index_groups=rin...  61.2 us
    convert_element_type x12, other arithmetic, narrow(): return values.astype(jnp.bfloat16)  20.4 us
  transfers between devices with their start and end apart: 48, of which 9 were waited for; matrix products, arithmetic and copies ran while one was open for 40% of the time, Pallas kernels for 14%

profile of v1, /device:TPU:0, one launch (start us, length us, event | category | flops | bytes accessed | tf_op | source)
XLA Modules:
  0.0 918.8 jit_solution(3697164828376204379)
XLA Ops:
  7.2 7.0 constant_dynamic-slice_fusion.1
  17.8 7.5 fusion.44.query
  25.4 9.0 fusion.47.key
  34.5 7.6 fusion.50.value
  42.1 14.2 %shard_map.67 = f32[16,3,1024]{2,1,0:T(4,128)S(1)} custom-call(s32[2]{0:T(128)S(1)} %pad_add_fusion.scalars, bf16[16,128,1024]{2,1,0:T(8,128)(2,1)S(1)} %fusion.44.query, bf16[16,128,1024]{2,1,0:T(8,128)(2,1)} %fusion.47.key, bf16[16,128,1024]{2,1,0:T(8,128)(2,1)} %fusion.50.value, bf16[16,128,1024]{2,1,0:T(8,128)(2,1)} %bitcast.256), custom_call_target="tpu_custom_call" | custom-call | flops 4294967296 | bytes 4294967 | tf_op jit(solution)/shard_map/pallas_call | solution.py:198
  82.8 12.0 %collective-permute-done.20 = bf16[16,32,1024]{2,1,0:T(8,128)(2,1)} collective-permute-done((bf16[16,32,1024]{2,1,0:T(8,128)(2,1)}, bf16[16,32,1024]{2,1,0:T(8,128)(2,1)}, u32[]{:S(2)}, u32[]{:S(2)}) %collective-permute-start.20) | collective-permute-done | bytes 1048608 | tf_op jit(solution)/shard_map/ppermute | solution.py:342
  95.7 7.4 convolution_convert_fusion.query
  116.9 6.5 collective-permute-start.10
  129.6 7.9 convolution_convert_fusion.1.value
  137.6 7.4 collective-permute-done.10
  151.2 46.5 %collective-permute-start.4 = (bf16[16,32,1024]{2,1,0:T(8,128)(2,1)S(1)}, bf16[16,32,1024]{2,1,0:T(8,128)(2,1)}, u32[]{:S(2)}, u32[]{:S(2)}) collective-permute-start(bf16[16,32,1024]{2,1,0:T(8,128)(2,1)S(1)} %copy-done.54), channel_id=1, source_target_pairs={{0,2},{1,3},{2,4},{3,5},{8,10},{9,11},{10,12},{11,13},{16,18},{17,... | collective-permute-start | bytes 3145736 | tf_op jit(solution)/shard_map/ppermute | solution.py:342
  209.8 9.0 collective-permute-done.4
  220.6 8.3 shard_map.74
  230.4 8.3 shard_map.72
  238.7 7.7 convolution_convert_fusion.5.value
  247.8 8.3 shard_map.70
  262.9 8.4 convolution_convert_fusion.7.value
  271.4 8.6 shard_map.68
  281.0 18.2 %shard_map.75 = (f32[16,3,512]{2,1,0:T(4,128)S(1)}, bf16[16,32,1024]{2,1,0:T(8,128)(2,1)S(1)}, bf16[16,32,1024]{2,1,0:T(8,128)(2,1)S(1)}, bf16[16,32,1024]{2,1,0...) custom-call(s32[2]{0:T(128)S(1)} %pad_add_fusion.6.scalars, ...), custom_call_target="tpu_custom_call" | custom-call | flops 4831838208 | bytes 4831838 | tf_op jit(solution)/shard_map/pallas_call | solution.py:198
  300.1 18.9 %shard_map.73 = (f32[16,3,512]{2,1,0:T(4,128)S(1)}, bf16[16,32,1024]{2,1,0:T(8,128)(2,1)S(1)}, bf16[16,32,1024]{2,1,0:T(8,128)(2,1)S(1)}, bf16[16,32,1024]{2,1,0...) custom-call(s32[2]{0:T(128)S(1)} %pad_add_fusion.5.scalars, ...), custom_call_target="tpu_custom_call" | custom-call | flops 4831838208 | bytes 4831838 | tf_op jit(solution)/shard_map/pallas_call | solution.py:198
  321.9 18.1 %shard_map.71 = (f32[16,3,512]{2,1,0:T(4,128)S(1)}, bf16[16,32,1024]{2,1,0:T(8,128)(2,1)S(1)}, bf16[16,32,1024]{2,1,0:T(8,128)(2,1)S(1)}, bf16[16,32,1024]{2,1,0...) custom-call(s32[2]{0:T(128)S(1)} %pad_add_fusion.4.scalars, ...), custom_call_target="tpu_custom_call" | custom-call | flops 4831838208 | bytes 4831838 | tf_op jit(solution)/shard_map/pallas_call | solution.py:198
  343.0 18.5 %shard_map.69 = (f32[16,3,512]{2,1,0:T(4,128)S(1)}, bf16[16,32,1024]{2,1,0:T(8,128)(2,1)S(1)}, bf16[16,32,1024]{2,1,0:T(8,128)(2,1)S(1)}, bf16[16,32,1024]{2,1,0...) custom-call(s32[2]{0:T(128)S(1)} %pad_add_fusion.1.scalars, ...), custom_call_target="tpu_custom_call" | custom-call | flops 4831838208 | bytes 4831838 | tf_op jit(solution)/shard_map/pallas_call | solution.py:198
  386.3 9.3 %fusion.28 = f32[16,96,1024]{2,0,1:T(8,128)} fusion(bf16[16,96,1024]{2,1,0:T(8,128)(2,1)S(1)} %copy-done.75, bf16[3,1024,1024]{2,1,0:T(8,128)(2,1)} %param.6), kind=kOutput, calls=%fused_computation.60 | convolution fusion | flops 3221225472 | bytes 11534336 | tf_op jit(solution)/shard_map/...f,df->...d/dot_general | solution.py:310
  395.6 6.3 fusion.32
  402.0 6.3 fusion.36
  408.3 6.4 fusion.40
  414.7 8.7 fusion.62
  423.3 8.8 fusion.59
  432.1 8.6 fusion.56
  440.8 8.7 fusion.53
  459.6 6.6 fusion.172
  476.4 6.7 fusion.173
  499.6 25.6 %shard_map.76 = (bf16[16,128,1024]{2,1,0:T(8,128)(2,1)S(1)}, bf16[16,128,1024]{2,1,0:T(8,128)(2,1)}, bf16[16,128,1024]{2,1,0:T(8,128)(2,1)}, bf16[16,128,1024]{2,1,0:T(8,128)(2,1)}) custom-call(s32[2]{0:T(128)S(1)} %copy-done.32, f32[16,3,1024]{2,1,0:T(4,128)S(1)} %reshape.84.stats, bf16[16,128,1024]{2,1,0:T(8,128)(2,1)} %copy-done, ...), custom_call_target="tpu_custom_call" | custom-call | flops 12884901888 | bytes 12884901 | tf_op jit(solution)/shard_map/pallas_call | solution.py:198
  525.3 9.8 %fusion.16 = f32[1024,1024,1]{0,1,2:T(8,128)} fusion(bf16[16,128,1024]{2,1,0:T(8,128)(2,1)} %get-tuple-element.66, bf16[1,16,128,1024]{3,2,1,0:T(8,128)(2,1)S(1)} %copy-done.45), kind=kOutput, calls=%fused_computation.43 | convolution fusion | flops 4294967296 | bytes 12582912 | tf_op jit(solution)/shard_map/abd,abf->df/dot_general | solution.py:314
  535.1 6.5 fusion.18
  541.7 10.7 %fusion.7 = bf16[1024,1024]{1,0:T(8,128)(2,1)S(1)} fusion(f32[1024,1024,1]{0,1,2:T(8,128)} %fusion.16, f32[1024,1024,1]{1,0,2:T(8,128)} %fusion.168, f32[1024,1024,1]{1,0,2:T(8,128)} %fusion.170, f32[1024,1024,1]{1,0,2:T(8,128)} %fusion.172, bf16[16,96,1024]{2,1,0:T(8,128)(2,1)S(1)} %copy-done.76, bf16[16,32,1024]{2,1,0:T(8,128)(2,1)} %get-tuple-element.96, ...), kind=kOutput, calls=%fused_computation.32 | convolution fusion | flops 3235905536 | bytes 25165824 | tf_op jit(solution)/shard_map/abd,abf->df/dot_general | solution.py:314
  552.4 10.5 %fusion.11 = bf16[1024,1024]{1,0:T(8,128)(2,1)S(1)} fusion(f32[1024,1024,1]{0,1,2:T(8,128)} %fusion.18, f32[1024,1024,1]{1,0,2:T(8,128)} %fusion.169, f32[1024,1024,1]{1,0,2:T(8,128)} %fusion.171, f32[1024,1024,1]{1,0,2:T(8,128)} %fusion.173, bf16[16,96,1024]{2,1,0:T(8,128)(2,1)S(1)} %copy-done.74, bf16[16,32,1024]{2,1,0:T(8,128)(2,1)} %get-tuple-element.96, ...), kind=kOutput, calls=%fused_computation.37 | convolution fusion | flops 3235905536 | bytes 25165824 | tf_op jit(solution)/shard_map/abd,abf->df/dot_general | solution.py:314
  563.1 6.5 fusion.20
  587.9 6.1 fusion.15
  629.7 109.2 %collective-permute-done.40 = bf16[16,32,1024]{2,0,1:T(8,128)(2,1)} collective-permute-done((bf16[16,32,1024]{2,0,1:T(8,128)(2,1)}, bf16[16,32,1024]{2,0,1:T(8,128)(2,1)}, u32[]{:S(2)}, u32[]{:S(2)}) %collective-permute-start.40) | collective-permute-done | bytes 1048608 | tf_op jit(solution)/shard_map/ppermute | solution.py:342
  743.1 18.2 %collective-permute-done.37 = bf16[16,32,1024]{2,0,1:T(8,128)(2,1)S(1)} collective-permute-done((bf16[16,32,1024]{2,0,1:T(8,128)(2,1)S(1)}, bf16[16,32,1024]{2,0,1:T(8,128)(2,1)S(1)}, u32[]{:S(2)}, u32[]{:S(2)}) %collective-permute-start.37) | collective-permute-done | bytes 1048608 | tf_op jit(solution)/shard_map/ppermute | solution.py:342
  764.5 19.3 %collective-permute-done.34 = bf16[16,32,1024]{2,0,1:T(8,128)(2,1)S(1)} collective-permute-done((bf16[16,32,1024]{2,0,1:T(8,128)(2,1)S(1)}, bf16[16,32,1024]{2,0,1:T(8,128)(2,1)S(1)}, u32[]{:S(2)}, u32[]{:S(2)}) %collective-permute-start.34) | collective-permute-done | bytes 1048608 | tf_op jit(solution)/shard_map/ppermute | solution.py:342
  787.0 19.1 %collective-permute-done.31 = bf16[16,32,1024]{2,0,1:T(8,128)(2,1)S(1)} collective-permute-done((bf16[16,32,1024]{2,0,1:T(8,128)(2,1)S(1)}, bf16[16,32,1024]{2,0,1:T(8,128)(2,1)S(1)}, u32[]{:S(2)}, u32[]{:S(2)}) %collective-permute-start.31) | collective-permute-done | bytes 1048608 | tf_op jit(solution)/shard_map/ppermute | solution.py:342
  813.7 6.9 fusion.109
  820.6 7.1 fusion.94
  827.7 6.7 fusion.2
  834.4 14.4 %fusion.3 = bf16[1,16,128,1024]{3,2,1,0:T(8,128)(2,1)} fusion(f32[16,128,1024]{2,1,0:T(8,128)} %fusion.109, f32[16,128,1024]{2,1,0:T(8,128)} %fusion.94, bf16[64,16,1024]{2,0,1:T(8,128)(2,1)} %collective-permute-done.42, bf16[64,16,1024]{2,0,1:T(8,128)(2,1)} %get-tuple-element.85, pred[]{:T(512)S(6)} %eq.12, bf16[16,128,1024]{2,1,0:T(8,128)(2,1)} %get-tuple-element.66, ...), kind=kOutput, calls=%fused_computation.23 | convolution fusion | flops 4324327424 | bytes 31457280 | tf_op jit(solution)/shard_map/...f,df->...d/dot_general | solution.py:310
  848.8 61.2 %reduce-scatter.5.cloned.1.call-done = bf16[3,1,128,256]{3,2,0,1:T(8,128)(2,1)} async-done(((bf16[3,4,128,256]{3,2,0,1:T(8,128)(2,1)}), bf16[3,1,128,256]{3,2,0,1:T(8,128)(2,1)}) %reduce-scatter.5.cloned.1.call-update) | async-done | bytes 196624 | tf_op jit(solution)/shard_map/reduce_scatter | solution.py:461
  (363 shorter events, 222.7 us)
Async XLA Ops:
  7.2 827.2 %reduce-scatter.3.cloned.1.call-start = ((), (), s32[]{:S(2)}) async-start(), calls=%async_computation.2 | async-start | bytes 3932160 | tf_op jit(solution)/shard_map/reduce_scatter | solution.py:459
  16.7 45.8 %collective-permute-start.2 = (bf16[64,16,1024]{2,1,0:T(8,128)(2,1)}, bf16[64,16,1024]{2,1,0:T(8,128)(2,1)}, u32[]{:S(2)}, u32[]{:S(2)}) collective-permute-start(bf16[64,16,1024]{2,1,0:T(8,128)(2,1)} %bitcast.250), channel_id=1, source_target_pairs={{0,1},{1,0},{2,3},{3,2},{4,5},{5,4},{6,7},{7,6},{8,9},{9,8},{10,11... | collective-permute-start | bytes 6291464 | tf_op jit(solution)/shard_map/ppermute | solution.py:342
  56.6 19.2 %collective-permute-start = (f32[64,3,8,16]{0,2,3,1:T(8,128)S(1)}, f32[64,3,8,16]{0,2,3,1:T(8,128)S(1)}, u32[]{:S(2)}, u32[]{:S(2)}) collective-permute-start(f32[64,3,8,16]{0,2,3,1:T(8,128)S(1)} %bitcast.272), channel_id=1, source_target_pairs={{0,1},{1,0},{2,3},{3,2},{4,5},{5,4},{6,7},{7,6},{8,9},{9,8},{10,11... | collective-permute-start | bytes 294920 | tf_op jit(solution)/shard_map/ppermute | solution.py:342
  60.9 46.1 %collective-permute-start.6 = (bf16[64,16,1024]{2,1,0:T(8,128)(2,1)}, bf16[64,16,1024]{2,1,0:T(8,128)(2,1)}, u32[]{:S(2)}, u32[]{:S(2)}) collective-permute-start(bf16[64,16,1024]{2,1,0:T(8,128)(2,1)} %bitcast.248), channel_id=1, source_target_pairs={{0,1},{1,0},{2,3},{3,2},{4,5},{5,4},{6,7},{7,6},{8,9},{9,8},{10,11... | collective-permute-start | bytes 6291464 | tf_op jit(solution)/shard_map/ppermute | solution.py:342
  66.5 28.3 %collective-permute-start.20 = (bf16[16,32,1024]{2,1,0:T(8,128)(2,1)}, bf16[16,32,1024]{2,1,0:T(8,128)(2,1)}, u32[]{:S(2)}, u32[]{:S(2)}) collective-permute-start(bf16[16,32,1024]{2,1,0:T(8,128)(2,1)} %get-tuple-element.96), channel_id=1, source_target_pairs={{0,2},{1,3},{2,4},{3,5},{8,10},{9,11},{10,12},{11,13},{16,18},{17,... | collective-permute-start | bytes 3145736 | tf_op jit(solution)/shard_map/ppermute | solution.py:342
  75.8 0.8 collective-permute-start.1
  80.3 36.6 %collective-permute-start.15 = (bf16[16,32,1024]{2,1,0:T(8,128)(2,1)}, bf16[16,32,1024]{2,1,0:T(8,128)(2,1)S(1)}, u32[]{:S(2)}, u32[]{:S(2)}) collective-permute-start(bf16[16,32,1024]{2,1,0:T(8,128)(2,1)} %get-tuple-element.95), channel_id=1, source_target_pairs={{0,2},{1,3},{2,4},{3,5},{8,10},{9,11},{10,12},{11,13},{16,18},{17,... | collective-permute-start | bytes 3145736 | tf_op jit(solution)/shard_map/ppermute | solution.py:342
  94.8 28.6 %collective-permute-start.21 = (bf16[16,32,1024]{2,1,0:T(8,128)(2,1)}, bf16[16,32,1024]{2,1,0:T(8,128)(2,1)S(1)}, u32[]{:S(2)}, u32[]{:S(2)}) collective-permute-start(bf16[16,32,1024]{2,1,0:T(8,128)(2,1)} %collective-permute-done.20), channel_id=1, source_target_pairs={{2,4},{3,5},{10,12},{11,13},{18,20},{19,21},{26,28},{27,29}} | collective-permute-start | bytes 3145736 | tf_op jit(solution)/shard_map/ppermute | solution.py:342
  106.3 45.0 %collective-permute-start.19 = (bf16[16,32,1024]{2,1,0:T(8,128)(2,1)S(1)}, bf16[16,32,1024]{2,1,0:T(8,128)(2,1)S(1)}, u32[]{:S(2)}, u32[]{:S(2)}) collective-permute-start(bf16[16,32,1024]{2,1,0:T(8,128)(2,1)S(1)} %get-tuple-element.98), channel_id=1, source_target_pairs={{6,4},{7,5},{14,12},{15,13},{22,20},{23,21},{30,28},{31,29}} | collective-permute-start | bytes 3145736 | tf_op jit(solution)/shard_map/ppermute | solution.py:342
  110.2 93.3 %collective-permute-start.22 = (bf16[16,32,1024]{2,1,0:T(8,128)(2,1)S(1)}, bf16[16,32,1024]{2,1,0:T(8,128)(2,1)S(1)}, u32[]{:S(2)}, u32[]{:S(2)}) collective-permute-start(bf16[16,32,1024]{2,1,0:T(8,128)(2,1)S(1)} %get-tuple-element.92), channel_id=1, source_target_pairs={{6,4},{7,5},{14,12},{15,13},{22,20},{23,21},{30,28},{31,29}} | collective-permute-start | bytes 3145736 | tf_op jit(solution)/shard_map/ppermute | solution.py:342
  110.9 118.0 %collective-permute-start.14 = (bf16[16,32,1024]{2,1,0:T(8,128)(2,1)}, bf16[16,32,1024]{2,1,0:T(8,128)(2,1)S(1)}, u32[]{:S(2)}, u32[]{:S(2)}) collective-permute-start(bf16[16,32,1024]{2,1,0:T(8,128)(2,1)} %get-tuple-element.99), channel_id=1, source_target_pairs={{6,4},{7,5},{14,12},{15,13},{22,20},{23,21},{30,28},{31,29}} | collective-permute-start | bytes 3145736 | tf_op jit(solution)/shard_map/ppermute | solution.py:342
  116.9 28.1 %collective-permute-start.10 = (bf16[16,32,1024]{2,1,0:T(8,128)(2,1)S(1)}, bf16[16,32,1024]{2,1,0:T(8,128)(2,1)S(1)}, u32[]{:S(2)}, u32[]{:S(2)}) collective-permute-start(bf16[16,32,1024]{2,1,0:T(8,128)(2,1)S(1)} %copy-done.57), channel_id=1, source_target_pairs={{0,2},{1,3},{2,4},{3,5},{8,10},{9,11},{10,12},{11,13},{16,18},{17,... | collective-permute-start | bytes 3145736 | tf_op jit(solution)/shard_map/ppermute | solution.py:342
  123.5 22.4 %collective-permute-start.16 = (bf16[16,32,1024]{2,1,0:T(8,128)(2,1)S(1)}, bf16[16,32,1024]{2,1,0:T(8,128)(2,1)S(1)}, u32[]{:S(2)}, u32[]{:S(2)}) collective-permute-start(bf16[16,32,1024]{2,1,0:T(8,128)(2,1)S(1)} %collective-permute-done.15), channel_id=1, source_target_pairs={{2,4},{3,5},{10,12},{11,13},{18,20},{19,21},{26,28},{27,29}} | collective-permute-start | bytes 3145736 | tf_op jit(solution)/shard_map/ppermute | solution.py:342
  145.0 84.7 %collective-permute-start.17 = (bf16[16,32,1024]{2,1,0:T(8,128)(2,1)}, bf16[16,32,1024]{2,1,0:T(8,128)(2,1)S(1)}, u32[]{:S(2)}, u32[]{:S(2)}) collective-permute-start(bf16[16,32,1024]{2,1,0:T(8,128)(2,1)} %get-tuple-element.91), channel_id=1, source_target_pairs={{6,4},{7,5},{14,12},{15,13},{22,20},{23,21},{30,28},{31,29}} | collective-permute-start | bytes 3145736 | tf_op jit(solution)/shard_map/ppermute | solution.py:342
  145.8 58.4 %collective-permute-start.11 = (bf16[16,32,1024]{2,1,0:T(8,128)(2,1)S(1)}, bf16[16,32,1024]{2,1,0:T(8,128)(2,1)S(1)}, u32[]{:S(2)}, u32[]{:S(2)}) collective-permute-start(bf16[16,32,1024]{2,1,0:T(8,128)(2,1)S(1)} %collective-permute-done.10), channel_id=1, source_target_pairs={{2,4},{3,5},{10,12},{11,13},{18,20},{19,21},{26,28},{27,29}} | collective-permute-start | bytes 3145736 | tf_op jit(solution)/shard_map/ppermute | solution.py:342
  151.2 67.5 %collective-permute-start.4 = (bf16[16,32,1024]{2,1,0:T(8,128)(2,1)S(1)}, bf16[16,32,1024]{2,1,0:T(8,128)(2,1)}, u32[]{:S(2)}, u32[]{:S(2)}) collective-permute-start(bf16[16,32,1024]{2,1,0:T(8,128)(2,1)S(1)} %copy-done.54), channel_id=1, source_target_pairs={{0,2},{1,3},{2,4},{3,5},{8,10},{9,11},{10,12},{11,13},{16,18},{17,... | collective-permute-start | bytes 3145736 | tf_op jit(solution)/shard_map/ppermute | solution.py:342
  203.5 42.9 %collective-permute-start.9 = (bf16[16,32,1024]{2,1,0:T(8,128)(2,1)}, bf16[16,32,1024]{2,1,0:T(8,128)(2,1)S(1)}, u32[]{:S(2)}, u32[]{:S(2)}) collective-permute-start(bf16[16,32,1024]{2,1,0:T(8,128)(2,1)} %get-tuple-element.100), channel_id=1, source_target_pairs={{6,4},{7,5},{14,12},{15,13},{22,20},{23,21},{30,28},{31,29}} | collective-permute-start | bytes 3145736 | tf_op jit(solution)/shard_map/ppermute | solution.py:342
  204.3 42.8 %collective-permute-start.12 = (bf16[16,32,1024]{2,1,0:T(8,128)(2,1)}, bf16[16,32,1024]{2,1,0:T(8,128)(2,1)S(1)}, u32[]{:S(2)}, u32[]{:S(2)}) collective-permute-start(bf16[16,32,1024]{2,1,0:T(8,128)(2,1)} %get-tuple-element.90), channel_id=1, source_target_pairs={{6,4},{7,5},{14,12},{15,13},{22,20},{23,21},{30,28},{31,29}} | collective-permute-start | bytes 3145736 | tf_op jit(solution)/shard_map/ppermute | solution.py:342
  218.8 37.3 %collective-permute-start.5 = (bf16[16,32,1024]{2,1,0:T(8,128)(2,1)}, bf16[16,32,1024]{2,1,0:T(8,128)(2,1)}, u32[]{:S(2)}, u32[]{:S(2)}) collective-permute-start(bf16[16,32,1024]{2,1,0:T(8,128)(2,1)} %collective-permute-done.4), channel_id=1, source_target_pairs={{2,4},{3,5},{10,12},{11,13},{18,20},{19,21},{26,28},{27,29}} | collective-permute-start | bytes 3145736 | tf_op jit(solution)/shard_map/ppermute | solution.py:342
  228.9 42.5 %collective-permute-start.3 = (bf16[16,32,1024]{2,1,0:T(8,128)(2,1)}, bf16[16,32,1024]{2,1,0:T(8,128)(2,1)S(1)}, u32[]{:S(2)}, u32[]{:S(2)}) collective-permute-start(bf16[16,32,1024]{2,1,0:T(8,128)(2,1)} %get-tuple-element.97), channel_id=1, source_target_pairs={{6,4},{7,5},{14,12},{15,13},{22,20},{23,21},{30,28},{31,29}} | collective-permute-start | bytes 3145736 | tf_op jit(solution)/shard_map/ppermute | solution.py:342
  229.7 41.7 %collective-permute-start.7 = (bf16[16,32,1024]{2,1,0:T(8,128)(2,1)}, bf16[16,32,1024]{2,1,0:T(8,128)(2,1)S(1)}, u32[]{:S(2)}, u32[]{:S(2)}) collective-permute-start(bf16[16,32,1024]{2,1,0:T(8,128)(2,1)} %get-tuple-element.89), channel_id=1, source_target_pairs={{6,4},{7,5},{14,12},{15,13},{22,20},{23,21},{30,28},{31,29}} | collective-permute-start | bytes 3145736 | tf_op jit(solution)/shard_map/ppermute | solution.py:342
  246.4 34.5 %collective-permute-start.23 = (f32[16,3,512]{2,1,0:T(4,128)S(1)}, f32[16,3,512]{2,1,0:T(4,128)S(1)}, u32[]{:S(2)}, u32[]{:S(2)}) collective-permute-start(f32[16,3,512]{2,1,0:T(4,128)S(1)} %get-tuple-element.53), channel_id=1, source_target_pairs={{4,6},{5,7},{6,4},{7,5},{12,14},{13,15},{14,12},{15,13},{20,22},{2... | collective-permute-start | bytes 294920 | tf_op jit(solution)/shard_map/ppermute | solution.py:342
  247.1 53.0 %collective-permute-start.18 = (f32[16,3,512]{2,1,0:T(4,128)S(1)}, f32[16,3,512]{2,1,0:T(4,128)S(1)}, u32[]{:S(2)}, u32[]{:S(2)}) collective-permute-start(f32[16,3,512]{2,1,0:T(4,128)S(1)} %get-tuple-element.50), channel_id=1, source_target_pairs={{4,6},{5,7},{6,4},{7,5},{12,14},{13,15},{14,12},{15,13},{20,22},{2... | collective-permute-start | bytes 294920 | tf_op jit(solution)/shard_map/ppermute | solution.py:342
  256.1 65.8 %collective-permute-start.13 = (f32[16,3,512]{2,1,0:T(4,128)S(1)}, f32[16,3,512]{2,1,0:T(4,128)S(1)}, u32[]{:S(2)}, u32[]{:S(2)}) collective-permute-start(f32[16,3,512]{2,1,0:T(4,128)S(1)} %get-tuple-element.47), channel_id=1, source_target_pairs={{4,6},{5,7},{6,4},{7,5},{12,14},{13,15},{14,12},{15,13},{20,22},{2... | collective-permute-start | bytes 294920 | tf_op jit(solution)/shard_map/ppermute | solution.py:342
  280.1 63.0 %collective-permute-start.8 = (f32[16,3,512]{2,1,0:T(4,128)S(1)}, f32[16,3,512]{2,1,0:T(4,128)S(1)}, u32[]{:S(2)}, u32[]{:S(2)}) collective-permute-start(f32[16,3,512]{2,1,0:T(4,128)S(1)} %get-tuple-element.44), channel_id=1, source_target_pairs={{4,6},{5,7},{6,4},{7,5},{12,14},{13,15},{14,12},{15,13},{20,22},{2... | collective-permute-start | bytes 294920 | tf_op jit(solution)/shard_map/ppermute | solution.py:342
  371.4 123.6 %collective-permute-start.24 = (f32[64,3,8,16]{0,3,2,1:T(8,128)}, f32[64,3,8,16]{0,3,2,1:T(8,128)}, u32[]{:S(2)}, u32[]{:S(2)}) collective-permute-start(f32[64,3,8,16]{0,3,2,1:T(8,128)} %copy.91), channel_id=1, source_target_pairs={{0,1},{1,0},{2,3},{3,2},{4,5},{5,4},{6,7},{7,6},{8,9},{9,8},{10,11... | collective-permute-start | bytes 294920 | tf_op jit(solution)/shard_map/ppermute | solution.py:342
  373.1 221.1 %collective-permute-start.28 = (bf16[16,32,1024]{2,0,1:T(8,128)(2,1)}, bf16[16,32,1024]{2,0,1:T(8,128)(2,1)}, u32[]{:S(2)}, u32[]{:S(2)}) collective-permute-start(bf16[16,32,1024]{2,0,1:T(8,128)(2,1)} %copy.103), channel_id=1, source_target_pairs={{4,6},{5,7},{12,14},{13,15},{20,22},{21,23},{28,30},{29,31}} | collective-permute-start | bytes 3145736 | tf_op jit(solution)/shard_map/ppermute | solution.py:342
  377.8 220.2 %collective-permute-start.27 = (bf16[16,32,1024]{2,0,1:T(8,128)(2,1)}, bf16[16,32,1024]{2,0,1:T(8,128)(2,1)}, u32[]{:S(2)}, u32[]{:S(2)}) collective-permute-start(bf16[16,32,1024]{2,0,1:T(8,128)(2,1)} %copy.101), channel_id=1, source_target_pairs={{4,6},{5,7},{12,14},{13,15},{20,22},{21,23},{28,30},{29,31}} | collective-permute-start | bytes 3145736 | tf_op jit(solution)/shard_map/ppermute | solution.py:342
  381.0 219.3 %collective-permute-start.26 = (bf16[16,32,1024]{2,0,1:T(8,128)(2,1)}, bf16[16,32,1024]{2,0,1:T(8,128)(2,1)}, u32[]{:S(2)}, u32[]{:S(2)}) collective-permute-start(bf16[16,32,1024]{2,0,1:T(8,128)(2,1)} %copy.99), channel_id=1, source_target_pairs={{4,6},{5,7},{12,14},{13,15},{20,22},{21,23},{28,30},{29,31}} | collective-permute-start | bytes 3145736 | tf_op jit(solution)/shard_map/ppermute | solution.py:342
  384.3 218.2 %collective-permute-start.25 = (bf16[16,32,1024]{2,0,1:T(8,128)(2,1)}, bf16[16,32,1024]{2,0,1:T(8,128)(2,1)}, u32[]{:S(2)}, u32[]{:S(2)}) collective-permute-start(bf16[16,32,1024]{2,0,1:T(8,128)(2,1)} %copy.97), channel_id=1, source_target_pairs={{4,6},{5,7},{12,14},{13,15},{20,22},{21,23},{28,30},{29,31}} | collective-permute-start | bytes 3145736 | tf_op jit(solution)/shard_map/ppermute | solution.py:342
  495.1 74.6 %collective-permute-start.38 = (bf16[16,32,1024]{2,1,0:T(8,128)(2,1)S(1)}, bf16[16,32,1024]{2,1,0:T(8,128)(2,1)}, u32[]{:S(2)}, u32[]{:S(2)}) collective-permute-start(bf16[16,32,1024]{2,1,0:T(8,128)(2,1)S(1)} %copy-done.36), channel_id=1, source_target_pairs={{4,6},{5,7},{12,14},{13,15},{20,22},{21,23},{28,30},{29,31}} | collective-permute-start | bytes 3145736 | tf_op jit(solution)/shard_map/ppermute | solution.py:342
  569.6 4.9 collective-permute-start.35
  574.6 6.1 collective-permute-start.32
  580.7 6.0 collective-permute-start.41
  586.7 20.5 %collective-permute-start.39 = (bf16[16,32,1024]{2,0,1:T(8,128)(2,1)S(1)}, bf16[16,32,1024]{2,0,1:T(8,128)(2,1)S(1)}, u32[]{:S(2)}, u32[]{:S(2)}) collective-permute-start(bf16[16,32,1024]{2,0,1:T(8,128)(2,1)S(1)} %copy-done.53), channel_id=1, source_target_pairs={{4,2},{5,3},{12,10},{13,11},{20,18},{21,19},{28,26},{29,27}} | collective-permute-start | bytes 3145736 | tf_op jit(solution)/shard_map/ppermute | solution.py:342
  594.2 24.5 %collective-permute-start.36 = (bf16[16,32,1024]{2,0,1:T(8,128)(2,1)}, bf16[16,32,1024]{2,0,1:T(8,128)(2,1)}, u32[]{:S(2)}, u32[]{:S(2)}) collective-permute-start(bf16[16,32,1024]{2,0,1:T(8,128)(2,1)} %slice.374), channel_id=1, source_target_pairs={{4,2},{5,3},{12,10},{13,11},{20,18},{21,19},{28,26},{29,27}} | collective-permute-start | bytes 3145736 | tf_op jit(solution)/shard_map/ppermute | solution.py:342
  598.0 13.9 %collective-permute-start.45 = (bf16[4,128,1024]{2,1,0:T(8,128)(2,1)S(1)}, bf16[4,128,1024]{2,1,0:T(8,128)(2,1)S(1)}, u32[]{:S(2)}, u32[]{:S(2)}) collective-permute-start(bf16[4,128,1024]{2,1,0:T(8,128)(2,1)S(1)} %dynamic-slice_bitcast_fusion), channel_id=1, source_target_pairs={{0,1},{1,0},{2,3},{3,2},{4,5},{5,4},{6,7},{7,6},{8,9},{9,8},{10,11... | collective-permute-start | bytes 3145736 | tf_op jit(solution)/shard_map/ppermute | solution.py:342
  600.3 13.6 %collective-permute-start.44 = (bf16[4,128,1024]{2,1,0:T(8,128)(2,1)S(1)}, bf16[4,128,1024]{2,1,0:T(8,128)(2,1)S(1)}, u32[]{:S(2)}, u32[]{:S(2)}) collective-permute-start(bf16[4,128,1024]{2,1,0:T(8,128)(2,1)S(1)} %dynamic-slice_bitcast_fusion.1), channel_id=1, source_target_pairs={{0,1},{1,0},{2,3},{3,2},{4,5},{5,4},{6,7},{7,6},{8,9},{9,8},{10,11... | collective-permute-start | bytes 3145736 | tf_op jit(solution)/shard_map/ppermute | solution.py:342
  602.5 12.1 %collective-permute-start.43 = (bf16[4,128,1024]{2,1,0:T(8,128)(2,1)S(1)}, bf16[4,128,1024]{2,1,0:T(8,128)(2,1)S(1)}, u32[]{:S(2)}, u32[]{:S(2)}) collective-permute-start(bf16[4,128,1024]{2,1,0:T(8,128)(2,1)S(1)} %dynamic-slice_bitcast_fusion.2), channel_id=1, source_target_pairs={{0,1},{1,0},{2,3},{3,2},{4,5},{5,4},{6,7},{7,6},{8,9},{9,8},{10,11... | collective-permute-start | bytes 3145736 | tf_op jit(solution)/shard_map/ppermute | solution.py:342
  607.2 15.1 %collective-permute-start.33 = (bf16[16,32,1024]{2,0,1:T(8,128)(2,1)}, bf16[16,32,1024]{2,0,1:T(8,128)(2,1)}, u32[]{:S(2)}, u32[]{:S(2)}) collective-permute-start(bf16[16,32,1024]{2,0,1:T(8,128)(2,1)} %slice.375), channel_id=1, source_target_pairs={{4,2},{5,3},{12,10},{13,11},{20,18},{21,19},{28,26},{29,27}} | collective-permute-start | bytes 3145736 | tf_op jit(solution)/shard_map/ppermute | solution.py:342
  611.9 14.0 %collective-permute-start.30 = (bf16[16,32,1024]{2,0,1:T(8,128)(2,1)}, bf16[16,32,1024]{2,0,1:T(8,128)(2,1)}, u32[]{:S(2)}, u32[]{:S(2)}) collective-permute-start(bf16[16,32,1024]{2,0,1:T(8,128)(2,1)} %slice.376), channel_id=1, source_target_pairs={{4,2},{5,3},{12,10},{13,11},{20,18},{21,19},{28,26},{29,27}} | collective-permute-start | bytes 3145736 | tf_op jit(solution)/shard_map/ppermute | solution.py:342
  613.9 213.8 %collective-permute-start.29 = (bf16[64,16,1024]{2,0,1:T(8,128)(2,1)}, bf16[64,16,1024]{2,0,1:T(8,128)(2,1)}, u32[]{:S(2)}, u32[]{:S(2)}) collective-permute-start(bf16[64,16,1024]{2,0,1:T(8,128)(2,1)} %get-tuple-element.88), channel_id=1, source_target_pairs={{0,1},{1,0},{2,3},{3,2},{4,5},{5,4},{6,7},{7,6},{8,9},{9,8},{10,11... | collective-permute-start | bytes 6291464 | tf_op jit(solution)/shard_map/ppermute | solution.py:342
  614.6 124.4 %collective-permute-start.40 = (bf16[16,32,1024]{2,0,1:T(8,128)(2,1)}, bf16[16,32,1024]{2,0,1:T(8,128)(2,1)}, u32[]{:S(2)}, u32[]{:S(2)}) collective-permute-start(bf16[16,32,1024]{2,0,1:T(8,128)(2,1)} %fusion.65), channel_id=1, source_target_pairs={{2,0},{3,1},{4,2},{5,3},{10,8},{11,9},{12,10},{13,11},{18,16},{19,... | collective-permute-start | bytes 3145736 | tf_op jit(solution)/shard_map/ppermute | solution.py:342
  618.4 291.6 %reduce-scatter.5.cloned.1.call-start = ((), (), s32[]{:S(2)}) async-start(), calls=%async_computation.3 | async-start | bytes 983040 | tf_op jit(solution)/shard_map/reduce_scatter | solution.py:461
  620.9 140.4 %collective-permute-start.37 = (bf16[16,32,1024]{2,0,1:T(8,128)(2,1)S(1)}, bf16[16,32,1024]{2,0,1:T(8,128)(2,1)S(1)}, u32[]{:S(2)}, u32[]{:S(2)}) collective-permute-start(bf16[16,32,1024]{2,0,1:T(8,128)(2,1)S(1)} %fusion.68), channel_id=1, source_target_pairs={{2,0},{3,1},{4,2},{5,3},{10,8},{11,9},{12,10},{13,11},{18,16},{19,... | collective-permute-start | bytes 3145736 | tf_op jit(solution)/shard_map/ppermute | solution.py:342
  624.6 159.2 %collective-permute-start.34 = (bf16[16,32,1024]{2,0,1:T(8,128)(2,1)S(1)}, bf16[16,32,1024]{2,0,1:T(8,128)(2,1)S(1)}, u32[]{:S(2)}, u32[]{:S(2)}) collective-permute-start(bf16[16,32,1024]{2,0,1:T(8,128)(2,1)S(1)} %fusion.71), channel_id=1, source_target_pairs={{2,0},{3,1},{4,2},{5,3},{10,8},{11,9},{12,10},{13,11},{18,16},{19,... | collective-permute-start | bytes 3145736 | tf_op jit(solution)/shard_map/ppermute | solution.py:342
  628.3 177.8 %collective-permute-start.31 = (bf16[16,32,1024]{2,0,1:T(8,128)(2,1)S(1)}, bf16[16,32,1024]{2,0,1:T(8,128)(2,1)S(1)}, u32[]{:S(2)}, u32[]{:S(2)}) collective-permute-start(bf16[16,32,1024]{2,0,1:T(8,128)(2,1)S(1)} %fusion.74), channel_id=1, source_target_pairs={{2,0},{3,1},{4,2},{5,3},{10,8},{11,9},{12,10},{13,11},{18,16},{19,... | collective-permute-start | bytes 3145736 | tf_op jit(solution)/shard_map/ppermute | solution.py:342
  812.7 21.7 %collective-permute-start.42 = (bf16[64,16,1024]{2,0,1:T(8,128)(2,1)}, bf16[64,16,1024]{2,0,1:T(8,128)(2,1)}, u32[]{:S(2)}, u32[]{:S(2)}) collective-permute-start(bf16[64,16,1024]{2,0,1:T(8,128)(2,1)} %get-tuple-element.86), channel_id=1, source_target_pairs={{0,1},{1,0},{2,3},{3,2},{4,5},{5,4},{6,7},{7,6},{8,9},{9,8},{10,11... | collective-permute-start | bytes 6291464 | tf_op jit(solution)/shard_map/ppermute | solution.py:342
  (93 other events, 1537.3 us)
Sparse Core Ops, SparseCore 0:
  618.6 144.9 reduce-scatter.2
  834.5 75.4 reduce-scatter.4

commit v2 on v1

v2 whole, which is shorter than its diff:
```python
import functools
import math

import jax
import jax.numpy as jnp
from jax import lax
from jax.experimental import pallas as pl
from jax.experimental.pallas import tpu as pltpu
from jax.sharding import PartitionSpec as P

HEADS = 8
ROW_STEP = 4
COL_STEP = 8
TILE = 256
GROUPS = 4
NONE = -1e30
FLOOR = -1e29
FAR = 1 << 20
NT = (((1,), (1,)), ((), ()))
NN = (((1,), (0,)), ((), ()))
TN = (((0,), (0,)), ((), ()))
VMEM_LIMIT = 48 * 1024 * 1024


def dot(left, right, form):
    return lax.dot_general(left, right, form, preferred_element_type=jnp.float32)


def spread(values, first, packed, width):
    zero = jnp.zeros((values.shape[0], width), values.dtype)
    lines = []
    for i in range(packed):
        own = values[:, (first + i) * width : (first + i + 1) * width]
        lines.append(jnp.concatenate([own if j == i else zero for j in range(packed)], axis=1))
    return jnp.concatenate(lines, axis=0)


def tile_lanes(values, times):
    return jnp.concatenate([values] * times, axis=1) if times > 1 else values


def part_stats(query, key, value, grad, mask, packed, store):
    width = key.shape[1] // HEADS
    scaling = 1.0 / math.sqrt(width)
    for first in range(0, HEADS, packed):
        lanes = slice(first * width, (first + packed) * width)
        scores = dot(key[:, lanes], spread(query, first, packed, width), NT) * scaling
        grad_prob = dot(value[:, lanes], spread(grad, first, packed, width), NT)
        scores = jnp.where(mask, scores, NONE)
        highest = jnp.maximum(jnp.max(scores, axis=0, keepdims=True), FLOOR)
        weights = jnp.exp(scores - highest)
        total = jnp.sum(weights, axis=0, keepdims=True)
        product = jnp.sum(weights * grad_prob, axis=0, keepdims=True)
        store(first, highest, total, product)


def part_grads(query, key, value, grad, mask, packed, load, store):
    width = key.shape[1] // HEADS
    scaling = 1.0 / math.sqrt(width)
    count = query.shape[0]
    for first in range(0, HEADS, packed):
        lanes = slice(first * width, (first + packed) * width)
        query_d = spread(query, first, packed, width)
        grad_d = spread(grad, first, packed, width)
        joint, inverse, delta = load(first)
        scores = dot(key[:, lanes], query_d, NT) * scaling
        grad_prob = dot(value[:, lanes], grad_d, NT)
        scores = jnp.where(mask, scores, NONE)
        prob = jnp.exp(scores - joint) * inverse
        grad_score = (prob * (grad_prob - delta)).astype(jnp.bfloat16)
        prob = prob.astype(jnp.bfloat16)
        grad_value = dot(prob, grad_d, NN)
        grad_key = dot(grad_score, query_d, NN) * scaling
        mixed, grad_query = [], []
        prob_t, score_t = prob.T, grad_score.T
        for i in range(packed):
            ours = slice(i * count, (i + 1) * count)
            head = slice((first + i) * width, (first + i + 1) * width)
            mixed.append(dot(prob_t[ours], value[:, head], NN))
            grad_query.append(dot(score_t[ours], key[:, head], NN) * scaling)
        store(
            lanes,
            jnp.concatenate(mixed, axis=1),
            jnp.concatenate(grad_query, axis=1),
            grad_key,
            grad_value,
        )


def row_mask(scalars, row, count, packed):
    keys = lax.broadcasted_iota(jnp.int32, (count, count), 0)
    queries = lax.broadcasted_iota(jnp.int32, (count, count), 1)
    limit = scalars[0] - row * count
    allowed = (keys < queries) & (keys < limit) | (keys == queries)
    return tile_lanes(allowed.astype(jnp.int32), packed) > 0


def thirds(ref, i):
    width = ref.shape[2] // 3
    return [ref[i, :, j * width : (j + 1) * width] for j in range(3)]


def halves(ref, i):
    width = ref.shape[2] // 2
    return ref[i, :, :width], ref[i, :, width:]


def row_stats_kernel(packed, scalars, qkv, grad, stats):
    count = qkv.shape[1]
    for i in range(qkv.shape[0]):
        mask = row_mask(scalars, scalars[1] + pl.program_id(0) * qkv.shape[0] + i, count, packed)

        def store(first, *items):
            for j, item in enumerate(items):
                stats[i, j : j + 1, first * count : (first + packed) * count] = item

        part_stats(*thirds(qkv, i), grad[i], mask, packed, store)


def row_grads_kernel(packed, scalars, stats, qkv, grad, mixed, g_qkv):
    count = qkv.shape[1]
    width = grad.shape[2]
    for i in range(qkv.shape[0]):
        mask = row_mask(scalars, scalars[1] + pl.program_id(0) * qkv.shape[0] + i, count, packed)

        def load(first):
            return [stats[i, j : j + 1, first * count : (first + packed) * count] for j in range(3)]

        def store(lanes, mixed_v, query_v, key_v, value_v):
            mixed[i, :, lanes] = mixed_v.astype(mixed.dtype)
            for j, item in enumerate((query_v, key_v, value_v)):
                place = slice(j * width + lanes.start, j * width + lanes.stop)
                g_qkv[i, :, place] = item.astype(g_qkv.dtype)

        part_grads(*thirds(qkv, i), grad[i], mask, packed, load, store)


def col_mask(scalars, key_rows, query_rows, column, stride):
    rows = key_rows[...]
    rows = jnp.where(rows * stride + column < scalars[0], rows, FAR)
    times = query_rows.shape[1] // rows.shape[1]
    return tile_lanes(rows, times) < query_rows[0:1, :]


def col_stats_kernel(
    packed, stride, scalars, key_rows, query_rows, query, guest, grad, guest_grad, weight, *rest
):
    *held, stats, crossed, kv, inputs = rest
    count = 2 * query.shape[1]
    half = query.shape[1]
    for b, item in enumerate(held):
        inputs[:, b * half : (b + 1) * half, :] = item[...]
    columns, keys, width = inputs.shape
    flat = inputs[...].reshape(columns * keys, width)
    for at in range(0, 2 * width, TILE):
        part = dot(flat, weight[:, at : at + TILE], NN).astype(kv.dtype)
        kv[:, :, at : at + TILE] = part.reshape(columns, keys, TILE)
    for i in range(kv.shape[0]):
        column = scalars[1] + pl.program_id(0) * kv.shape[0] + i
        mask = col_mask(scalars, key_rows, query_rows, column, stride)

        def store(first, *items):
            lanes = slice(first * count, (first + packed) * count)
            for j, item in enumerate(items):
                stats[i, j : j + 1, lanes] = item
                pieces = []
                for h in range(packed):
                    pieces.append(item[:, h * count + half : (h + 1) * count])
                    pieces.append(item[:, h * count : h * count + half])
                crossed[i, j : j + 1, lanes] = jnp.concatenate(pieces, axis=1)

        query_v = jnp.concatenate([query[i], guest[i]], axis=0)
        grad_v = jnp.concatenate([grad[i], guest_grad[i]], axis=0)
        part_stats(query_v, *halves(kv, i), grad_v, mask, packed, store)


def join(parts):
    highs = [jnp.where(total > 0.0, high, NONE) for high, total, _ in parts]
    joint = functools.reduce(jnp.maximum, highs)
    factors = [jnp.exp(high - joint) for high in highs]
    total = sum(part[1] * factor for part, factor in zip(parts, factors))
    product = sum(part[2] * factor for part, factor in zip(parts, factors))
    inverse = jnp.where(total > 0.0, 1.0 / jnp.where(total > 0.0, total, 1.0), 0.0)
    return joint, inverse, product * inverse


def col_grads_kernel(
    packed, stride, scalars, key_rows, query_rows, row_part, own_part, other_part,
    query, guest, kv, grad, guest_grad, weight,
    final, mixed, g_query, back, g_kv, *terms,
):
    half = query.shape[1]
    count = 2 * half
    width = query.shape[2]
    for i in range(kv.shape[0]):
        column = scalars[1] + pl.program_id(0) * kv.shape[0] + i
        mask = col_mask(scalars, key_rows, query_rows, column, stride)

        def load(first):
            lanes = slice(first * count, (first + packed) * count)
            parts = [
                [part[i, j : j + 1, lanes] for j in range(3)]
                for part in (row_part, own_part, other_part)
            ]
            result = join(parts)
            for j in range(3):
                final[i, j : j + 1, lanes] = result[j]
            return result

        def store(lanes, mixed_v, query_v, key_v, value_v):
            mixed[i, :, lanes] = mixed_v[:half].astype(mixed.dtype)
            g_query[i, :, lanes] = query_v[:half].astype(g_query.dtype)
            second = slice(width + lanes.start, width + lanes.stop)
            back[i, :, lanes] = mixed_v[half:].astype(back.dtype)
            back[i, :, second] = query_v[half:].astype(back.dtype)
            g_kv[i, :, lanes] = key_v.astype(g_kv.dtype)
            g_kv[i, :, second] = value_v.astype(g_kv.dtype)

        query_v = jnp.concatenate([query[i], guest[i]], axis=0)
        grad_v = jnp.concatenate([grad[i], guest_grad[i]], axis=0)
        part_grads(query_v, *halves(kv, i), grad_v, mask, packed, load, store)

    columns, keys, _ = g_kv.shape
    flat = g_kv[...].reshape(columns * keys, 2 * width)
    for at in range(0, width, TILE):
        part = dot(flat, weight[:, at : at + TILE], NN).astype(g_kv.dtype).reshape(columns, keys, TILE)
        for b, term in enumerate(terms):
            term[:, :, at : at + TILE] = part[:, b * half : (b + 1) * half]


def call(kernel, steps, in_specs, out_specs, out_shapes, flops, operands):
    return pl.pallas_call(
        kernel,
        grid=(steps,),
        in_specs=in_specs,
        out_specs=out_specs,
        out_shape=out_shapes,
        compiler_params=pltpu.CompilerParams(vmem_limit_bytes=VMEM_LIMIT),
        cost_estimate=pl.CostEstimate(flops=flops, bytes_accessed=flops // 1000, transcendentals=0),
    )(*operands)


def block(shape, offset=0):
    rest = (0,) * (len(shape) - 1)
    return pl.BlockSpec(shape, lambda s: (s + offset,) + rest)


def whole(shape):
    return pl.BlockSpec(shape, lambda s: (0,) * len(shape))


SCALARS = pl.BlockSpec(memory_space=pltpu.SMEM)


def row_stats(scalars, qkv, grad):
    rows, count, width = grad.shape
    packed = max(1, min(HEADS, 256 // count))
    step = math.gcd(rows, ROW_STEP)
    return call(
        functools.partial(row_stats_kernel, packed),
        rows // step,
        [SCALARS, block((step, count, 3 * width)), block((step, count, width))],
        block((step, 3, HEADS * count)),
        jax.ShapeDtypeStruct((rows, 3, HEADS * count), jnp.float32),
        4 * rows * count * count * width * 4,
        (scalars, qkv, grad),
    )


def row_grads(scalars, stats, qkv, grad):
    rows, count, width = grad.shape
    packed = max(1, min(HEADS, 256 // count))
    step = math.gcd(rows, ROW_STEP)
    one, three = block((step, count, width)), block((step, count, 3 * width))
    return call(
        functools.partial(row_grads_kernel, packed),
        rows // step,
        [SCALARS, block((step, 3, HEADS * count)), three, one],
        [one, three],
        [jax.ShapeDtypeStruct(x.shape, jnp.bfloat16) for x in (grad, qkv)],
        12 * rows * count * count * width * 4,
        (scalars, stats, qkv, grad),
    )


def col_sizes(query):
    columns, half, width = query.shape
    packed = max(1, min(HEADS, 256 // (2 * half)))
    return half, packed, columns, math.gcd(columns, COL_STEP), width


def col_stats(scalars, key_rows, query_rows, query, guest, grad, guest_grad, weight, held, stride):
    half, packed, columns, step, width = col_sizes(query)
    keys = half * len(held)
    own = block((step, half, width))
    stat = block((step, 3, HEADS * 2 * half))
    shape = jax.ShapeDtypeStruct((columns, 3, HEADS * 2 * half), jnp.float32)
    large = jax.ShapeDtypeStruct((columns, keys, 2 * width), jnp.bfloat16)
    joined = jax.ShapeDtypeStruct((columns, keys, width), jnp.bfloat16)
    return call(
        functools.partial(col_stats_kernel, packed, stride),
        columns // step,
        [SCALARS, whole(key_rows.shape), whole(query_rows.shape)]
        + [own, own, own, own, whole(weight.shape)]
        + [own] * len(held),
        [stat, stat, block((step, keys, 2 * width)), block((step, keys, width))],
        [shape, shape, large, joined],
        4 * columns * keys * width * (2 * half * 4 + width),
        (scalars, key_rows, query_rows, query, guest, grad, guest_grad, weight, *held),
    )


def col_grads(
    scalars, key_rows, query_rows, row_part, own_part, other_part,
    query, guest, kv, grad, guest_grad, weight, offset, stride,
):
    half, packed, columns, step, width = col_sizes(query)
    keys = kv.shape[1]
    blocks = keys // half
    own = block((step, half, width))
    both = block((step, half, 2 * width))
    pair = block((step, keys, 2 * width))
    stat = block((step, 3, HEADS * 2 * half))
    stat_off = block((step, 3, HEADS * 2 * half), offset // step)
    shape = jax.ShapeDtypeStruct((columns, 3, HEADS * 2 * half), jnp.float32)
    small = jax.ShapeDtypeStruct((columns, half, width), jnp.bfloat16)
    twice = jax.ShapeDtypeStruct((columns, half, 2 * width), jnp.bfloat16)
    large = jax.ShapeDtypeStruct(kv.shape, jnp.bfloat16)
    return call(
        functools.partial(col_grads_kernel, packed, stride),
        columns // step,
        [SCALARS, whole(key_rows.shape), whole(query_rows.shape), stat_off, stat, stat]
        + [own, own, pair, own, own, whole(weight.shape)],
        [stat, own, own, both, pair] + [own] * blocks,
        [shape, small, small, twice, large] + [small] * blocks,
        4 * columns * keys * width * (6 * half * 4 + width),
        (scalars, key_rows, query_rows, row_part, own_part, other_part)
        + (query, guest, kv, grad, guest_grad, weight),
    )


def product(values, weight):
    return jnp.einsum("...d,df->...f", values, weight, preferred_element_type=jnp.float32)


def product_t(values, weight):
    return jnp.einsum("...f,df->...d", values, weight, preferred_element_type=jnp.float32)


def weight_product(values, grads):
    return jnp.einsum("abd,abf->df", values, grads, preferred_element_type=jnp.float32)


def narrow(values):
    return values.astype(jnp.bfloat16)


def body(tokens, lengths, w_qkv, out_grad):
    seq_count = lax.axis_size("seq")
    seq_index = lax.axis_index("seq")
    chips = seq_count // 2
    chip, core = seq_index // 2, seq_index % 2
    seq_local, row_local, columns, width = tokens.shape
    half_cols = columns // 2
    chip_rows = 2 * row_local
    group = half_cols // GROUPS
    w_q = w_qkv[0]
    w_kv = jnp.concatenate([w_qkv[1], w_qkv[2]], axis=1)
    w_all = jnp.concatenate([w_q, w_kv], axis=1)
    w_kv_t = jnp.concatenate([w_qkv[1].T, w_qkv[2].T], axis=0)

    def pairs(links):
        return [(2 * a + c, 2 * b + c) for a, b in links for c in (0, 1)]

    swap = [(i, i ^ 1) for i in range(seq_count)]
    up = {k: pairs([(z - 1, z) for z in range(k, chips - 1)]) for k in range(1, chips - 1)}
    down = {k: [(b, a) for a, b in up[k]] for k in up}
    guest_up = pairs([(chips - 2, chips - 1)])
    guest_down = pairs([(chips - 1, chips - 2)])

    def send(values, perm):
        return lax.ppermute(values, "seq", perm)

    def to_columns(values, axis, row_axis):
        mine = lax.dynamic_slice_in_dim(values, core * half_cols, half_cols, axis)
        others = lax.dynamic_slice_in_dim(values, (1 - core) * half_cols, half_cols, axis)
        return jnp.concatenate([mine, send(others, swap)], axis=row_axis)

    def to_rows(values, axis, row_axis):
        mine = lax.slice_in_dim(values, 0, row_local, axis=row_axis)
        others = send(lax.slice_in_dim(values, row_local, chip_rows, axis=row_axis), swap)
        return jnp.where(
            core == 0,
            jnp.concatenate([mine, others], axis=axis),
            jnp.concatenate([others, mine], axis=axis),
        )

    tokens_r, grad_r = tokens[0], out_grad[0]
    limit = lengths[0]


    def by_group(values):
        values = jnp.swapaxes(values, 0, 1)
        mine = lax.dynamic_slice_in_dim(values, core * half_cols, half_cols, 0)
        others = lax.dynamic_slice_in_dim(values, (1 - core) * half_cols, half_cols, 0)
        items = []
        for g in range(GROUPS):
            part = slice(g * group, (g + 1) * group)
            items.append(jnp.concatenate([mine[part], send(others[part], swap)], axis=1))
        return items

    tokens_c, grad_c = by_group(tokens_r), by_group(grad_r)

    order = (jnp.arange(chip_rows, dtype=jnp.int32) + core * row_local) % chip_rows
    key_ids = []
    for k in range(chips - 2, -1, -1):
        valid = (chip >= k) & (chip <= chips - 2) if k > 0 else chip >= 0
        key_ids.append(jnp.where(valid, (chip - k) * chip_rows + order, FAR))
    key_ids = jnp.concatenate(key_ids)
    query_ids = jnp.concatenate(
        [chip * chip_rows + order, jnp.where(chip == chips - 2, (chip + 1) * chip_rows + order, -1)]
    )
    packed = max(1, min(HEADS, 256 // (2 * chip_rows)))
    lane = min(128, packed * 2 * chip_rows)
    key_rows = jnp.broadcast_to(key_ids[:, None], (key_ids.shape[0], lane))
    query_rows = jnp.broadcast_to(jnp.tile(query_ids, packed)[None], (8, packed * 2 * chip_rows))

    hops = chips - 2
    live = dict(tokens_c=tokens_c, grad_c=grad_c, tokens_r=tokens_r, grad_r=grad_r)
    live["held"] = [[tokens_c[g]] for g in range(GROUPS)]
    row_scalars = jnp.stack([limit, seq_index * row_local]).astype(jnp.int32)
    cross = guest_up + guest_down
    names = ("guest", "guest_grad", "kv", "own", "other", "final", "mixed", "query", "terms")
    names += ("back", "moving", "swapped", "w_parts", "query_c")
    live.update({name: [None] * GROUPS for name in names})

    def scalars_of(g):
        return jnp.stack([limit, core * half_cols + g * group]).astype(jnp.int32)

    def step(g, s):
        if 0 <= s < hops:
            live["held"][g].append(send(live["held"][g][-1], up[s + 1]))
        if s == max(hops - 2, 0):
            live["query_c"][g] = narrow(product(live["tokens_c"][g], w_q))
        if s == hops - 1:
            query, grad = live["query_c"][g], live["grad_c"][g]
            if g > 0:
                query, grad, live["crossed"] = lax.optimization_barrier((query, grad, live["crossed"]))
            live["guest"][g] = send(query, guest_down)
            live["guest_grad"][g] = send(grad, guest_down)
        if s == hops:
            live["own"][g], crossed, live["kv"][g], live["held"][g] = col_stats(
                scalars_of(g), key_rows, query_rows,
                live["query_c"][g], live["guest"][g], live["grad_c"][g], live["guest_grad"][g],
                w_kv, live["held"][g][::-1], columns
            )
            live["crossed"] = crossed
            live["other"][g] = send(crossed, cross)
        if s == hops + 1:
            row_part = live["row_part"]
            if g + 1 < GROUPS:
                row_part, live["own"][g + 1] = lax.optimization_barrier((row_part, live["own"][g + 1]))
            final, mixed, g_query, back, g_kv, *terms = col_grads(
                scalars_of(g), key_rows, query_rows, row_part, live["own"][g], live["other"][g],
                live["query_c"][g], live["guest"][g], live["kv"][g], live["grad_c"][g],
                live["guest_grad"][g], w_kv_t, g * group, columns
            )
            live["final"][g], live["mixed"][g], live["query"][g] = final, mixed, g_query
            live["kv"][g], live["back"][g], live["terms"][g] = g_kv, back, terms
        if s == hops + 2:
            back = live["back"][g]
            if g + 2 < GROUPS:
                back, live["crossed"] = lax.optimization_barrier((back, live["crossed"]))
            live["back"][g] = send(back, guest_up)
        if s == hops + 3:
            back = live["back"][g]
            live["mixed"][g] = narrow(
                live["mixed"][g].astype(jnp.float32) + back[..., :width].astype(jnp.float32)
            )
            live["query"][g] = narrow(
                live["query"][g].astype(jnp.float32) + back[..., width:].astype(jnp.float32)
            )
            live["swapped"][g] = send(live["mixed"][g][:, row_local:], swap)
            live["w_parts"][g] = [
                narrow(weight_product(live["tokens_c"][g], live["query"][g])),
                narrow(weight_product(live["held"][g], live["kv"][g])),
            ]
        if hops + 2 <= s <= 2 * hops + 2:
            k = 2 * hops + 2 - s
            term = live["terms"][g][hops - k]
            if k < hops:
                term = term.astype(jnp.float32) + live["moving"][g].astype(jnp.float32)
            if k > 0:
                live["moving"][g] = send(narrow(term), down[k])
            else:
                own = narrow(term + product_t(live["query"][g], w_q))
                live["moving"][g] = (own[:, :row_local], send(own[:, row_local:], swap))

    for t in range(GROUPS + 2 * hops + 2):
        if t == 0:
            live["rows"] = narrow(product(live["tokens_r"], w_all))
        if t == 1:
            part = row_stats(row_scalars, live["rows"], live["grad_r"])
            part = part.reshape(row_local, 3, HEADS, columns).transpose(3, 1, 2, 0)
            part = to_columns(part, 0, 3)
            part = jnp.concatenate([part, send(part, guest_down)], axis=3)
            live["row_part"] = part.reshape(half_cols, 3, HEADS * 2 * chip_rows)
        if t == GROUPS + hops + 1:
            final = jnp.concatenate(live["final"], axis=0).reshape(half_cols, 3, HEADS, 2 * chip_rows)
            final = to_rows(final[..., :chip_rows], 0, 3)
            final = final.transpose(3, 1, 2, 0).reshape(row_local, 3, HEADS * columns)
            live["row_grads"] = row_grads(row_scalars, final, live["rows"], live["grad_r"])
        if t == GROUPS + hops + 2:
            live["w_row"] = weight_product(live["tokens_r"], live["row_grads"][1])
        for g in sorted(range(GROUPS), key=lambda g: t - g != hops):
            step(g, t - g)
        live = lax.optimization_barrier(live)

    def assemble(mine, others):
        mine, others = jnp.concatenate(mine, axis=0), jnp.concatenate(others, axis=0)
        joined = jnp.where(
            core == 0,
            jnp.concatenate([mine, others], axis=0),
            jnp.concatenate([others, mine], axis=0),
        )
        return jnp.swapaxes(joined, 0, 1).astype(jnp.float32)

    mixed_r, row_g = live["row_grads"]
    mixed_b = assemble([item[:, :row_local] for item in live["mixed"]], live["swapped"])
    attention = narrow(mixed_r.astype(jnp.float32) + mixed_b)
    terms_b = assemble(*zip(*live["moving"]))
    input_grad = narrow(product_t(row_g, w_all) + terms_b)

    shares = []
    for j in range(3):
        place = slice(j * width, (j + 1) * width)
        total = live["w_row"][:, place]
        for first, second in live["w_parts"]:
            part = first if j == 0 else second[:, (j - 1) * width : j * width]
            total = total + part.astype(jnp.float32)
        total = narrow(total).reshape(chips, 2, width // seq_count, width)
        mine = lax.dynamic_index_in_dim(total, core, 1, keepdims=False)
        others = lax.dynamic_index_in_dim(total, 1 - core, 1, keepdims=False)
        shares.append(narrow(mine.astype(jnp.float32) + send(others, swap).astype(jnp.float32)))
    share = jnp.stack(shares)
    share = lax.psum_scatter(share, "dp", scatter_dimension=3, tiled=True)
    rings = [[2 * z + c for z in range(chips)] for c in (0, 1)]
    share = lax.psum_scatter(share, "seq", scatter_dimension=1, axis_index_groups=rings, tiled=True)
    w_grads = share[:, 0].astype(jnp.float32)
    return (attention[None], input_grad[None], w_grads)


def solution(mesh):
    in_specs = (P("dp", "seq", None, None), P("dp"), P(), P("dp", "seq", None, None))
    out_specs = (P("dp", "seq", None, None), P("dp", "seq", None, None), P(None, "seq", "dp"))
    return jax.shard_map(body, mesh=mesh, in_specs=in_specs, out_specs=out_specs, check_vma=False)
```

time: 927 us -> 765 us (0.83)
  waiting for transfers between devices: 256 us -> 117 us
  matrix products: 282 us -> 145 us
  Pallas kernels: 147 us -> 191 us
  local copies, waits for them, and re-layouts: 69.4 us -> 104 us
  other arithmetic: 46.9 us -> 69.9 us
  starting transfers between devices: 101 us -> 115 us
    ppermute x46 -> x54, waiting for transfers between devices: 195 us -> 79.9 us  [send(): return lax.ppermute(values, 'seq', perm)]
    dot_general x15 -> x5, matrix products: 105 us -> 34.9 us  [product_t(): jnp.einsum('...f,df->...d', values, weight, preferred_element_type=jnp.fl...]
    reduce_scatter x1, waiting for transfers between devices: 61.2 us -> 10.6 us  [body(): lax.psum_scatter(share, 'seq', scatter_dimension=1, axis_index_groups=rin...]
    dot_general x12 -> x5, matrix products: 81.5 us -> 35.1 us  [product(): jnp.einsum('...d,df->...f', values, weight, preferred_element_type=jnp.fl...]
    pallas_call x10, Pallas kernels: 147 us -> 191 us  [call(): pl.pallas_call(kernel, grid=(steps,), in_specs=in_specs, out_specs=out_sp...]
    reduce_scatter x1, waiting for transfers between devices: 0.01 us -> 26 us  [body(): share = lax.psum_scatter(share, 'dp', scatter_dimension=3, tiled=True)]
    unnamed x188 -> x241, local copies, waits for them, and re-layouts: 13.4 us -> 37.5 us
    dot_general x15 -> x9, matrix products: 95.7 us -> 74.7 us  [weight_product(): jnp.einsum('abd,abf->df', values, grads, preferred_element_type=jnp.float32)]
  transfers between devices with their start and end apart: 48 -> 56, of which waited for: 9 -> 10; matrix products, arithmetic and copies ran while one was open for 40% -> 35% of each run, Pallas kernels for 14% -> 16%
where the time goes in v2:
time: 765 us; the launch traced here: 757 us
  Pallas kernels  191 us (25%)
  matrix products  145 us (19%)
  waiting for transfers between devices  117 us (15%)
  starting transfers between devices  115 us (15%)
  local copies, waits for them, and re-layouts  104 us (14%)
  other arithmetic  69.9 us (9%)
  between operations  16.7 us (2%)
    pallas_call x10, Pallas kernels, call(): pl.pallas_call(kernel, grid=(steps,), in_specs=in_specs, out_specs=out_sp...  191 us
    ppermute x54, starting transfers between devices, send(): return lax.ppermute(values, 'seq', perm)  115 us
    ppermute x54, waiting for transfers between devices, send(): return lax.ppermute(values, 'seq', perm)  79.9 us
    dot_general x9, matrix products, weight_product(): jnp.einsum('abd,abf->df', values, grads, preferred_element_type=jnp.float32)  74.7 us
    unnamed x241, local copies, waits for them, and re-layouts  37.5 us
    convert_element_type x9, other arithmetic, narrow(): return values.astype(jnp.bfloat16)  36 us
    dot_general x5, matrix products, product(): jnp.einsum('...d,df->...f', values, weight, preferred_element_type=jnp.fl...  35.1 us
    dot_general x5, matrix products, product_t(): jnp.einsum('...f,df->...d', values, weight, preferred_element_type=jnp.fl...  34.9 us
  transfers between devices with their start and end apart: 56, of which 10 were waited for; matrix products, arithmetic and copies ran while one was open for 35% of the time, Pallas kernels for 16%

profile of v2, /device:TPU:0, one launch (start us, length us, event | category | flops | bytes accessed | tf_op | source)
XLA Modules:
  0.0 757.3 jit_solution(6314717253094441320)
XLA Ops:
  7.2 4.5 constant_dynamic-slice_fusion.3
  29.1 4.6 copy.247
  33.7 3.9 copy.246
  37.6 4.2 pad_maximum_fusion
  41.8 18.3 %convert_bitcast_fusion.qkv = bf16[16,128,3072]{2,1,0:T(8,128)(2,1)} fusion(bf16[1024,1024]{0,1:T(8,128)(2,1)S(1)} %bitcast.202, bf16[1024,1024]{0,1:T(8,128)(2,1)S(1)} %bitcast.207, bf16[1024,1024]{0,1:T(8,128)(2,1)} %bitcast.222, bf16[1,16,128,1024]{3,2,1,0:T(8,128)(2,1)} %param.4), kind=kOutput, calls=%fused_computation | convolution fusion | flops 12910067712 | bytes 23068672 | tf_op jit(solution)/shard_map/...d,df->...f/dot_general | solution.py:343
  63.7 6.5 copy.154.weight
  74.2 5.6 collective-permute-start.5
  88.3 4.1 fusion.24.query
  92.4 9.4 %collective-permute-done.5.rest_1_ = bf16[16,32,1024]{2,1,0:T(8,128)(2,1)} collective-permute-done((bf16[16,32,1024]{2,1,0:T(8,128)(2,1)S(1)}, bf16[16,32,1024]{2,1,0:T(8,128)(2,1)}, u32[]{:S(2)}, u32[]{:S(2)}) %collective-permute-start.5) | collective-permute-done | bytes 1048608 | tf_op jit(solution)/shard_map/ppermute | solution.py:382
  106.8 7.6 collective-permute-start.12
  114.4 8.7 %shard_map.67 = f32[16,3,1024]{2,1,0:T(4,128)S(1)} custom-call(s32[2]{0:T(128)S(1)} %get-tuple-element.821.scalars, bf16[16,128,3072]{2,1,0:T(8,128)(2,1)} %convert_bitcast_fusion.qkv, bf16[16,128,1024]{2,1,0:T(8,128)(2,1)S(1)} %bitcast.200), custom_call_target="tpu_custom_call" | custom-call | flops 4294967296 | bytes 4294967 | tf_op jit(solution)/shard_map/pallas_call | solution.py:232
  126.0 4.2 fusion.27.query
  135.6 16.8 %shard_map.68 = (f32[16,3,512]{2,1,0:T(4,128)S(1)}, f32[16,3,512]{2,1,0:T(4,128)S(1)}, bf16[16,96,2048]{2,1,0:T(8,128)(2,1)}, bf16[16,96,1024]{2,1,0:T(8,128)(2,1)}) custom-call(s32[2]{0:T(128)S(1)} %get-tuple-element.820.scalars, s32[96,128]{1,0:T(8,128)S(1)} %broadcast_in_dim.29.key_rows, s32[8,256]{1,0:T(8,128)S(1)} %broadcast_in_dim.32.query_rows, ...), custom_call_target="tpu_custom_call" | custom-call | flops 8053063680 | bytes 8053063 | tf_op jit(solution)/shard_map/pallas_call | solution.py:232
  157.4 34.9 %collective-permute-start.18 = (bf16[16,32,1024]{2,1,0:T(8,128)(2,1)}, bf16[16,32,1024]{2,1,0:T(8,128)(2,1)}, u32[]{:S(2)}, u32[]{:S(2)}) collective-permute-start(bf16[16,32,1024]{2,1,0:T(8,128)(2,1)} %pad_maximum_fusion.9.rest_2_), channel_id=1, source_target_pairs={{0,2},{1,3},{2,4},{3,5},{8,10},{9,11},{10,12},{11,13},{16,18},{17,... | collective-permute-start | bytes 3145736 | tf_op jit(solution)/shard_map/ppermute | solution.py:382
  192.4 4.7 pad_maximum_fusion.1.weight
  197.7 3.2 fusion.30.query
  201.0 11.5 %collective-permute-done.18.rest_1_ = bf16[16,32,1024]{2,1,0:T(8,128)(2,1)} collective-permute-done((bf16[16,32,1024]{2,1,0:T(8,128)(2,1)}, bf16[16,32,1024]{2,1,0:T(8,128)(2,1)}, u32[]{:S(2)}, u32[]{:S(2)}) %collective-permute-start.18) | collective-permute-done | bytes 1048608 | tf_op jit(solution)/shard_map/ppermute | solution.py:382
  212.5 16.6 %shard_map.69 = (f32[16,3,512]{2,1,0:T(4,128)S(1)}, f32[16,3,512]{2,1,0:T(4,128)S(1)}, bf16[16,96,2048]{2,1,0:T(8,128)(2,1)}, bf16[16,96,1024]{2,1,0:T(8,128)(2,1)}) custom-call(s32[2]{0:T(128)S(1)} %pad_add_fusion.4.scalars, s32[96,128]{1,0:T(8,128)S(1)} %broadcast_in_dim.29.key_rows, s32[8,256]{1,0:T(8,128)S(1)} %broadcast_in_dim.32.query_rows, ...), custom_call_target="tpu_custom_call" | custom-call | flops 8053063680 | bytes 8053063 | tf_op jit(solution)/shard_map/pallas_call | solution.py:232
  232.3 28.2 %collective-permute-start.23 = (bf16[16,32,1024]{2,1,0:T(8,128)(2,1)S(1)}, bf16[16,32,1024]{2,1,0:T(8,128)(2,1)S(1)}, u32[]{:S(2)}, u32[]{:S(2)}) collective-permute-start(bf16[16,32,1024]{2,1,0:T(8,128)(2,1)S(1)} %copy-done.83), channel_id=1, source_target_pairs={{0,2},{1,3},{2,4},{3,5},{8,10},{9,11},{10,12},{11,13},{16,18},{17,... | collective-permute-start | bytes 3145736 | tf_op jit(solution)/shard_map/ppermute | solution.py:382
  260.5 22.7 %shard_map.70 = (f32[16,3,512]{2,1,0:T(4,128)S(1)}, bf16[16,32,1024]{2,1,0:T(8,128)(2,1)S(1)}, bf16[16,32,1024]{2,1,0:T(8,128)(2,1)S(1)}, bf16[16,32,2048]{2,1,0...) custom-call(s32[2]{0:T(128)S(1)} %get-tuple-element.820.scalars, ...), custom_call_target="tpu_custom_call" | custom-call | flops 11274289152 | bytes 11274289 | tf_op jit(solution)/shard_map/pallas_call | solution.py:232
  283.2 5.3 fusion.33.query
  288.6 16.4 %shard_map.71 = (f32[16,3,512]{2,1,0:T(4,128)S(1)}, f32[16,3,512]{2,1,0:T(4,128)S(1)}, bf16[16,96,2048]{2,1,0:T(8,128)(2,1)}, bf16[16,96,1024]{2,1,0:T(8,128)(2,1)}) custom-call(s32[2]{0:T(128)S(1)} %pad_add_fusion.5.scalars, s32[96,128]{1,0:T(8,128)S(1)} %broadcast_in_dim.29.key_rows, s32[8,256]{1,0:T(8,128)S(1)} %broadcast_in_dim.32.query_rows, ...), custom_call_target="tpu_custom_call" | custom-call | flops 8053063680 | bytes 8053063 | tf_op jit(solution)/shard_map/pallas_call | solution.py:232
  316.9 23.0 %shard_map.72 = (f32[16,3,512]{2,1,0:T(4,128)S(1)}, bf16[16,32,1024]{2,1,0:T(8,128)(2,1)S(1)}, bf16[16,32,1024]{2,1,0:T(8,128)(2,1)S(1)}, bf16[16,32,2048]{2,1,0...) custom-call(s32[2]{0:T(128)S(1)} %pad_add_fusion.4.scalars, ...), custom_call_target="tpu_custom_call" | custom-call | flops 11274289152 | bytes 11274289 | tf_op jit(solution)/shard_map/pallas_call | solution.py:232
  340.0 16.1 %shard_map.73 = (f32[16,3,512]{2,1,0:T(4,128)S(1)}, f32[16,3,512]{2,1,0:T(4,128)S(1)}, bf16[16,96,2048]{2,1,0:T(8,128)(2,1)}, bf16[16,96,1024]{2,1,0:T(8,128)(2,1)}) custom-call(s32[2]{0:T(128)S(1)} %pad_add_fusion.6.scalars, s32[96,128]{1,0:T(8,128)S(1)} %broadcast_in_dim.29.key_rows, s32[8,256]{1,0:T(8,128)S(1)} %broadcast_in_dim.32.query_rows, ...), custom_call_target="tpu_custom_call" | custom-call | flops 8053063680 | bytes 8053063 | tf_op jit(solution)/shard_map/pallas_call | solution.py:232
  365.9 4.0 add_convert_fusion.16
  370.9 8.6 %bitcast_convert_fusion.3 = bf16[1024,2048]{1,0:T(8,128)(2,1)} fusion(bf16[16,96,1024]{2,1,0:T(8,128)(2,1)S(1)} %copy-done.98, bf16[16,96,2048]{2,1,0:T(8,128)(2,1)S(1)} %bitcast.232), kind=kOutput, calls=%fused_computation.8 | convolution fusion | flops 6444548096 | bytes 13631488 | tf_op jit(solution)/shard_map/abd,abf->df/dot_general | solution.py:351
  379.9 22.9 %shard_map.74 = (f32[16,3,512]{2,1,0:T(4,128)S(1)}, bf16[16,32,1024]{2,1,0:T(8,128)(2,1)S(1)}, bf16[16,32,1024]{2,1,0:T(8,128)(2,1)S(1)}, bf16[16,32,2048]{2,1,0...) custom-call(s32[2]{0:T(128)S(1)} %pad_add_fusion.5.scalars, ...), custom_call_target="tpu_custom_call" | custom-call | flops 11274289152 | bytes 11274289 | tf_op jit(solution)/shard_map/pallas_call | solution.py:232
  402.8 4.6 bitcast_convert_fusion.7
  407.4 25.6 %collective-permute-done.32 = bf16[16,32,1024]{2,0,1:T(8,128)(2,1)} collective-permute-done((bf16[16,32,1024]{2,0,1:T(8,128)(2,1)}, bf16[16,32,1024]{2,0,1:T(8,128)(2,1)}, u32[]{:S(2)}, u32[]{:S(2)}) %collective-permute-start.32) | collective-permute-done | bytes 1048608 | tf_op jit(solution)/shard_map/ppermute | solution.py:382
  437.8 3.8 add_convert_fusion.14
  452.5 9.1 %bitcast_convert_fusion.2 = bf16[1024,2048]{1,0:T(8,128)(2,1)} fusion(bf16[16,96,1024]{2,1,0:T(8,128)(2,1)S(1)} %copy-done.97, bf16[16,96,2048]{2,1,0:T(8,128)(2,1)S(1)} %bitcast.230), kind=kOutput, calls=%fused_computation.7 | convolution fusion | flops 6444548096 | bytes 13631488 | tf_op jit(solution)/shard_map/abd,abf->df/dot_general | solution.py:351
  461.8 22.8 %shard_map.75 = (f32[16,3,512]{2,1,0:T(4,128)S(1)}, bf16[16,32,1024]{2,1,0:T(8,128)(2,1)S(1)}, bf16[16,32,1024]{2,1,0:T(8,128)(2,1)S(1)}, bf16[16,32,2048]{2,1,0...) custom-call(s32[2]{0:T(128)S(1)} %pad_add_fusion.6.scalars, ...), custom_call_target="tpu_custom_call" | custom-call | flops 11274289152 | bytes 11274289 | tf_op jit(solution)/shard_map/pallas_call | solution.py:232
  484.7 5.5 bitcast_convert_fusion.6
  490.2 12.9 %collective-permute-done.38 = bf16[16,32,1024]{2,0,1:T(8,128)(2,1)} collective-permute-done((bf16[16,32,1024]{2,0,1:T(8,128)(2,1)}, bf16[16,32,1024]{2,0,1:T(8,128)(2,1)}, u32[]{:S(2)}, u32[]{:S(2)}) %collective-permute-start.38) | collective-permute-done | bytes 1048608 | tf_op jit(solution)/shard_map/ppermute | solution.py:382
  507.6 3.6 add_convert_fusion.10
  527.0 11.4 %bitcast_convert_fusion.1 = bf16[1024,2048]{1,0:T(8,128)(2,1)} fusion(bf16[16,96,1024]{2,1,0:T(8,128)(2,1)} %get-tuple-element.634, bf16[16,96,2048]{2,1,0:T(8,128)(2,1)} %get-tuple-element.636), kind=kOutput, calls=%fused_computation.6 | convolution fusion | flops 6444548096 | bytes 13631488 | tf_op jit(solution)/shard_map/abd,abf->df/dot_general | solution.py:351
  540.9 4.5 bitcast_convert_fusion.5
  547.0 24.8 %shard_map.76 = (bf16[16,128,1024]{2,1,0:T(8,128)(2,1)S(1)}, bf16[16,128,3072]{2,1,0:T(8,128)(2,1)}) custom-call(s32[2]{0:T(128)S(1)} %copy-done.17, f32[16,3,1024]{2,1,0:T(4,128)S(1)} %reshape.85.stats, bf16[16,128,3072]{2,1,0:T(8,128)(2,1)} %convert_bitcast_fusion.qkv, bf16[16,128,1024]{2,1,0:T(8,128)(2,1)} %bitcast.199), custom_call_target="tpu_custom_call" | custom-call | flops 12884901888 | bytes 12884901 | tf_op jit(solution)/shard_map/pallas_call | solution.py:232
  571.9 5.2 add_convert_fusion.6
  586.4 11.9 %bitcast_convert_fusion = bf16[1024,2048]{1,0:T(8,128)(2,1)} fusion(bf16[16,96,1024]{2,1,0:T(8,128)(2,1)S(1)} %copy-done.96, bf16[16,96,2048]{2,1,0:T(8,128)(2,1)} %get-tuple-element.669), kind=kOutput, calls=%fused_computation.5 | convolution fusion | flops 6444548096 | bytes 13631488 | tf_op jit(solution)/shard_map/abd,abf->df/dot_general | solution.py:351
  598.4 16.2 %convolution_bitcast_fusion = f32[1024,3072]{1,0:T(8,128)} fusion(bf16[16,128,1024]{2,1,0:T(8,128)(2,1)S(1)} %bitcast.221, bf16[16,128,3072]{2,1,0:T(8,128)(2,1)S(1)} %bitcast.228), kind=kOutput, calls=%fused_computation.9 | convolution fusion | flops 12884901888 | bytes 29360128 | tf_op jit(solution)/shard_map/abd,abf->df/dot_general | solution.py:351
  617.6 15.0 %collective-permute-done.48 = bf16[16,32,1024]{2,0,1:T(8,128)(2,1)S(1)} collective-permute-done((bf16[16,32,1024]{2,0,1:T(8,128)(2,1)S(1)}, bf16[16,32,1024]{2,0,1:T(8,128)(2,1)S(1)}, u32[]{:S(2)}, u32[]{:S(2)}) %collective-permute-start.48) | collective-permute-done | bytes 1048608 | tf_op jit(solution)/shard_map/ppermute | solution.py:382
  632.6 3.4 add_convert_fusion.3
  638.9 15.4 %add_convert_fusion.1 = (bf16[1024,1024]{1,0:T(8,128)(2,1)S(1)}, bf16[1024,1024]{1,0:T(8,128)(2,1)S(1)}, bf16[1024,1024]{1,0:T(8,128)(2,1)S(1)}) fusion(f32[1024,3072]{1,0:T(8,128)} %convolution_bitcast_fusion, bf16[1024,2048]{1,0:T(8,128)(2,1)} %bitcast_convert_fusion, bf16[1024,2048]{1,0:T(8,128)(2,1)} %bitcast_convert_fusion.1, ...), kind=kLoop, calls=%fused_computation.20 | loop fusion | flops 28311552 | bytes 44040192 | tf_op jit(solution)/shard_map/convert_element_type | solution.py:355
  677.9 19.0 %fusion.3 = bf16[1,16,128,1024]{3,2,1,0:T(8,128)(2,1)} fusion(bf16[128,16,1024]{2,0,1:T(8,128)(2,1)} %constant_dynamic-update-slice_fusion.8, bf16[128,16,1024]{2,0,1:T(8,128)(2,1)} %copy-done.94, pred[]{:T(512)S(6)} %eq.13, bf16[16,128,3072]{2,1,0:T(8,128)(2,1)} %get-tuple-element.735, bf16[1024,1024]{0,1:T(8,128)(2,1)S(1)} %bitcast.204, ...), kind=kOutput, calls=%fused_computation.12 | convolution fusion | flops 12912164864 | bytes 31457280 | tf_op jit(solution)/shard_map/...f,df->...d/dot_general | solution.py:347
  696.9 26.0 %reduce-scatter.3.cloned.1.call-done = bf16[3,4,128,256]{3,2,0,1:T(8,128)(2,1)} async-done(((bf16[3,4,128,1024]{3,2,0,1:T(8,128)(2,1)}), bf16[3,4,128,256]{3,2,0,1:T(8,128)(2,1)}) %reduce-scatter.3.cloned.1.call-update) | async-done | bytes 786448 | tf_op jit(solution)/shard_map/reduce_scatter | solution.py:546
  730.5 7.5 fusion.2
  738.0 10.6 %reduce-scatter.5.cloned.1.call-done = bf16[3,1,128,256]{3,2,0,1:T(8,128)(2,1)} async-done(((bf16[3,4,128,256]{3,2,0,1:T(8,128)(2,1)}), bf16[3,1,128,256]{3,2,0,1:T(8,128)(2,1)}) %reduce-scatter.5.cloned.1.call-update) | async-done | bytes 196624 | tf_op jit(solution)/shard_map/reduce_scatter | solution.py:548
  (430 shorter events, 165.4 us)
Async XLA Ops:
  7.2 715.8 %reduce-scatter.3.cloned.1.call-start = ((), (), s32[]{:S(2)}) async-start(), calls=%async_computation.2 | async-start | bytes 3932160 | tf_op jit(solution)/shard_map/reduce_scatter | solution.py:546
  14.2 56.1 %collective-permute-start = (bf16[16,16,1024]{2,1,0:T(8,128)(2,1)}, bf16[16,16,1024]{2,1,0:T(8,128)(2,1)}, u32[]{:S(2)}, u32[]{:S(2)}) collective-permute-start(bf16[16,16,1024]{2,1,0:T(8,128)(2,1)} %get-tuple-element.788), channel_id=1, source_target_pairs={{0,1},{1,0},{2,3},{3,2},{4,5},{5,4},{6,7},{7,6},{8,9},{9,8},{10,11... | collective-permute-start | bytes 1572872 | tf_op jit(solution)/shard_map/ppermute | solution.py:382
  14.7 59.5 %collective-permute-start.1 = (bf16[16,16,1024]{2,1,0:T(8,128)(2,1)}, bf16[16,16,1024]{2,1,0:T(8,128)(2,1)}, u32[]{:S(2)}, u32[]{:S(2)}) collective-permute-start(bf16[16,16,1024]{2,1,0:T(8,128)(2,1)} %get-tuple-element.787), channel_id=1, source_target_pairs={{0,1},{1,0},{2,3},{3,2},{4,5},{5,4},{6,7},{7,6},{8,9},{9,8},{10,11... | collective-permute-start | bytes 1572872 | tf_op jit(solution)/shard_map/ppermute | solution.py:382
  14.8 67.3 %collective-permute-start.2 = (bf16[16,16,1024]{2,1,0:T(8,128)(2,1)}, bf16[16,16,1024]{2,1,0:T(8,128)(2,1)}, u32[]{:S(2)}, u32[]{:S(2)}) collective-permute-start(bf16[16,16,1024]{2,1,0:T(8,128)(2,1)} %get-tuple-element.786), channel_id=1, source_target_pairs={{0,1},{1,0},{2,3},{3,2},{4,5},{5,4},{6,7},{7,6},{8,9},{9,8},{10,11... | collective-permute-start | bytes 1572872 | tf_op jit(solution)/shard_map/ppermute | solution.py:382
  15.2 68.1 %collective-permute-start.3 = (bf16[16,16,1024]{2,1,0:T(8,128)(2,1)}, bf16[16,16,1024]{2,1,0:T(8,128)(2,1)}, u32[]{:S(2)}, u32[]{:S(2)}) collective-permute-start(bf16[16,16,1024]{2,1,0:T(8,128)(2,1)} %get-tuple-element.785), channel_id=1, source_target_pairs={{0,1},{1,0},{2,3},{3,2},{4,5},{5,4},{6,7},{7,6},{8,9},{9,8},{10,11... | collective-permute-start | bytes 1572872 | tf_op jit(solution)/shard_map/ppermute | solution.py:382
  17.8 54.9 %collective-permute-start.4 = (bf16[16,16,1024]{2,1,0:T(8,128)(2,1)}, bf16[16,16,1024]{2,1,0:T(8,128)(2,1)}, u32[]{:S(2)}, u32[]{:S(2)}) collective-permute-start(bf16[16,16,1024]{2,1,0:T(8,128)(2,1)} %get-tuple-element.780), channel_id=1, source_target_pairs={{0,1},{1,0},{2,3},{3,2},{4,5},{5,4},{6,7},{7,6},{8,9},{9,8},{10,11... | collective-permute-start | bytes 1572872 | tf_op jit(solution)/shard_map/ppermute | solution.py:382
  70.3 14.5 %collective-permute-start.6 = (bf16[16,16,1024]{2,1,0:T(8,128)(2,1)}, bf16[16,16,1024]{2,1,0:T(8,128)(2,1)S(1)}, u32[]{:S(2)}, u32[]{:S(2)}) collective-permute-start(bf16[16,16,1024]{2,1,0:T(8,128)(2,1)} %get-tuple-element.779), channel_id=1, source_target_pairs={{0,1},{1,0},{2,3},{3,2},{4,5},{5,4},{6,7},{7,6},{8,9},{9,8},{10,11... | collective-permute-start | bytes 1572872 | tf_op jit(solution)/shard_map/ppermute | solution.py:382
  72.7 13.4 %collective-permute-start.7 = (bf16[16,16,1024]{2,1,0:T(8,128)(2,1)}, bf16[16,16,1024]{2,1,0:T(8,128)(2,1)S(1)}, u32[]{:S(2)}, u32[]{:S(2)}) collective-permute-start(bf16[16,16,1024]{2,1,0:T(8,128)(2,1)} %get-tuple-element.778), channel_id=1, source_target_pairs={{0,1},{1,0},{2,3},{3,2},{4,5},{5,4},{6,7},{7,6},{8,9},{9,8},{10,11... | collective-permute-start | bytes 1572872 | tf_op jit(solution)/shard_map/ppermute | solution.py:382
  74.2 27.6 %collective-permute-start.5 = (bf16[16,32,1024]{2,1,0:T(8,128)(2,1)S(1)}, bf16[16,32,1024]{2,1,0:T(8,128)(2,1)}, u32[]{:S(2)}, u32[]{:S(2)}) collective-permute-start(bf16[16,32,1024]{2,1,0:T(8,128)(2,1)S(1)} %pad_maximum_fusion.7.rest_2_), channel_id=1, source_target_pairs={{0,2},{1,3},{2,4},{3,5},{8,10},{9,11},{10,12},{11,13},{16,18},{17,... | collective-permute-start | bytes 3145736 | tf_op jit(solution)/shard_map/ppermute | solution.py:382
  101.8 31.7 %collective-permute-start.9 = (bf16[16,32,1024]{2,1,0:T(8,128)(2,1)}, bf16[16,32,1024]{2,1,0:T(8,128)(2,1)}, u32[]{:S(2)}, u32[]{:S(2)}) collective-permute-start(bf16[16,32,1024]{2,1,0:T(8,128)(2,1)} %fusion.24.query), channel_id=1, source_target_pairs={{6,4},{7,5},{14,12},{15,13},{22,20},{23,21},{30,28},{31,29}} | collective-permute-start | bytes 3145736 | tf_op jit(solution)/shard_map/ppermute | solution.py:382
  103.5 30.0 %collective-permute-start.10 = (bf16[16,32,1024]{2,1,0:T(8,128)(2,1)}, bf16[16,32,1024]{2,1,0:T(8,128)(2,1)}, u32[]{:S(2)}, u32[]{:S(2)}) collective-permute-start(bf16[16,32,1024]{2,1,0:T(8,128)(2,1)} %pad_maximum_fusion.3.grad), channel_id=1, source_target_pairs={{6,4},{7,5},{14,12},{15,13},{22,20},{23,21},{30,28},{31,29}} | collective-permute-start | bytes 3145736 | tf_op jit(solution)/shard_map/ppermute | solution.py:382
  105.1 28.4 %collective-permute-start.11 = (bf16[16,32,1024]{2,1,0:T(8,128)(2,1)}, bf16[16,32,1024]{2,1,0:T(8,128)(2,1)}, u32[]{:S(2)}, u32[]{:S(2)}) collective-permute-start(bf16[16,32,1024]{2,1,0:T(8,128)(2,1)} %collective-permute-done.5.rest_1_), channel_id=1, source_target_pairs={{2,4},{3,5},{10,12},{11,13},{18,20},{19,21},{26,28},{27,29}} | collective-permute-start | bytes 3145736 | tf_op jit(solution)/shard_map/ppermute | solution.py:382
  106.8 28.7 %collective-permute-start.12 = (bf16[16,32,1024]{2,1,0:T(8,128)(2,1)}, bf16[16,32,1024]{2,1,0:T(8,128)(2,1)}, u32[]{:S(2)}, u32[]{:S(2)}) collective-permute-start(bf16[16,32,1024]{2,1,0:T(8,128)(2,1)} %pad_maximum_fusion.8.rest_2_), channel_id=1, source_target_pairs={{0,2},{1,3},{2,4},{3,5},{8,10},{9,11},{10,12},{11,13},{16,18},{17,... | collective-permute-start | bytes 3145736 | tf_op jit(solution)/shard_map/ppermute | solution.py:382
  152.4 48.5 %collective-permute-start.15 = (bf16[16,32,1024]{2,1,0:T(8,128)(2,1)}, bf16[16,32,1024]{2,1,0:T(8,128)(2,1)}, u32[]{:S(2)}, u32[]{:S(2)}) collective-permute-start(bf16[16,32,1024]{2,1,0:T(8,128)(2,1)} %fusion.27.query), channel_id=1, source_target_pairs={{6,4},{7,5},{14,12},{15,13},{22,20},{23,21},{30,28},{31,29}} | collective-permute-start | bytes 3145736 | tf_op jit(solution)/shard_map/ppermute | solution.py:382
  154.1 46.9 %collective-permute-start.16 = (bf16[16,32,1024]{2,1,0:T(8,128)(2,1)S(1)}, bf16[16,32,1024]{2,1,0:T(8,128)(2,1)}, u32[]{:S(2)}, u32[]{:S(2)}) collective-permute-start(bf16[16,32,1024]{2,1,0:T(8,128)(2,1)S(1)} %copy-done.5), channel_id=1, source_target_pairs={{6,4},{7,5},{14,12},{15,13},{22,20},{23,21},{30,28},{31,29}} | collective-permute-start | bytes 3145736 | tf_op jit(solution)/shard_map/ppermute | solution.py:382
  155.7 45.3 %collective-permute-start.17 = (bf16[16,32,1024]{2,1,0:T(8,128)(2,1)}, bf16[16,32,1024]{2,1,0:T(8,128)(2,1)}, u32[]{:S(2)}, u32[]{:S(2)}) collective-permute-start(bf16[16,32,1024]{2,1,0:T(8,128)(2,1)} %collective-permute-done.12.rest_1_), channel_id=1, source_target_pairs={{2,4},{3,5},{10,12},{11,13},{18,20},{19,21},{26,28},{27,29}} | collective-permute-start | bytes 3145736 | tf_op jit(solution)/shard_map/ppermute | solution.py:382
  157.4 55.1 %collective-permute-start.18 = (bf16[16,32,1024]{2,1,0:T(8,128)(2,1)}, bf16[16,32,1024]{2,1,0:T(8,128)(2,1)}, u32[]{:S(2)}, u32[]{:S(2)}) collective-permute-start(bf16[16,32,1024]{2,1,0:T(8,128)(2,1)} %pad_maximum_fusion.9.rest_2_), channel_id=1, source_target_pairs={{0,2},{1,3},{2,4},{3,5},{8,10},{9,11},{10,12},{11,13},{16,18},{17,... | collective-permute-start | bytes 3145736 | tf_op jit(solution)/shard_map/ppermute | solution.py:382
  229.4 59.2 %collective-permute-start.24 = (f32[16,3,512]{2,1,0:T(4,128)S(1)}, f32[16,3,512]{2,1,0:T(4,128)S(1)}, u32[]{:S(2)}, u32[]{:S(2)}) collective-permute-start(f32[16,3,512]{2,1,0:T(4,128)S(1)} %get-tuple-element.447), channel_id=1, source_target_pairs={{4,6},{5,7},{6,4},{7,5},{12,14},{13,15},{14,12},{15,13},{20,22},{2... | collective-permute-start | bytes 294920 | tf_op jit(solution)/shard_map/ppermute | solution.py:382
  230.0 58.5 %collective-permute-start.20 = (bf16[16,32,1024]{2,1,0:T(8,128)(2,1)S(1)}, bf16[16,32,1024]{2,1,0:T(8,128)(2,1)S(1)}, u32[]{:S(2)}, u32[]{:S(2)}) collective-permute-start(bf16[16,32,1024]{2,1,0:T(8,128)(2,1)S(1)} %fusion.30.query), channel_id=1, source_target_pairs={{6,4},{7,5},{14,12},{15,13},{22,20},{23,21},{30,28},{31,29}} | collective-permute-start | bytes 3145736 | tf_op jit(solution)/shard_map/ppermute | solution.py:382
  230.8 57.8 %collective-permute-start.21 = (bf16[16,32,1024]{2,1,0:T(8,128)(2,1)S(1)}, bf16[16,32,1024]{2,1,0:T(8,128)(2,1)S(1)}, u32[]{:S(2)}, u32[]{:S(2)}) collective-permute-start(bf16[16,32,1024]{2,1,0:T(8,128)(2,1)S(1)} %pad_maximum_fusion.5.grad), channel_id=1, source_target_pairs={{6,4},{7,5},{14,12},{15,13},{22,20},{23,21},{30,28},{31,29}} | collective-permute-start | bytes 3145736 | tf_op jit(solution)/shard_map/ppermute | solution.py:382
  231.5 57.1 %collective-permute-start.22 = (bf16[16,32,1024]{2,1,0:T(8,128)(2,1)}, bf16[16,32,1024]{2,1,0:T(8,128)(2,1)S(1)}, u32[]{:S(2)}, u32[]{:S(2)}) collective-permute-start(bf16[16,32,1024]{2,1,0:T(8,128)(2,1)} %collective-permute-done.18.rest_1_), channel_id=1, source_target_pairs={{2,4},{3,5},{10,12},{11,13},{18,20},{19,21},{26,28},{27,29}} | collective-permute-start | bytes 3145736 | tf_op jit(solution)/shard_map/ppermute | solution.py:382
  232.3 56.3 %collective-permute-start.23 = (bf16[16,32,1024]{2,1,0:T(8,128)(2,1)S(1)}, bf16[16,32,1024]{2,1,0:T(8,128)(2,1)S(1)}, u32[]{:S(2)}, u32[]{:S(2)}) collective-permute-start(bf16[16,32,1024]{2,1,0:T(8,128)(2,1)S(1)} %copy-done.83), channel_id=1, source_target_pairs={{0,2},{1,3},{2,4},{3,5},{8,10},{9,11},{10,12},{11,13},{16,18},{17,... | collective-permute-start | bytes 3145736 | tf_op jit(solution)/shard_map/ppermute | solution.py:382
  308.2 31.7 %collective-permute-start.25 = (bf16[16,32,2048]{2,0,1:T(8,128)(2,1)}, bf16[16,32,2048]{2,0,1:T(8,128)(2,1)}, u32[]{:S(2)}, u32[]{:S(2)}) collective-permute-start(bf16[16,32,2048]{2,0,1:T(8,128)(2,1)} %copy.160), channel_id=1, source_target_pairs={{4,6},{5,7},{12,14},{13,15},{20,22},{21,23},{28,30},{29,31}} | collective-permute-start | bytes 6291464 | tf_op jit(solution)/shard_map/ppermute | solution.py:382
  312.3 27.6 %collective-permute-start.26 = (bf16[16,32,1024]{2,1,0:T(8,128)(2,1)}, bf16[16,32,1024]{2,1,0:T(8,128)(2,1)S(1)}, u32[]{:S(2)}, u32[]{:S(2)}) collective-permute-start(bf16[16,32,1024]{2,1,0:T(8,128)(2,1)} %fusion.33.query), channel_id=1, source_target_pairs={{6,4},{7,5},{14,12},{15,13},{22,20},{23,21},{30,28},{31,29}} | collective-permute-start | bytes 3145736 | tf_op jit(solution)/shard_map/ppermute | solution.py:382
  313.0 26.9 %collective-permute-start.27 = (bf16[16,32,1024]{2,1,0:T(8,128)(2,1)S(1)}, bf16[16,32,1024]{2,1,0:T(8,128)(2,1)S(1)}, u32[]{:S(2)}, u32[]{:S(2)}) collective-permute-start(bf16[16,32,1024]{2,1,0:T(8,128)(2,1)S(1)} %pad_maximum_fusion.6.grad), channel_id=1, source_target_pairs={{6,4},{7,5},{14,12},{15,13},{22,20},{23,21},{30,28},{31,29}} | collective-permute-start | bytes 3145736 | tf_op jit(solution)/shard_map/ppermute | solution.py:382
  313.8 26.2 %collective-permute-start.28 = (bf16[16,32,1024]{2,1,0:T(8,128)(2,1)}, bf16[16,32,1024]{2,1,0:T(8,128)(2,1)S(1)}, u32[]{:S(2)}, u32[]{:S(2)}) collective-permute-start(bf16[16,32,1024]{2,1,0:T(8,128)(2,1)} %copy-done.95), channel_id=1, source_target_pairs={{2,4},{3,5},{10,12},{11,13},{18,20},{19,21},{26,28},{27,29}} | collective-permute-start | bytes 3145736 | tf_op jit(solution)/shard_map/ppermute | solution.py:382
  315.1 24.9 %collective-permute-start.29 = (bf16[16,32,1024]{2,0,1:T(8,128)(2,1)S(1)}, bf16[16,32,1024]{2,0,1:T(8,128)(2,1)S(1)}, u32[]{:S(2)}, u32[]{:S(2)}) collective-permute-start(bf16[16,32,1024]{2,0,1:T(8,128)(2,1)S(1)} %copy.162), channel_id=1, source_target_pairs={{4,2},{5,3},{12,10},{13,11},{20,18},{21,19},{28,26},{29,27}} | collective-permute-start | bytes 3145736 | tf_op jit(solution)/shard_map/ppermute | solution.py:382
  356.1 51.3 %collective-permute-start.34 = (f32[16,3,512]{2,1,0:T(4,128)S(1)}, f32[16,3,512]{2,1,0:T(4,128)S(1)}, u32[]{:S(2)}, u32[]{:S(2)}) collective-permute-start(f32[16,3,512]{2,1,0:T(4,128)S(1)} %get-tuple-element.531), channel_id=1, source_target_pairs={{4,6},{5,7},{6,4},{7,5},{12,14},{13,15},{14,12},{15,13},{20,22},{2... | collective-permute-start | bytes 294920 | tf_op jit(solution)/shard_map/ppermute | solution.py:382
  359.4 73.7 %collective-permute-start.31 = (bf16[16,32,2048]{2,0,1:T(8,128)(2,1)}, bf16[16,32,2048]{2,0,1:T(8,128)(2,1)S(1)}, u32[]{:S(2)}, u32[]{:S(2)}) collective-permute-start(bf16[16,32,2048]{2,0,1:T(8,128)(2,1)} %copy.164), channel_id=1, source_target_pairs={{4,6},{5,7},{12,14},{13,15},{20,22},{21,23},{28,30},{29,31}} | collective-permute-start | bytes 6291464 | tf_op jit(solution)/shard_map/ppermute | solution.py:382
  362.0 71.0 %collective-permute-start.32 = (bf16[16,32,1024]{2,0,1:T(8,128)(2,1)}, bf16[16,32,1024]{2,0,1:T(8,128)(2,1)}, u32[]{:S(2)}, u32[]{:S(2)}) collective-permute-start(bf16[16,32,1024]{2,0,1:T(8,128)(2,1)} %add_convert_fusion.17), channel_id=1, source_target_pairs={{2,0},{3,1},{4,2},{5,3},{10,8},{11,9},{12,10},{13,11},{18,16},{19,... | collective-permute-start | bytes 3145736 | tf_op jit(solution)/shard_map/ppermute | solution.py:382
  365.0 68.0 %collective-permute-start.33 = (bf16[16,32,1024]{2,0,1:T(8,128)(2,1)}, bf16[16,32,1024]{2,0,1:T(8,128)(2,1)S(1)}, u32[]{:S(2)}, u32[]{:S(2)}) collective-permute-start(bf16[16,32,1024]{2,0,1:T(8,128)(2,1)} %copy.168), channel_id=1, source_target_pairs={{4,2},{5,3},{12,10},{13,11},{20,18},{21,19},{28,26},{29,27}} | collective-permute-start | bytes 3145736 | tf_op jit(solution)/shard_map/ppermute | solution.py:382
  370.9 36.5 %collective-permute-start.35 = (bf16[16,16,1024]{2,0,1:T(8,128)(2,1)}, bf16[16,16,1024]{2,0,1:T(8,128)(2,1)S(1)}, u32[]{:S(2)}, u32[]{:S(2)}) collective-permute-start(bf16[16,16,1024]{2,0,1:T(8,128)(2,1)} %slice.245), channel_id=1, source_target_pairs={{0,1},{1,0},{2,3},{3,2},{4,5},{5,4},{6,7},{7,6},{8,9},{9,8},{10,11... | collective-permute-start | bytes 1572872 | tf_op jit(solution)/shard_map/ppermute | solution.py:382
  437.0 66.2 %collective-permute-start.36 = (bf16[16,32,2048]{2,0,1:T(8,128)(2,1)}, bf16[16,32,2048]{2,0,1:T(8,128)(2,1)S(1)}, u32[]{:S(2)}, u32[]{:S(2)}) collective-permute-start(bf16[16,32,2048]{2,0,1:T(8,128)(2,1)} %copy.171), channel_id=1, source_target_pairs={{4,6},{5,7},{12,14},{13,15},{20,22},{21,23},{28,30},{29,31}} | collective-permute-start | bytes 6291464 | tf_op jit(solution)/shard_map/ppermute | solution.py:382
  442.6 47.6 %collective-permute-start.37 = (bf16[16,16,1024]{2,0,1:T(8,128)(2,1)}, bf16[16,16,1024]{2,0,1:T(8,128)(2,1)S(1)}, u32[]{:S(2)}, u32[]{:S(2)}) collective-permute-start(bf16[16,16,1024]{2,0,1:T(8,128)(2,1)} %get-tuple-element.803), channel_id=1, source_target_pairs={{0,1},{1,0},{2,3},{3,2},{4,5},{5,4},{6,7},{7,6},{8,9},{9,8},{10,11... | collective-permute-start | bytes 1572872 | tf_op jit(solution)/shard_map/ppermute | solution.py:382
  445.8 57.4 %collective-permute-start.38 = (bf16[16,32,1024]{2,0,1:T(8,128)(2,1)}, bf16[16,32,1024]{2,0,1:T(8,128)(2,1)}, u32[]{:S(2)}, u32[]{:S(2)}) collective-permute-start(bf16[16,32,1024]{2,0,1:T(8,128)(2,1)} %add_convert_fusion.13), channel_id=1, source_target_pairs={{2,0},{3,1},{4,2},{5,3},{10,8},{11,9},{12,10},{13,11},{18,16},{19,... | collective-permute-start | bytes 3145736 | tf_op jit(solution)/shard_map/ppermute | solution.py:382
  448.6 54.5 %collective-permute-start.39 = (bf16[16,32,1024]{2,0,1:T(8,128)(2,1)}, bf16[16,32,1024]{2,0,1:T(8,128)(2,1)S(1)}, u32[]{:S(2)}, u32[]{:S(2)}) collective-permute-start(bf16[16,32,1024]{2,0,1:T(8,128)(2,1)} %copy.179), channel_id=1, source_target_pairs={{4,2},{5,3},{12,10},{13,11},{20,18},{21,19},{28,26},{29,27}} | collective-permute-start | bytes 3145736 | tf_op jit(solution)/shard_map/ppermute | solution.py:382
  452.0 38.2 %collective-permute-start.40 = (bf16[16,16,1024]{2,0,1:T(8,128)(2,1)S(1)}, bf16[16,16,1024]{2,0,1:T(8,128)(2,1)S(1)}, u32[]{:S(2)}, u32[]{:S(2)}) collective-permute-start(bf16[16,16,1024]{2,0,1:T(8,128)(2,1)S(1)} %slice.248), channel_id=1, source_target_pairs={{0,1},{1,0},{2,3},{3,2},{4,5},{5,4},{6,7},{7,6},{8,9},{9,8},{10,11... | collective-permute-start | bytes 1572872 | tf_op jit(solution)/shard_map/ppermute | solution.py:382
  505.7 66.2 %collective-permute-start.41 = (bf16[16,32,2048]{2,0,1:T(8,128)(2,1)}, bf16[16,32,2048]{2,0,1:T(8,128)(2,1)}, u32[]{:S(2)}, u32[]{:S(2)}) collective-permute-start(bf16[16,32,2048]{2,0,1:T(8,128)(2,1)} %copy.182), channel_id=1, source_target_pairs={{4,6},{5,7},{12,14},{13,15},{20,22},{21,23},{28,30},{29,31}} | collective-permute-start | bytes 6291464 | tf_op jit(solution)/shard_map/ppermute | solution.py:382
  512.4 59.5 %collective-permute-start.42 = (bf16[16,16,1024]{2,0,1:T(8,128)(2,1)}, bf16[16,16,1024]{2,0,1:T(8,128)(2,1)}, u32[]{:S(2)}, u32[]{:S(2)}) collective-permute-start(bf16[16,16,1024]{2,0,1:T(8,128)(2,1)} %get-tuple-element.801), channel_id=1, source_target_pairs={{0,1},{1,0},{2,3},{3,2},{4,5},{5,4},{6,7},{7,6},{8,9},{9,8},{10,11... | collective-permute-start | bytes 1572872 | tf_op jit(solution)/shard_map/ppermute | solution.py:382
  514.1 57.7 %collective-permute-start.43 = (bf16[16,32,1024]{2,0,1:T(8,128)(2,1)}, bf16[16,32,1024]{2,0,1:T(8,128)(2,1)}, u32[]{:S(2)}, u32[]{:S(2)}) collective-permute-start(bf16[16,32,1024]{2,0,1:T(8,128)(2,1)} %add_convert_fusion.9), channel_id=1, source_target_pairs={{2,0},{3,1},{4,2},{5,3},{10,8},{11,9},{12,10},{13,11},{18,16},{19,... | collective-permute-start | bytes 3145736 | tf_op jit(solution)/shard_map/ppermute | solution.py:382
  517.0 54.9 %collective-permute-start.44 = (bf16[16,32,1024]{2,0,1:T(8,128)(2,1)}, bf16[16,32,1024]{2,0,1:T(8,128)(2,1)}, u32[]{:S(2)}, u32[]{:S(2)}) collective-permute-start(bf16[16,32,1024]{2,0,1:T(8,128)(2,1)} %copy.189), channel_id=1, source_target_pairs={{4,2},{5,3},{12,10},{13,11},{20,18},{21,19},{28,26},{29,27}} | collective-permute-start | bytes 3145736 | tf_op jit(solution)/shard_map/ppermute | solution.py:382
  526.5 20.0 %collective-permute-start.45 = (f32[64,3,8,16]{0,3,2,1:T(8,128)}, f32[64,3,8,16]{0,3,2,1:T(8,128)S(1)}, u32[]{:S(2)}, u32[]{:S(2)}) collective-permute-start(f32[64,3,8,16]{0,3,2,1:T(8,128)} %copy.192), channel_id=1, source_target_pairs={{0,1},{1,0},{2,3},{3,2},{4,5},{5,4},{6,7},{7,6},{8,9},{9,8},{10,11... | collective-permute-start | bytes 294920 | tf_op jit(solution)/shard_map/ppermute | solution.py:382
  546.5 25.3 %collective-permute-start.46 = (bf16[16,16,1024]{2,0,1:T(8,128)(2,1)}, bf16[16,16,1024]{2,0,1:T(8,128)(2,1)S(1)}, u32[]{:S(2)}, u32[]{:S(2)}) collective-permute-start(bf16[16,16,1024]{2,0,1:T(8,128)(2,1)} %slice.253), channel_id=1, source_target_pairs={{0,1},{1,0},{2,3},{3,2},{4,5},{5,4},{6,7},{7,6},{8,9},{9,8},{10,11... | collective-permute-start | bytes 1572872 | tf_op jit(solution)/shard_map/ppermute | solution.py:382
  578.1 39.5 %collective-permute-start.47 = (bf16[16,16,1024]{2,0,1:T(8,128)(2,1)S(1)}, bf16[16,16,1024]{2,0,1:T(8,128)(2,1)S(1)}, u32[]{:S(2)}, u32[]{:S(2)}) collective-permute-start(bf16[16,16,1024]{2,0,1:T(8,128)(2,1)S(1)} %get-tuple-element.799), channel_id=1, source_target_pairs={{0,1},{1,0},{2,3},{3,2},{4,5},{5,4},{6,7},{7,6},{8,9},{9,8},{10,11... | collective-permute-start | bytes 1572872 | tf_op jit(solution)/shard_map/ppermute | solution.py:382
  580.4 52.2 %collective-permute-start.48 = (bf16[16,32,1024]{2,0,1:T(8,128)(2,1)S(1)}, bf16[16,32,1024]{2,0,1:T(8,128)(2,1)S(1)}, u32[]{:S(2)}, u32[]{:S(2)}) collective-permute-start(bf16[16,32,1024]{2,0,1:T(8,128)(2,1)S(1)} %add_convert_fusion.5), channel_id=1, source_target_pairs={{2,0},{3,1},{4,2},{5,3},{10,8},{11,9},{12,10},{13,11},{18,16},{19,... | collective-permute-start | bytes 3145736 | tf_op jit(solution)/shard_map/ppermute | solution.py:382
  586.2 31.3 %collective-permute-start.49 = (bf16[16,16,1024]{2,0,1:T(8,128)(2,1)S(1)}, bf16[16,16,1024]{2,0,1:T(8,128)(2,1)S(1)}, u32[]{:S(2)}, u32[]{:S(2)}) collective-permute-start(bf16[16,16,1024]{2,0,1:T(8,128)(2,1)S(1)} %slice.256), channel_id=1, source_target_pairs={{0,1},{1,0},{2,3},{3,2},{4,5},{5,4},{6,7},{7,6},{8,9},{9,8},{10,11... | collective-permute-start | bytes 1572872 | tf_op jit(solution)/shard_map/ppermute | solution.py:382
  654.7 6.9 collective-permute-start.52
  665.7 82.9 %reduce-scatter.5.cloned.1.call-start = ((), (), s32[]{:S(2)}) async-start(), calls=%async_computation.3 | async-start | bytes 983040 | tf_op jit(solution)/shard_map/reduce_scatter | solution.py:548
  (116 other events, 2053.0 us)
Sparse Core Ops, SparseCore 0:
  665.8 57.1 reduce-scatter.2
  725.3 23.2 reduce-scatter.4

commit v3 on v2

--- a/solution.py
+++ b/solution.py
@@ -143,7 +143,7 @@
 
 
 def col_stats_kernel(
-    packed, stride, scalars, key_rows, query_rows, query, guest, grad, guest_grad, weight, *rest
+    packed, stride, scalars, key_rows, query_rows, query, guest, grad, key_weight, value_weight, *rest
 ):
     *held, stats, crossed, kv, inputs = rest
     count = 2 * query.shape[1]
@@ -152,9 +152,10 @@
         inputs[:, b * half : (b + 1) * half, :] = item[...]
     columns, keys, width = inputs.shape
     flat = inputs[...].reshape(columns * keys, width)
-    for at in range(0, 2 * width, TILE):
-        part = dot(flat, weight[:, at : at + TILE], NN).astype(kv.dtype)
-        kv[:, :, at : at + TILE] = part.reshape(columns, keys, TILE)
+    for j, weight in enumerate((key_weight, value_weight)):
+        for at in range(0, width, TILE):
+            part = dot(flat, weight[0, :, at : at + TILE], NN).astype(kv.dtype)
+            kv[:, :, j * width + at : j * width + at + TILE] = part.reshape(columns, keys, TILE)
     for i in range(kv.shape[0]):
         column = scalars[1] + pl.program_id(0) * kv.shape[0] + i
         mask = col_mask(scalars, key_rows, query_rows, column, stride)
@@ -169,8 +170,8 @@
                     pieces.append(item[:, h * count : h * count + half])
                 crossed[i, j : j + 1, lanes] = jnp.concatenate(pieces, axis=1)
 
-        query_v = jnp.concatenate([query[i], guest[i]], axis=0)
-        grad_v = jnp.concatenate([grad[i], guest_grad[i]], axis=0)
+        query_v = jnp.concatenate([query[i], guest[i, :, :width]], axis=0)
+        grad_v = jnp.concatenate([grad[i], guest[i, :, width:]], axis=0)
         part_stats(query_v, *halves(kv, i), grad_v, mask, packed, store)
 
 
@@ -186,7 +187,7 @@
 
 def col_grads_kernel(
     packed, stride, scalars, key_rows, query_rows, row_part, own_part, other_part,
-    query, guest, kv, grad, guest_grad, weight,
+    query, guest, kv, grad, key_weight, value_weight,
     final, mixed, g_query, back, g_kv, *terms,
 ):
     half = query.shape[1]
@@ -216,14 +217,16 @@
             g_kv[i, :, lanes] = key_v.astype(g_kv.dtype)
             g_kv[i, :, second] = value_v.astype(g_kv.dtype)
 
-        query_v = jnp.concatenate([query[i], guest[i]], axis=0)
-        grad_v = jnp.concatenate([grad[i], guest_grad[i]], axis=0)
+        query_v = jnp.concatenate([query[i], guest[i, :, :width]], axis=0)
+        grad_v = jnp.concatenate([grad[i], guest[i, :, width:]], axis=0)
         part_grads(query_v, *halves(kv, i), grad_v, mask, packed, load, store)
 
     columns, keys, _ = g_kv.shape
     flat = g_kv[...].reshape(columns * keys, 2 * width)
     for at in range(0, width, TILE):
-        part = dot(flat, weight[:, at : at + TILE], NN).astype(g_kv.dtype).reshape(columns, keys, TILE)
+        part = dot(flat[:, :width], key_weight[0, at : at + TILE, :], NT)
+        part = part + dot(flat[:, width:], value_weight[0, at : at + TILE, :], NT)
+        part = part.astype(g_kv.dtype).reshape(columns, keys, TILE)
         for b, term in enumerate(terms):
             term[:, :, at : at + TILE] = part[:, b * half : (b + 1) * half]
 
@@ -289,7 +292,12 @@
     return half, packed, columns, math.gcd(columns, COL_STEP), width
 
 
-def col_stats(scalars, key_rows, query_rows, query, guest, grad, guest_grad, weight, held, stride):
+def weights_of(weight):
+    one = (1,) + weight.shape[1:]
+    return [pl.BlockSpec(one, lambda s, j=j: (j, 0, 0)) for j in (1, 2)]
+
+
+def col_stats(scalars, key_rows, query_rows, query, guest, grad, weight, held, stride):
     half, packed, columns, step, width = col_sizes(query)
     keys = half * len(held)
     own = block((step, half, width))
@@ -301,18 +309,19 @@
         functools.partial(col_stats_kernel, packed, stride),
         columns // step,
         [SCALARS, whole(key_rows.shape), whole(query_rows.shape)]
-        + [own, own, own, own, whole(weight.shape)]
+        + [own, block((step, half, 2 * width)), own]
+        + weights_of(weight)
         + [own] * len(held),
         [stat, stat, block((step, keys, 2 * width)), block((step, keys, width))],
         [shape, shape, large, joined],
         4 * columns * keys * width * (2 * half * 4 + width),
-        (scalars, key_rows, query_rows, query, guest, grad, guest_grad, weight, *held),
+        (scalars, key_rows, query_rows, query, guest, grad, weight, weight, *held),
     )
 
 
 def col_grads(
     scalars, key_rows, query_rows, row_part, own_part, other_part,
-    query, guest, kv, grad, guest_grad, weight, offset, stride,
+    query, guest, kv, grad, weight, offset, stride,
 ):
     half, packed, columns, step, width = col_sizes(query)
     keys = kv.shape[1]
@@ -330,12 +339,13 @@
         functools.partial(col_grads_kernel, packed, stride),
         columns // step,
         [SCALARS, whole(key_rows.shape), whole(query_rows.shape), stat_off, stat, stat]
-        + [own, own, pair, own, own, whole(weight.shape)],
+        + [own, both, pair, own]
+        + weights_of(weight),
         [stat, own, own, both, pair] + [own] * blocks,
         [shape, small, small, twice, large] + [small] * blocks,
         4 * columns * keys * width * (6 * half * 4 + width),
         (scalars, key_rows, query_rows, row_part, own_part, other_part)
-        + (query, guest, kv, grad, guest_grad, weight),
+        + (query, guest, kv, grad, weight, weight),
     )
 
 
@@ -365,9 +375,7 @@
     chip_rows = 2 * row_local
     group = half_cols // GROUPS
     w_q = w_qkv[0]
-    w_kv = jnp.concatenate([w_qkv[1], w_qkv[2]], axis=1)
-    w_all = jnp.concatenate([w_q, w_kv], axis=1)
-    w_kv_t = jnp.concatenate([w_qkv[1].T, w_qkv[2].T], axis=0)
+    w_all = jnp.concatenate([w_qkv[0], w_qkv[1], w_qkv[2]], axis=1)
 
     def pairs(links):
         return [(2 * a + c, 2 * b + c) for a, b in links for c in (0, 1)]
@@ -430,7 +438,7 @@
     live["held"] = [[tokens_c[g]] for g in range(GROUPS)]
     row_scalars = jnp.stack([limit, seq_index * row_local]).astype(jnp.int32)
     cross = guest_up + guest_down
-    names = ("guest", "guest_grad", "kv", "own", "other", "final", "mixed", "query", "terms")
+    names = ("guest", "kv", "own", "other", "final", "mixed", "query", "terms")
     names += ("back", "moving", "swapped", "w_parts", "query_c")
     live.update({name: [None] * GROUPS for name in names})
 
@@ -443,18 +451,14 @@
         if s == max(hops - 2, 0):
             live["query_c"][g] = narrow(product(live["tokens_c"][g], w_q))
         if s == hops - 1:
-            query, grad = live["query_c"][g], live["grad_c"][g]
-            if g > 0:
-                query, grad, live["crossed"] = lax.optimization_barrier((query, grad, live["crossed"]))
-            live["guest"][g] = send(query, guest_down)
-            live["guest_grad"][g] = send(grad, guest_down)
+            visit = jnp.concatenate([live["query_c"][g], live["grad_c"][g]], axis=2)
+            live["guest"][g] = send(visit, guest_down)
         if s == hops:
             live["own"][g], crossed, live["kv"][g], live["held"][g] = col_stats(
                 scalars_of(g), key_rows, query_rows,
-                live["query_c"][g], live["guest"][g], live["grad_c"][g], live["guest_grad"][g],
-                w_kv, live["held"][g][::-1], columns
+                live["query_c"][g], live["guest"][g], live["grad_c"][g],
+                w_qkv, live["held"][g][::-1], columns
             )
-            live["crossed"] = crossed
             live["other"][g] = send(crossed, cross)
         if s == hops + 1:
             row_part = live["row_part"]
@@ -463,14 +467,12 @@
             final, mixed, g_query, back, g_kv, *terms = col_grads(
                 scalars_of(g), key_rows, query_rows, row_part, live["own"][g], live["other"][g],
                 live["query_c"][g], live["guest"][g], live["kv"][g], live["grad_c"][g],
-                live["guest_grad"][g], w_kv_t, g * group, columns
+                w_qkv, g * group, columns
             )
             live["final"][g], live["mixed"][g], live["query"][g] = final, mixed, g_query
             live["kv"][g], live["back"][g], live["terms"][g] = g_kv, back, terms
         if s == hops + 2:
             back = live["back"][g]
-            if g + 2 < GROUPS:
-                back, live["crossed"] = lax.optimization_barrier((back, live["crossed"]))
             live["back"][g] = send(back, guest_up)
         if s == hops + 3:
             back = live["back"][g]

time: 765 us -> 705 us (0.922)
  waiting for transfers between devices: 117 us -> 70.7 us
    ppermute x54 -> x50, waiting for transfers between devices: 79.9 us -> 35.8 us  [send(): return lax.ppermute(values, 'seq', perm)]
    optimization_barrier x7 -> x9, local copies, waits for them, and re-layouts: 10.4 us -> 17.3 us  [body(): live = lax.optimization_barrier(live)]
    ppermute x54 -> x50, starting transfers between devices: 115 us -> 108 us  [send(): return lax.ppermute(values, 'seq', perm)]
    unnamed x241 -> x244, local copies, waits for them, and re-layouts: 37.5 us -> 39.3 us
  transfers between devices with their start and end apart: 56 -> 52, of which waited for: 10 -> 6; matrix products, arithmetic and copies ran while one was open for 35% -> 35% of each run, Pallas kernels for 16% -> 27%
where the time goes in v3:
time: 705 us; the launch traced here: 698 us
  Pallas kernels  188 us (27%)
  matrix products  144 us (20%)
  starting transfers between devices  108 us (15%)
  local copies, waits for them, and re-layouts  103 us (15%)
  waiting for transfers between devices  70.7 us (10%)
  other arithmetic  67.7 us (10%)
  between operations  16.6 us (2%)
    pallas_call x10, Pallas kernels, call(): pl.pallas_call(kernel, grid=(steps,), in_specs=in_specs, out_specs=out_sp...  188 us
    ppermute x50, starting transfers between devices, send(): return lax.ppermute(values, 'seq', perm)  108 us
    dot_general x9, matrix products, weight_product(): jnp.einsum('abd,abf->df', values, grads, preferred_element_type=jnp.float32)  73.7 us
    unnamed x244, local copies, waits for them, and re-layouts  39.3 us
    convert_element_type x9, other arithmetic, narrow(): return values.astype(jnp.bfloat16)  37.9 us
    dot_general x5, matrix products, product_t(): jnp.einsum('...f,df->...d', values, weight, preferred_element_type=jnp.fl...  37.2 us
    ppermute x50, waiting for transfers between devices, send(): return lax.ppermute(values, 'seq', perm)  35.8 us
    dot_general x5, matrix products, product(): jnp.einsum('...d,df->...f', values, weight, preferred_element_type=jnp.fl...  33.5 us
  transfers between devices with their start and end apart: 52, of which 6 were waited for; matrix products, arithmetic and copies ran while one was open for 35% of the time, Pallas kernels for 27%

profile of v3, /device:TPU:0, one launch (start us, length us, event | category | flops | bytes accessed | tf_op | source)
XLA Modules:
  0.0 698.1 jit_solution(5784047197270543139)
XLA Ops:
  7.2 4.5 constant_dynamic-slice_fusion.3
  20.8 2.9 slice_bitcast_fusion.2
  23.6 19.6 %convert_bitcast_fusion.qkv = bf16[16,128,3072]{2,1,0:T(8,128)(2,1)} fusion(bf16[1024,1024]{1,0:T(8,128)(2,1)} %get-tuple-element.727, bf16[1024,1024]{1,0:T(8,128)(2,1)} %get-tuple-element.728, bf16[1024,1024]{1,0:T(8,128)(2,1)} %get-tuple-element.726, bf16[1,16,128,1024]{3,2,1,0:T(8,128)(2,1)} %param.4), kind=kOutput, calls=%fused_computation | convolution fusion | flops 12910067712 | bytes 23068672 | tf_op jit(solution)/shard_map/...d,df->...f/dot_general | solution.py:353
  48.3 4.6 collective-permute-start.5
  60.5 2.8 fusion.24.query
  63.3 12.5 %collective-permute-done.5.rest_1_ = bf16[16,32,1024]{2,1,0:T(8,128)(2,1)S(1)} collective-permute-done((bf16[16,32,1024]{2,1,0:T(8,128)(2,1)S(1)}, bf16[16,32,1024]{2,1,0:T(8,128)(2,1)S(1)}, u32[]{:S(2)}, u32[]{:S(2)}) %collective-permute-start.5) | collective-permute-done | bytes 1048608 | tf_op jit(solution)/shard_map/ppermute | solution.py:390
  82.7 7.6 %collective-permute-start.11 = (bf16[16,32,1024]{2,1,0:T(8,128)(2,1)}, bf16[16,32,1024]{2,1,0:T(8,128)(2,1)}, u32[]{:S(2)}, u32[]{:S(2)}) collective-permute-start(bf16[16,32,1024]{2,1,0:T(8,128)(2,1)} %pad_maximum_fusion.10.rest_2_), channel_id=1, source_target_pairs={{0,2},{1,3},{2,4},{3,5},{8,10},{9,11},{10,12},{11,13},{16,18},{17,... | collective-permute-start | bytes 3145736 | tf_op jit(solution)/shard_map/ppermute | solution.py:390
  92.5 8.9 %shard_map.67 = f32[16,3,1024]{2,1,0:T(4,128)S(1)} custom-call(s32[2]{0:T(128)S(1)} %get-tuple-element.789.scalars, bf16[16,128,3072]{2,1,0:T(8,128)(2,1)} %convert_bitcast_fusion.qkv, bf16[16,128,1024]{2,1,0:T(8,128)(2,1)S(1)} %bitcast.183), custom_call_target="tpu_custom_call" | custom-call | flops 4294967296 | bytes 4294967 | tf_op jit(solution)/shard_map/pallas_call | solution.py:235
  105.6 4.1 fusion.27.query
  120.9 33.0 %collective-permute-start.16 = (bf16[16,32,1024]{2,1,0:T(8,128)(2,1)}, bf16[16,32,1024]{2,1,0:T(8,128)(2,1)S(1)}, u32[]{:S(2)}, u32[]{:S(2)}) collective-permute-start(bf16[16,32,1024]{2,1,0:T(8,128)(2,1)} %pad_maximum_fusion.11.rest_2_), channel_id=1, source_target_pairs={{0,2},{1,3},{2,4},{3,5},{8,10},{9,11},{10,12},{11,13},{16,18},{17,... | collective-permute-start | bytes 3145736 | tf_op jit(solution)/shard_map/ppermute | solution.py:390
  158.9 15.7 %shard_map.68 = (f32[16,3,512]{2,1,0:T(4,128)S(1)}, f32[16,3,512]{2,1,0:T(4,128)S(1)}, bf16[16,96,2048]{2,1,0:T(8,128)(2,1)}, bf16[16,96,1024]{2,1,0:T(8,128)(2,1)}) custom-call(s32[2]{0:T(128)S(1)} %get-tuple-element.788.scalars, s32[96,128]{1,0:T(8,128)S(1)} %broadcast_in_dim.29.key_rows, s32[8,256]{1,0:T(8,128)S(1)} %broadcast_in_dim.32.query_rows, ...), custom_call_target="tpu_custom_call" | custom-call | flops 8053063680 | bytes 8053063 | tf_op jit(solution)/shard_map/pallas_call | solution.py:235
  175.4 2.8 fusion.30.query
  181.7 16.0 %shard_map.69 = (f32[16,3,512]{2,1,0:T(4,128)S(1)}, f32[16,3,512]{2,1,0:T(4,128)S(1)}, bf16[16,96,2048]{2,1,0:T(8,128)(2,1)}, bf16[16,96,1024]{2,1,0:T(8,128)(2,1)}) custom-call(s32[2]{0:T(128)S(1)} %pad_add_fusion.4.scalars, s32[96,128]{1,0:T(8,128)S(1)} %broadcast_in_dim.29.key_rows, s32[8,256]{1,0:T(8,128)S(1)} %broadcast_in_dim.32.query_rows, ...), custom_call_target="tpu_custom_call" | custom-call | flops 8053063680 | bytes 8053063 | tf_op jit(solution)/shard_map/pallas_call | solution.py:235
  198.7 23.8 %collective-permute-start.20 = (bf16[16,32,1024]{2,1,0:T(8,128)(2,1)S(1)}, bf16[16,32,1024]{2,1,0:T(8,128)(2,1)S(1)}, u32[]{:S(2)}, u32[]{:S(2)}) collective-permute-start(bf16[16,32,1024]{2,1,0:T(8,128)(2,1)S(1)} %copy-done.8), channel_id=1, source_target_pairs={{0,2},{1,3},{2,4},{3,5},{8,10},{9,11},{10,12},{11,13},{16,18},{17,... | collective-permute-start | bytes 3145736 | tf_op jit(solution)/shard_map/ppermute | solution.py:390
  223.2 22.6 %shard_map.70 = (f32[16,3,512]{2,1,0:T(4,128)S(1)}, bf16[16,32,1024]{2,1,0:T(8,128)(2,1)S(1)}, bf16[16,32,1024]{2,1,0:T(8,128)(2,1)S(1)}, bf16[16,32,2048]{2,1,0...) custom-call(s32[2]{0:T(128)S(1)} %get-tuple-element.788.scalars, ...), custom_call_target="tpu_custom_call" | custom-call | flops 11274289152 | bytes 11274289 | tf_op jit(solution)/shard_map/pallas_call | solution.py:235
  246.8 4.0 fusion.33.query
  264.0 15.7 %shard_map.71 = (f32[16,3,512]{2,1,0:T(4,128)S(1)}, f32[16,3,512]{2,1,0:T(4,128)S(1)}, bf16[16,96,2048]{2,1,0:T(8,128)(2,1)}, bf16[16,96,1024]{2,1,0:T(8,128)(2,1)}) custom-call(s32[2]{0:T(128)S(1)} %pad_add_fusion.5.scalars, s32[96,128]{1,0:T(8,128)S(1)} %broadcast_in_dim.29.key_rows, s32[8,256]{1,0:T(8,128)S(1)} %broadcast_in_dim.32.query_rows, ...), custom_call_target="tpu_custom_call" | custom-call | flops 8053063680 | bytes 8053063 | tf_op jit(solution)/shard_map/pallas_call | solution.py:235
  282.8 22.8 %shard_map.72 = (f32[16,3,512]{2,1,0:T(4,128)S(1)}, bf16[16,32,1024]{2,1,0:T(8,128)(2,1)S(1)}, bf16[16,32,1024]{2,1,0:T(8,128)(2,1)S(1)}, bf16[16,32,2048]{2,1,0...) custom-call(s32[2]{0:T(128)S(1)} %pad_add_fusion.4.scalars, ...), custom_call_target="tpu_custom_call" | custom-call | flops 11274289152 | bytes 11274289 | tf_op jit(solution)/shard_map/pallas_call | solution.py:235
  306.7 4.2 copy.124
  319.3 15.7 %shard_map.73 = (f32[16,3,512]{2,1,0:T(4,128)S(1)}, f32[16,3,512]{2,1,0:T(4,128)S(1)}, bf16[16,96,2048]{2,1,0:T(8,128)(2,1)}, bf16[16,96,1024]{2,1,0:T(8,128)(2,1)}) custom-call(s32[2]{0:T(128)S(1)} %pad_add_fusion.6.scalars, s32[96,128]{1,0:T(8,128)S(1)} %broadcast_in_dim.29.key_rows, s32[8,256]{1,0:T(8,128)S(1)} %broadcast_in_dim.32.query_rows, ...), custom_call_target="tpu_custom_call" | custom-call | flops 8053063680 | bytes 8053063 | tf_op jit(solution)/shard_map/pallas_call | solution.py:235
  335.8 3.1 add_convert_fusion.16
  339.9 11.6 %bitcast_convert_fusion.3 = bf16[1024,2048]{1,0:T(8,128)(2,1)} fusion(bf16[16,96,1024]{2,1,0:T(8,128)(2,1)S(1)} %copy-done.103, bf16[16,96,2048]{2,1,0:T(8,128)(2,1)} %get-tuple-element.520), kind=kOutput, calls=%fused_computation.8 | convolution fusion | flops 6444548096 | bytes 13631488 | tf_op jit(solution)/shard_map/abd,abf->df/dot_general | solution.py:361
  351.8 22.8 %shard_map.74 = (f32[16,3,512]{2,1,0:T(4,128)S(1)}, bf16[16,32,1024]{2,1,0:T(8,128)(2,1)S(1)}, bf16[16,32,1024]{2,1,0:T(8,128)(2,1)S(1)}, bf16[16,32,2048]{2,1,0...) custom-call(s32[2]{0:T(128)S(1)} %pad_add_fusion.5.scalars, ...), custom_call_target="tpu_custom_call" | custom-call | flops 11274289152 | bytes 11274289 | tf_op jit(solution)/shard_map/pallas_call | solution.py:235
  374.7 2.8 bitcast_convert_fusion.7
  380.9 3.6 add_convert_fusion.14
  386.1 3.0 add_convert_fusion.13
  393.9 4.0 add_convert_fusion.12
  398.8 8.8 %bitcast_convert_fusion.2 = bf16[1024,2048]{1,0:T(8,128)(2,1)} fusion(bf16[16,96,1024]{2,1,0:T(8,128)(2,1)S(1)} %copy-done.102, bf16[16,96,2048]{2,1,0:T(8,128)(2,1)S(1)} %bitcast.203), kind=kOutput, calls=%fused_computation.7 | convolution fusion | flops 6444548096 | bytes 13631488 | tf_op jit(solution)/shard_map/abd,abf->df/dot_general | solution.py:361
  407.9 23.1 %shard_map.75 = (f32[16,3,512]{2,1,0:T(4,128)S(1)}, bf16[16,32,1024]{2,1,0:T(8,128)(2,1)S(1)}, bf16[16,32,1024]{2,1,0:T(8,128)(2,1)S(1)}, bf16[16,32,2048]{2,1,0...) custom-call(s32[2]{0:T(128)S(1)} %pad_add_fusion.6.scalars, ...), custom_call_target="tpu_custom_call" | custom-call | flops 11274289152 | bytes 11274289 | tf_op jit(solution)/shard_map/pallas_call | solution.py:235
  431.0 4.9 bitcast_convert_fusion.6
  440.5 3.5 add_convert_fusion.10
  445.6 2.9 add_convert_fusion.9
  454.4 2.8 fusion.72
  459.3 11.5 %bitcast_convert_fusion.1 = bf16[1024,2048]{1,0:T(8,128)(2,1)} fusion(bf16[16,96,1024]{2,1,0:T(8,128)(2,1)} %get-tuple-element.602, bf16[16,96,2048]{2,1,0:T(8,128)(2,1)} %get-tuple-element.604), kind=kOutput, calls=%fused_computation.6 | convolution fusion | flops 6444548096 | bytes 13631488 | tf_op jit(solution)/shard_map/abd,abf->df/dot_general | solution.py:361
  473.3 2.9 bitcast_convert_fusion.5
  482.8 24.8 %shard_map.76 = (bf16[16,128,1024]{2,1,0:T(8,128)(2,1)S(1)}, bf16[16,128,3072]{2,1,0:T(8,128)(2,1)}) custom-call(s32[2]{0:T(128)S(1)} %copy-done.38, f32[16,3,1024]{2,1,0:T(4,128)S(1)} %reshape.78.stats, bf16[16,128,3072]{2,1,0:T(8,128)(2,1)} %convert_bitcast_fusion.qkv, bf16[16,128,1024]{2,1,0:T(8,128)(2,1)} %bitcast.182), custom_call_target="tpu_custom_call" | custom-call | flops 12884901888 | bytes 12884901 | tf_op jit(solution)/shard_map/pallas_call | solution.py:235
  507.7 4.9 add_convert_fusion.6
  517.1 3.1 add_convert_fusion.4
  520.9 12.2 %bitcast_convert_fusion = bf16[1024,2048]{1,0:T(8,128)(2,1)} fusion(bf16[16,96,1024]{2,1,0:T(8,128)(2,1)S(1)} %copy-done.101, bf16[16,96,2048]{2,1,0:T(8,128)(2,1)} %get-tuple-element.637), kind=kOutput, calls=%fused_computation.5 | convolution fusion | flops 6444548096 | bytes 13631488 | tf_op jit(solution)/shard_map/abd,abf->df/dot_general | solution.py:361
  533.2 16.0 %convolution_bitcast_fusion = f32[1024,3072]{1,0:T(8,128)} fusion(bf16[16,128,1024]{2,1,0:T(8,128)(2,1)S(1)} %bitcast.196, bf16[16,128,3072]{2,1,0:T(8,128)(2,1)S(1)} %bitcast.201), kind=kOutput, calls=%fused_computation.9 | convolution fusion | flops 12884901888 | bytes 29360128 | tf_op jit(solution)/shard_map/abd,abf->df/dot_general | solution.py:361
  549.1 2.9 bitcast_convert_fusion.4
  552.1 19.8 %collective-permute-done.44 = bf16[16,32,1024]{2,0,1:T(8,128)(2,1)S(1)} collective-permute-done((bf16[16,32,1024]{2,0,1:T(8,128)(2,1)S(1)}, bf16[16,32,1024]{2,0,1:T(8,128)(2,1)S(1)}, u32[]{:S(2)}, u32[]{:S(2)}) %collective-permute-start.44) | collective-permute-done | bytes 1048608 | tf_op jit(solution)/shard_map/ppermute | solution.py:390
  571.9 3.3 add_convert_fusion.3
  580.1 15.6 %add_convert_fusion.1 = (bf16[1024,1024]{1,0:T(8,128)(2,1)S(1)}, bf16[1024,1024]{1,0:T(8,128)(2,1)S(1)}, bf16[1024,1024]{1,0:T(8,128)(2,1)S(1)}) fusion(f32[1024,3072]{1,0:T(8,128)} %convolution_bitcast_fusion, bf16[1024,2048]{1,0:T(8,128)(2,1)} %bitcast_convert_fusion, bf16[1024,2048]{1,0:T(8,128)(2,1)} %bitcast_convert_fusion.1, ...), kind=kLoop, calls=%fused_computation.18 | loop fusion | flops 28311552 | bytes 44040192 | tf_op jit(solution)/shard_map/convert_element_type | solution.py:365
  618.6 21.8 %fusion.3 = bf16[1,16,128,1024]{3,2,1,0:T(8,128)(2,1)} fusion(bf16[128,16,1024]{2,0,1:T(8,128)(2,1)} %constant_dynamic-update-slice_fusion.8, bf16[128,16,1024]{2,0,1:T(8,128)(2,1)} %copy-done.100, pred[]{:T(512)S(6)} %eq.13, bf16[16,128,3072]{2,1,0:T(8,128)(2,1)} %get-tuple-element.703, bf16[1024,1024]{1,0:T(8,128)(2,1)} %get-tuple-element.727, ...), kind=kOutput, calls=%fused_computation.12 | convolution fusion | flops 12912164864 | bytes 31457280 | tf_op jit(solution)/shard_map/...f,df->...d/dot_general | solution.py:357
  640.4 23.4 %reduce-scatter.3.cloned.1.call-done = bf16[3,4,128,256]{3,2,0,1:T(8,128)(2,1)} async-done(((bf16[3,4,128,1024]{3,2,0,1:T(8,128)(2,1)}), bf16[3,4,128,256]{3,2,0,1:T(8,128)(2,1)}) %reduce-scatter.3.cloned.1.call-update) | async-done | bytes 786448 | tf_op jit(solution)/shard_map/reduce_scatter | solution.py:548
  670.4 7.5 %fusion.2 = bf16[1,16,128,1024]{3,2,1,0:T(8,128)(2,1)} fusion(bf16[16,128,1024]{2,1,0:T(8,128)(2,1)S(1)} %copy-done.2, bf16[128,16,1024]{2,0,1:T(8,128)(2,1)} %constant_dynamic-update-slice_fusion, bf16[128,16,1024]{2,0,1:T(8,128)(2,1)} %get-tuple-element.757, pred[]{:T(512)S(6)} %eq.13), kind=kLoop, calls=%fused_computation.11 | loop fusion | flops 10485760 | bytes 16777216 | tf_op jit(solution)/shard_map/broadcast_in_dim | solution.py:552
  677.9 11.5 %reduce-scatter.5.cloned.1.call-done = bf16[3,1,128,256]{3,2,0,1:T(8,128)(2,1)} async-done(((bf16[3,4,128,256]{3,2,0,1:T(8,128)(2,1)}), bf16[3,1,128,256]{3,2,0,1:T(8,128)(2,1)}) %reduce-scatter.5.cloned.1.call-update) | async-done | bytes 196624 | tf_op jit(solution)/shard_map/reduce_scatter | solution.py:550
  (425 shorter events, 159.2 us)
Async XLA Ops:
  7.2 656.6 %reduce-scatter.3.cloned.1.call-start = ((), (), s32[]{:S(2)}) async-start(), calls=%async_computation.2 | async-start | bytes 3932160 | tf_op jit(solution)/shard_map/reduce_scatter | solution.py:548
  14.3 32.1 %collective-permute-start = (bf16[16,16,1024]{2,1,0:T(8,128)(2,1)}, bf16[16,16,1024]{2,1,0:T(8,128)(2,1)}, u32[]{:S(2)}, u32[]{:S(2)}) collective-permute-start(bf16[16,16,1024]{2,1,0:T(8,128)(2,1)} %get-tuple-element.756), channel_id=1, source_target_pairs={{0,1},{1,0},{2,3},{3,2},{4,5},{5,4},{6,7},{7,6},{8,9},{9,8},{10,11... | collective-permute-start | bytes 1572872 | tf_op jit(solution)/shard_map/ppermute | solution.py:390
  14.7 33.6 %collective-permute-start.1 = (bf16[16,16,1024]{2,1,0:T(8,128)(2,1)}, bf16[16,16,1024]{2,1,0:T(8,128)(2,1)S(1)}, u32[]{:S(2)}, u32[]{:S(2)}) collective-permute-start(bf16[16,16,1024]{2,1,0:T(8,128)(2,1)} %get-tuple-element.755), channel_id=1, source_target_pairs={{0,1},{1,0},{2,3},{3,2},{4,5},{5,4},{6,7},{7,6},{8,9},{9,8},{10,11... | collective-permute-start | bytes 1572872 | tf_op jit(solution)/shard_map/ppermute | solution.py:390
  14.8 39.3 %collective-permute-start.2 = (bf16[16,16,1024]{2,1,0:T(8,128)(2,1)}, bf16[16,16,1024]{2,1,0:T(8,128)(2,1)}, u32[]{:S(2)}, u32[]{:S(2)}) collective-permute-start(bf16[16,16,1024]{2,1,0:T(8,128)(2,1)} %get-tuple-element.754), channel_id=1, source_target_pairs={{0,1},{1,0},{2,3},{3,2},{4,5},{5,4},{6,7},{7,6},{8,9},{9,8},{10,11... | collective-permute-start | bytes 1572872 | tf_op jit(solution)/shard_map/ppermute | solution.py:390
  15.2 40.4 %collective-permute-start.3 = (bf16[16,16,1024]{2,1,0:T(8,128)(2,1)}, bf16[16,16,1024]{2,1,0:T(8,128)(2,1)}, u32[]{:S(2)}, u32[]{:S(2)}) collective-permute-start(bf16[16,16,1024]{2,1,0:T(8,128)(2,1)} %get-tuple-element.753), channel_id=1, source_target_pairs={{0,1},{1,0},{2,3},{3,2},{4,5},{5,4},{6,7},{7,6},{8,9},{9,8},{10,11... | collective-permute-start | bytes 1572872 | tf_op jit(solution)/shard_map/ppermute | solution.py:390
  17.8 29.9 %collective-permute-start.4 = (bf16[16,16,1024]{2,1,0:T(8,128)(2,1)}, bf16[16,16,1024]{2,1,0:T(8,128)(2,1)S(1)}, u32[]{:S(2)}, u32[]{:S(2)}) collective-permute-start(bf16[16,16,1024]{2,1,0:T(8,128)(2,1)} %get-tuple-element.748), channel_id=1, source_target_pairs={{0,1},{1,0},{2,3},{3,2},{4,5},{5,4},{6,7},{7,6},{8,9},{9,8},{10,11... | collective-permute-start | bytes 1572872 | tf_op jit(solution)/shard_map/ppermute | solution.py:390
  46.4 10.8 %collective-permute-start.6 = (bf16[16,16,1024]{2,1,0:T(8,128)(2,1)S(1)}, bf16[16,16,1024]{2,1,0:T(8,128)(2,1)S(1)}, u32[]{:S(2)}, u32[]{:S(2)}) collective-permute-start(bf16[16,16,1024]{2,1,0:T(8,128)(2,1)S(1)} %copy-done.97), channel_id=1, source_target_pairs={{0,1},{1,0},{2,3},{3,2},{4,5},{5,4},{6,7},{7,6},{8,9},{9,8},{10,11... | collective-permute-start | bytes 1572872 | tf_op jit(solution)/shard_map/ppermute | solution.py:390
  47.7 10.7 %collective-permute-start.7 = (bf16[16,16,1024]{2,1,0:T(8,128)(2,1)S(1)}, bf16[16,16,1024]{2,1,0:T(8,128)(2,1)S(1)}, u32[]{:S(2)}, u32[]{:S(2)}) collective-permute-start(bf16[16,16,1024]{2,1,0:T(8,128)(2,1)S(1)} %copy-done.96), channel_id=1, source_target_pairs={{0,1},{1,0},{2,3},{3,2},{4,5},{5,4},{6,7},{7,6},{8,9},{9,8},{10,11... | collective-permute-start | bytes 1572872 | tf_op jit(solution)/shard_map/ppermute | solution.py:390
  48.3 27.6 %collective-permute-start.5 = (bf16[16,32,1024]{2,1,0:T(8,128)(2,1)S(1)}, bf16[16,32,1024]{2,1,0:T(8,128)(2,1)S(1)}, u32[]{:S(2)}, u32[]{:S(2)}) collective-permute-start(bf16[16,32,1024]{2,1,0:T(8,128)(2,1)S(1)} %pad_maximum_fusion.9.rest_2_), channel_id=1, source_target_pairs={{0,2},{1,3},{2,4},{3,5},{8,10},{9,11},{10,12},{11,13},{16,18},{17,... | collective-permute-start | bytes 3145736 | tf_op jit(solution)/shard_map/ppermute | solution.py:390
  54.1 5.3 collective-permute-start.8
  78.4 36.7 %collective-permute-start.9 = (bf16[16,32,2048]{2,1,0:T(8,128)(2,1)}, bf16[16,32,2048]{2,1,0:T(8,128)(2,1)}, u32[]{:S(2)}, u32[]{:S(2)}) collective-permute-start(bf16[16,32,2048]{2,1,0:T(8,128)(2,1)} %pad_maximum_fusion.1), channel_id=1, source_target_pairs={{6,4},{7,5},{14,12},{15,13},{22,20},{23,21},{30,28},{31,29}} | collective-permute-start | bytes 6291464 | tf_op jit(solution)/shard_map/ppermute | solution.py:390
  81.1 34.0 %collective-permute-start.10 = (bf16[16,32,1024]{2,1,0:T(8,128)(2,1)}, bf16[16,32,1024]{2,1,0:T(8,128)(2,1)}, u32[]{:S(2)}, u32[]{:S(2)}) collective-permute-start(bf16[16,32,1024]{2,1,0:T(8,128)(2,1)} %copy-done.39), channel_id=1, source_target_pairs={{2,4},{3,5},{10,12},{11,13},{18,20},{19,21},{26,28},{27,29}} | collective-permute-start | bytes 3145736 | tf_op jit(solution)/shard_map/ppermute | solution.py:390
  82.7 32.4 %collective-permute-start.11 = (bf16[16,32,1024]{2,1,0:T(8,128)(2,1)}, bf16[16,32,1024]{2,1,0:T(8,128)(2,1)}, u32[]{:S(2)}, u32[]{:S(2)}) collective-permute-start(bf16[16,32,1024]{2,1,0:T(8,128)(2,1)} %pad_maximum_fusion.10.rest_2_), channel_id=1, source_target_pairs={{0,2},{1,3},{2,4},{3,5},{8,10},{9,11},{10,12},{11,13},{16,18},{17,... | collective-permute-start | bytes 3145736 | tf_op jit(solution)/shard_map/ppermute | solution.py:390
  117.8 60.4 %collective-permute-start.14 = (bf16[16,32,2048]{2,1,0:T(8,128)(2,1)}, bf16[16,32,2048]{2,1,0:T(8,128)(2,1)}, u32[]{:S(2)}, u32[]{:S(2)}) collective-permute-start(bf16[16,32,2048]{2,1,0:T(8,128)(2,1)} %pad_maximum_fusion.2), channel_id=1, source_target_pairs={{6,4},{7,5},{14,12},{15,13},{22,20},{23,21},{30,28},{31,29}} | collective-permute-start | bytes 6291464 | tf_op jit(solution)/shard_map/ppermute | solution.py:390
  120.2 58.1 %collective-permute-start.15 = (bf16[16,32,1024]{2,1,0:T(8,128)(2,1)}, bf16[16,32,1024]{2,1,0:T(8,128)(2,1)S(1)}, u32[]{:S(2)}, u32[]{:S(2)}) collective-permute-start(bf16[16,32,1024]{2,1,0:T(8,128)(2,1)} %collective-permute-done.11.rest_1_), channel_id=1, source_target_pairs={{2,4},{3,5},{10,12},{11,13},{18,20},{19,21},{26,28},{27,29}} | collective-permute-start | bytes 3145736 | tf_op jit(solution)/shard_map/ppermute | solution.py:390
  120.9 57.4 %collective-permute-start.16 = (bf16[16,32,1024]{2,1,0:T(8,128)(2,1)}, bf16[16,32,1024]{2,1,0:T(8,128)(2,1)S(1)}, u32[]{:S(2)}, u32[]{:S(2)}) collective-permute-start(bf16[16,32,1024]{2,1,0:T(8,128)(2,1)} %pad_maximum_fusion.11.rest_2_), channel_id=1, source_target_pairs={{0,2},{1,3},{2,4},{3,5},{8,10},{9,11},{10,12},{11,13},{16,18},{17,... | collective-permute-start | bytes 3145736 | tf_op jit(solution)/shard_map/ppermute | solution.py:390
  179.6 71.4 %collective-permute-start.18 = (bf16[16,32,2048]{2,1,0:T(8,128)(2,1)S(1)}, bf16[16,32,2048]{2,1,0:T(8,128)(2,1)}, u32[]{:S(2)}, u32[]{:S(2)}) collective-permute-start(bf16[16,32,2048]{2,1,0:T(8,128)(2,1)S(1)} %pad_maximum_fusion.3), channel_id=1, source_target_pairs={{6,4},{7,5},{14,12},{15,13},{22,20},{23,21},{30,28},{31,29}} | collective-permute-start | bytes 6291464 | tf_op jit(solution)/shard_map/ppermute | solution.py:390
  198.0 52.9 %collective-permute-start.19 = (bf16[16,32,1024]{2,1,0:T(8,128)(2,1)S(1)}, bf16[16,32,1024]{2,1,0:T(8,128)(2,1)S(1)}, u32[]{:S(2)}, u32[]{:S(2)}) collective-permute-start(bf16[16,32,1024]{2,1,0:T(8,128)(2,1)S(1)} %collective-permute-done.16.rest_1_), channel_id=1, source_target_pairs={{2,4},{3,5},{10,12},{11,13},{18,20},{19,21},{26,28},{27,29}} | collective-permute-start | bytes 3145736 | tf_op jit(solution)/shard_map/ppermute | solution.py:390
  198.7 52.2 %collective-permute-start.20 = (bf16[16,32,1024]{2,1,0:T(8,128)(2,1)S(1)}, bf16[16,32,1024]{2,1,0:T(8,128)(2,1)S(1)}, u32[]{:S(2)}, u32[]{:S(2)}) collective-permute-start(bf16[16,32,1024]{2,1,0:T(8,128)(2,1)S(1)} %copy-done.8), channel_id=1, source_target_pairs={{0,2},{1,3},{2,4},{3,5},{8,10},{9,11},{10,12},{11,13},{16,18},{17,... | collective-permute-start | bytes 3145736 | tf_op jit(solution)/shard_map/ppermute | solution.py:390
  222.5 28.4 %collective-permute-start.21 = (f32[16,3,512]{2,1,0:T(4,128)S(1)}, f32[16,3,512]{2,1,0:T(4,128)S(1)}, u32[]{:S(2)}, u32[]{:S(2)}) collective-permute-start(f32[16,3,512]{2,1,0:T(4,128)S(1)} %get-tuple-element.434), channel_id=1, source_target_pairs={{4,6},{5,7},{6,4},{7,5},{12,14},{13,15},{14,12},{15,13},{20,22},{2... | collective-permute-start | bytes 294920 | tf_op jit(solution)/shard_map/ppermute | solution.py:390
  253.5 53.1 %collective-permute-start.22 = (bf16[16,32,2048]{2,0,1:T(8,128)(2,1)}, bf16[16,32,2048]{2,0,1:T(8,128)(2,1)}, u32[]{:S(2)}, u32[]{:S(2)}) collective-permute-start(bf16[16,32,2048]{2,0,1:T(8,128)(2,1)} %copy.121), channel_id=1, source_target_pairs={{4,6},{5,7},{12,14},{13,15},{20,22},{21,23},{28,30},{29,31}} | collective-permute-start | bytes 6291464 | tf_op jit(solution)/shard_map/ppermute | solution.py:390
  257.0 49.6 %collective-permute-start.23 = (bf16[16,32,2048]{2,1,0:T(8,128)(2,1)}, bf16[16,32,2048]{2,1,0:T(8,128)(2,1)}, u32[]{:S(2)}, u32[]{:S(2)}) collective-permute-start(bf16[16,32,2048]{2,1,0:T(8,128)(2,1)} %pad_maximum_fusion.4), channel_id=1, source_target_pairs={{6,4},{7,5},{14,12},{15,13},{22,20},{23,21},{30,28},{31,29}} | collective-permute-start | bytes 6291464 | tf_op jit(solution)/shard_map/ppermute | solution.py:390
  280.1 26.5 %collective-permute-start.24 = (bf16[16,32,1024]{2,1,0:T(8,128)(2,1)S(1)}, bf16[16,32,1024]{2,1,0:T(8,128)(2,1)S(1)}, u32[]{:S(2)}, u32[]{:S(2)}) collective-permute-start(bf16[16,32,1024]{2,1,0:T(8,128)(2,1)S(1)} %copy-done.42), channel_id=1, source_target_pairs={{2,4},{3,5},{10,12},{11,13},{18,20},{19,21},{26,28},{27,29}} | collective-permute-start | bytes 3145736 | tf_op jit(solution)/shard_map/ppermute | solution.py:390
  281.4 25.2 %collective-permute-start.25 = (bf16[16,32,1024]{2,0,1:T(8,128)(2,1)S(1)}, bf16[16,32,1024]{2,0,1:T(8,128)(2,1)S(1)}, u32[]{:S(2)}, u32[]{:S(2)}) collective-permute-start(bf16[16,32,1024]{2,0,1:T(8,128)(2,1)S(1)} %copy.123), channel_id=1, source_target_pairs={{4,2},{5,3},{12,10},{13,11},{20,18},{21,19},{28,26},{29,27}} | collective-permute-start | bytes 3145736 | tf_op jit(solution)/shard_map/ppermute | solution.py:390
  282.1 24.5 %collective-permute-start.26 = (f32[16,3,512]{2,1,0:T(4,128)S(1)}, f32[16,3,512]{2,1,0:T(4,128)S(1)}, u32[]{:S(2)}, u32[]{:S(2)}) collective-permute-start(f32[16,3,512]{2,1,0:T(4,128)S(1)} %get-tuple-element.479), channel_id=1, source_target_pairs={{4,6},{5,7},{6,4},{7,5},{12,14},{13,15},{14,12},{15,13},{20,22},{2... | collective-permute-start | bytes 294920 | tf_op jit(solution)/shard_map/ppermute | solution.py:390
  310.9 66.7 %collective-permute-start.27 = (bf16[16,32,2048]{2,0,1:T(8,128)(2,1)}, bf16[16,32,2048]{2,0,1:T(8,128)(2,1)}, u32[]{:S(2)}, u32[]{:S(2)}) collective-permute-start(bf16[16,32,2048]{2,0,1:T(8,128)(2,1)} %copy.124), channel_id=1, source_target_pairs={{4,6},{5,7},{12,14},{13,15},{20,22},{21,23},{28,30},{29,31}} | collective-permute-start | bytes 6291464 | tf_op jit(solution)/shard_map/ppermute | solution.py:390
  314.6 63.0 %collective-permute-start.28 = (bf16[16,32,1024]{2,0,1:T(8,128)(2,1)}, bf16[16,32,1024]{2,0,1:T(8,128)(2,1)}, u32[]{:S(2)}, u32[]{:S(2)}) collective-permute-start(bf16[16,32,1024]{2,0,1:T(8,128)(2,1)} %add_convert_fusion.17), channel_id=1, source_target_pairs={{2,0},{3,1},{4,2},{5,3},{10,8},{11,9},{12,10},{13,11},{18,16},{19,... | collective-permute-start | bytes 3145736 | tf_op jit(solution)/shard_map/ppermute | solution.py:390
  317.5 60.1 %collective-permute-start.29 = (bf16[16,32,1024]{2,0,1:T(8,128)(2,1)}, bf16[16,32,1024]{2,0,1:T(8,128)(2,1)}, u32[]{:S(2)}, u32[]{:S(2)}) collective-permute-start(bf16[16,32,1024]{2,0,1:T(8,128)(2,1)} %copy.128), channel_id=1, source_target_pairs={{4,2},{5,3},{12,10},{13,11},{20,18},{21,19},{28,26},{29,27}} | collective-permute-start | bytes 3145736 | tf_op jit(solution)/shard_map/ppermute | solution.py:390
  335.0 42.5 %collective-permute-start.30 = (f32[16,3,512]{2,1,0:T(4,128)S(1)}, f32[16,3,512]{2,1,0:T(4,128)S(1)}, u32[]{:S(2)}, u32[]{:S(2)}) collective-permute-start(f32[16,3,512]{2,1,0:T(4,128)S(1)} %get-tuple-element.530), channel_id=1, source_target_pairs={{4,6},{5,7},{6,4},{7,5},{12,14},{13,15},{14,12},{15,13},{20,22},{2... | collective-permute-start | bytes 294920 | tf_op jit(solution)/shard_map/ppermute | solution.py:390
  339.9 37.6 %collective-permute-start.31 = (bf16[16,16,1024]{2,0,1:T(8,128)(2,1)}, bf16[16,16,1024]{2,0,1:T(8,128)(2,1)S(1)}, u32[]{:S(2)}, u32[]{:S(2)}) collective-permute-start(bf16[16,16,1024]{2,0,1:T(8,128)(2,1)} %slice.244), channel_id=1, source_target_pairs={{0,1},{1,0},{2,3},{3,2},{4,5},{5,4},{6,7},{7,6},{8,9},{9,8},{10,11... | collective-permute-start | bytes 1572872 | tf_op jit(solution)/shard_map/ppermute | solution.py:390
  380.1 56.0 %collective-permute-start.32 = (bf16[16,32,2048]{2,0,1:T(8,128)(2,1)}, bf16[16,32,2048]{2,0,1:T(8,128)(2,1)S(1)}, u32[]{:S(2)}, u32[]{:S(2)}) collective-permute-start(bf16[16,32,2048]{2,0,1:T(8,128)(2,1)} %copy.131), channel_id=1, source_target_pairs={{4,6},{5,7},{12,14},{13,15},{20,22},{21,23},{28,30},{29,31}} | collective-permute-start | bytes 6291464 | tf_op jit(solution)/shard_map/ppermute | solution.py:390
  385.6 50.4 %collective-permute-start.33 = (bf16[16,16,1024]{2,0,1:T(8,128)(2,1)}, bf16[16,16,1024]{2,0,1:T(8,128)(2,1)}, u32[]{:S(2)}, u32[]{:S(2)}) collective-permute-start(bf16[16,16,1024]{2,0,1:T(8,128)(2,1)} %get-tuple-element.771), channel_id=1, source_target_pairs={{0,1},{1,0},{2,3},{3,2},{4,5},{5,4},{6,7},{7,6},{8,9},{9,8},{10,11... | collective-permute-start | bytes 1572872 | tf_op jit(solution)/shard_map/ppermute | solution.py:390
  389.2 46.9 %collective-permute-start.34 = (bf16[16,32,1024]{2,0,1:T(8,128)(2,1)}, bf16[16,32,1024]{2,0,1:T(8,128)(2,1)}, u32[]{:S(2)}, u32[]{:S(2)}) collective-permute-start(bf16[16,32,1024]{2,0,1:T(8,128)(2,1)} %add_convert_fusion.13), channel_id=1, source_target_pairs={{2,0},{3,1},{4,2},{5,3},{10,8},{11,9},{12,10},{13,11},{18,16},{19,... | collective-permute-start | bytes 3145736 | tf_op jit(solution)/shard_map/ppermute | solution.py:390
  392.1 44.0 %collective-permute-start.35 = (bf16[16,32,1024]{2,0,1:T(8,128)(2,1)}, bf16[16,32,1024]{2,0,1:T(8,128)(2,1)}, u32[]{:S(2)}, u32[]{:S(2)}) collective-permute-start(bf16[16,32,1024]{2,0,1:T(8,128)(2,1)} %copy.138), channel_id=1, source_target_pairs={{4,2},{5,3},{12,10},{13,11},{20,18},{21,19},{28,26},{29,27}} | collective-permute-start | bytes 3145736 | tf_op jit(solution)/shard_map/ppermute | solution.py:390
  398.8 37.2 %collective-permute-start.36 = (bf16[16,16,1024]{2,0,1:T(8,128)(2,1)}, bf16[16,16,1024]{2,0,1:T(8,128)(2,1)S(1)}, u32[]{:S(2)}, u32[]{:S(2)}) collective-permute-start(bf16[16,16,1024]{2,0,1:T(8,128)(2,1)} %slice.247), channel_id=1, source_target_pairs={{0,1},{1,0},{2,3},{3,2},{4,5},{5,4},{6,7},{7,6},{8,9},{9,8},{10,11... | collective-permute-start | bytes 1572872 | tf_op jit(solution)/shard_map/ppermute | solution.py:390
  438.5 69.2 %collective-permute-start.37 = (bf16[16,32,2048]{2,0,1:T(8,128)(2,1)}, bf16[16,32,2048]{2,0,1:T(8,128)(2,1)}, u32[]{:S(2)}, u32[]{:S(2)}) collective-permute-start(bf16[16,32,2048]{2,0,1:T(8,128)(2,1)} %copy.141), channel_id=1, source_target_pairs={{4,6},{5,7},{12,14},{13,15},{20,22},{21,23},{28,30},{29,31}} | collective-permute-start | bytes 6291464 | tf_op jit(solution)/shard_map/ppermute | solution.py:390
  445.1 62.5 %collective-permute-start.38 = (bf16[16,16,1024]{2,0,1:T(8,128)(2,1)}, bf16[16,16,1024]{2,0,1:T(8,128)(2,1)}, u32[]{:S(2)}, u32[]{:S(2)}) collective-permute-start(bf16[16,16,1024]{2,0,1:T(8,128)(2,1)} %get-tuple-element.769), channel_id=1, source_target_pairs={{0,1},{1,0},{2,3},{3,2},{4,5},{5,4},{6,7},{7,6},{8,9},{9,8},{10,11... | collective-permute-start | bytes 1572872 | tf_op jit(solution)/shard_map/ppermute | solution.py:390
  448.5 59.1 %collective-permute-start.39 = (bf16[16,32,1024]{2,0,1:T(8,128)(2,1)}, bf16[16,32,1024]{2,0,1:T(8,128)(2,1)}, u32[]{:S(2)}, u32[]{:S(2)}) collective-permute-start(bf16[16,32,1024]{2,0,1:T(8,128)(2,1)} %add_convert_fusion.9), channel_id=1, source_target_pairs={{2,0},{3,1},{4,2},{5,3},{10,8},{11,9},{12,10},{13,11},{18,16},{19,... | collective-permute-start | bytes 3145736 | tf_op jit(solution)/shard_map/ppermute | solution.py:390
  451.4 56.3 %collective-permute-start.40 = (bf16[16,32,1024]{2,0,1:T(8,128)(2,1)}, bf16[16,32,1024]{2,0,1:T(8,128)(2,1)}, u32[]{:S(2)}, u32[]{:S(2)}) collective-permute-start(bf16[16,32,1024]{2,0,1:T(8,128)(2,1)} %copy.147), channel_id=1, source_target_pairs={{4,2},{5,3},{12,10},{13,11},{20,18},{21,19},{28,26},{29,27}} | collective-permute-start | bytes 3145736 | tf_op jit(solution)/shard_map/ppermute | solution.py:390
  459.2 19.8 %collective-permute-start.41 = (f32[64,3,8,16]{0,3,2,1:T(8,128)}, f32[64,3,8,16]{0,3,2,1:T(8,128)}, u32[]{:S(2)}, u32[]{:S(2)}) collective-permute-start(f32[64,3,8,16]{0,3,2,1:T(8,128)} %copy.150), channel_id=1, source_target_pairs={{0,1},{1,0},{2,3},{3,2},{4,5},{5,4},{6,7},{7,6},{8,9},{9,8},{10,11... | collective-permute-start | bytes 294920 | tf_op jit(solution)/shard_map/ppermute | solution.py:390
  479.0 28.6 %collective-permute-start.42 = (bf16[16,16,1024]{2,0,1:T(8,128)(2,1)}, bf16[16,16,1024]{2,0,1:T(8,128)(2,1)}, u32[]{:S(2)}, u32[]{:S(2)}) collective-permute-start(bf16[16,16,1024]{2,0,1:T(8,128)(2,1)} %slice.252), channel_id=1, source_target_pairs={{0,1},{1,0},{2,3},{3,2},{4,5},{5,4},{6,7},{7,6},{8,9},{9,8},{10,11... | collective-permute-start | bytes 1572872 | tf_op jit(solution)/shard_map/ppermute | solution.py:390
  513.6 38.5 %collective-permute-start.43 = (bf16[16,16,1024]{2,0,1:T(8,128)(2,1)S(1)}, bf16[16,16,1024]{2,0,1:T(8,128)(2,1)S(1)}, u32[]{:S(2)}, u32[]{:S(2)}) collective-permute-start(bf16[16,16,1024]{2,0,1:T(8,128)(2,1)S(1)} %get-tuple-element.767), channel_id=1, source_target_pairs={{0,1},{1,0},{2,3},{3,2},{4,5},{5,4},{6,7},{7,6},{8,9},{9,8},{10,11... | collective-permute-start | bytes 1572872 | tf_op jit(solution)/shard_map/ppermute | solution.py:390
  515.5 56.4 %collective-permute-start.44 = (bf16[16,32,1024]{2,0,1:T(8,128)(2,1)S(1)}, bf16[16,32,1024]{2,0,1:T(8,128)(2,1)S(1)}, u32[]{:S(2)}, u32[]{:S(2)}) collective-permute-start(bf16[16,32,1024]{2,0,1:T(8,128)(2,1)S(1)} %add_convert_fusion.5), channel_id=1, source_target_pairs={{2,0},{3,1},{4,2},{5,3},{10,8},{11,9},{12,10},{13,11},{18,16},{19,... | collective-permute-start | bytes 3145736 | tf_op jit(solution)/shard_map/ppermute | solution.py:390
  520.4 31.7 %collective-permute-start.45 = (bf16[16,16,1024]{2,0,1:T(8,128)(2,1)S(1)}, bf16[16,16,1024]{2,0,1:T(8,128)(2,1)S(1)}, u32[]{:S(2)}, u32[]{:S(2)}) collective-permute-start(bf16[16,16,1024]{2,0,1:T(8,128)(2,1)S(1)} %slice.255), channel_id=1, source_target_pairs={{0,1},{1,0},{2,3},{3,2},{4,5},{5,4},{6,7},{7,6},{8,9},{9,8},{10,11... | collective-permute-start | bytes 1572872 | tf_op jit(solution)/shard_map/ppermute | solution.py:390
  595.9 7.4 %collective-permute-start.49 = (bf16[4,128,1024]{2,1,0:T(8,128)(2,1)S(1)}, bf16[4,128,1024]{2,1,0:T(8,128)(2,1)S(1)}, u32[]{:S(2)}, u32[]{:S(2)}) collective-permute-start(bf16[4,128,1024]{2,1,0:T(8,128)(2,1)S(1)} %dynamic-slice_bitcast_fusion), channel_id=1, source_target_pairs={{0,1},{1,0},{2,3},{3,2},{4,5},{5,4},{6,7},{7,6},{8,9},{9,8},{10,11... | collective-permute-start | bytes 3145736 | tf_op jit(solution)/shard_map/ppermute | solution.py:390
  596.2 7.5 %collective-permute-start.48 = (bf16[4,128,1024]{2,1,0:T(8,128)(2,1)S(1)}, bf16[4,128,1024]{2,1,0:T(8,128)(2,1)S(1)}, u32[]{:S(2)}, u32[]{:S(2)}) collective-permute-start(bf16[4,128,1024]{2,1,0:T(8,128)(2,1)S(1)} %dynamic-slice_bitcast_fusion.1), channel_id=1, source_target_pairs={{0,1},{1,0},{2,3},{3,2},{4,5},{5,4},{6,7},{7,6},{8,9},{9,8},{10,11... | collective-permute-start | bytes 3145736 | tf_op jit(solution)/shard_map/ppermute | solution.py:390
  596.7 7.5 %collective-permute-start.47 = (bf16[4,128,1024]{2,1,0:T(8,128)(2,1)S(1)}, bf16[4,128,1024]{2,1,0:T(8,128)(2,1)S(1)}, u32[]{:S(2)}, u32[]{:S(2)}) collective-permute-start(bf16[4,128,1024]{2,1,0:T(8,128)(2,1)S(1)} %dynamic-slice_bitcast_fusion.2), channel_id=1, source_target_pairs={{0,1},{1,0},{2,3},{3,2},{4,5},{5,4},{6,7},{7,6},{8,9},{9,8},{10,11... | collective-permute-start | bytes 3145736 | tf_op jit(solution)/shard_map/ppermute | solution.py:390
  607.8 81.6 %reduce-scatter.5.cloned.1.call-start = ((), (), s32[]{:S(2)}) async-start(), calls=%async_computation.3 | async-start | bytes 983040 | tf_op jit(solution)/shard_map/reduce_scatter | solution.py:550
  (115 other events, 1621.9 us)
Sparse Core Ops, SparseCore 0:
  607.9 55.7 reduce-scatter.2
  666.1 23.2 reduce-scatter.4
